TPU v7x, 32 devices: a whole 2x2x4 slice. The times are simulated.
32 devices in a mesh: grp: 2 (over x), site: 8 (over z, y), sec: 2 (over core).
Axes of the slice: x: 2, y: 2, z: 4, core: 2. Of those that a mesh axis runs over, the one named last changes fastest.
Arguments:
- tensors: bfloat16 [32, 2, 20, 256, 256], P(('grp', 'site'), None, 'sec'), parts along dimension 0, may hold values from -0.25 to 0.25
- sources: int32 [32, 2, 20], P('grp'), parts along dimension 0, may hold values from -1 to 19, as said below
- operators: float32 [2, 2], replicated, may hold values from -1 to 1
- insert_at: int32 [16, 2], P(('grp', 'site')), parts along dimension 0, may hold values from 0 to 1
- schmidt: float32 [32, 20, 256], P('grp', 'sec'), parts along dimension 0, may hold values from 0.2 to 4
Outputs:
- final_env: bfloat16 [16, 2, 20, 256, 256], P(('grp', 'site'), None, 'sec'), parts along dimension 0
- correlation: float32 [32, 2, 2], P(('grp', 'site')), parts along dimension 0
There are 2 independent parts, one for each index of `grp`. A program takes and returns all parts, laid end to end along the dimension named above; an argument that names none is the same for every part. Nothing has to cross between parts.
Inputs may be any that keep to these rules, and one draw needn't show every extreme that they name: Charge conservation: each site i has one charge offset c_i in the finite set (-1, 0, 1), and sources[i, s, r] = r + c_i + 2s - 1 where that lies between 0 and 19, else -1.
All inputs are finite; a program needn't handle non-finite values.
Results may differ from a plain program's by a relative error of at most 0.013.
Values may be sent and summed in bfloat16 or wider, within the bound.
No kernel may reach another device: no remote copies, remote signals or barrier semaphores. Data moves between devices by JAX's collectives and lax.ppermute only.
A program may use at most 128 MiB of HBM per device.

v0:
```python
import jax
import jax.numpy as jnp
from jax import lax
from jax.sharding import PartitionSpec as P


def padded(cells, sides, width):
    for axis, dim in sides:
        count = lax.axis_size(axis)
        ends = count - 1
        head = lax.slice_in_dim(cells, 0, width, axis=dim)
        tail = lax.slice_in_dim(cells, cells.shape[dim] - width, cells.shape[dim], axis=dim)
        cells = jnp.concatenate(
            [
                lax.ppermute(tail, axis, [(i, (i + 1) % count) for i in range(ends)]),
                cells,
                lax.ppermute(head, axis, [((i + 1) % count, i) for i in range(ends)]),
            ],
            axis=dim,
        )
    return cells


def shifted(block, axis, distance):
    devices = range(lax.axis_size(axis))
    route = [(i - distance, i) for i in devices if i - distance in devices]
    return lax.ppermute(block, axis, route)


def measure(environment, radius):
    diagonal = jnp.diagonal(environment, axis1=2, axis2=3).astype(jnp.float32)
    return jnp.sum(diagonal * (radius * radius)[None], axis=(1, 2))


def site_charge(full_row):
    sector = jnp.arange(full_row.shape[1], dtype=jnp.int32)[None, :]
    state = jnp.arange(2, dtype=jnp.int32)[:, None]
    offsets = jnp.where(full_row >= 0, full_row - sector - 2 * state + 1, jnp.int32(-2))
    return jnp.max(offsets)


def shards(tensors, sources, operators, insert_at, schmidt):
    shard_width = tensors.shape[2]
    core_index = lax.axis_index("sec")
    pair_index = lax.axis_index("site")
    first_sector = core_index * shard_width

    def advance(environment, blocks, source_rows, charge, weight):
        wider = padded(environment, (("sec", 1),), 2)
        base = charge + 1
        total = jnp.zeros(environment.shape, jnp.float32)
        for state in range(2):
            state_rows = source_rows[state]
            picked = lax.dynamic_slice_in_dim(wider, base + 2 * state, shard_width, 1)
            picked = jnp.where(
                (state_rows >= 0)[None, :, None, None], picked, jnp.zeros((), picked.dtype)
            )
            middle = jnp.einsum(
                "krab,rbc->krac", picked, blocks[state], preferred_element_type=jnp.float32
            ).astype(jnp.bfloat16)
            product = lax.dot_general(
                middle,
                blocks[state],
                (((2,), (1,)), ((1,), (0,))),
                preferred_element_type=jnp.float32,
            )
            product = jnp.swapaxes(product, 2, 3)
            product = jnp.swapaxes(product, 0, 1)
            total = total + weight[:, state][:, None, None, None] * product
        return total.astype(jnp.bfloat16)

    near_full = lax.dynamic_slice_in_dim(sources, 2 * pair_index, 2, 0)
    source_rows = lax.dynamic_slice_in_dim(near_full, first_sector, shard_width, 2)
    charges = (site_charge(near_full[0]), site_charge(near_full[1]))
    radius_rows = lax.dynamic_slice_in_dim(schmidt, 2 * pair_index, 2, 0)
    squares = jnp.einsum(
        "srba,srbc->srac", tensors[0], tensors[0], preferred_element_type=jnp.float32
    )
    squares = jnp.where((source_rows[0] >= 0)[:, :, None, None], squares, jnp.float32(0.0))
    chosen = insert_at[0][:, None]
    first_weight = jnp.where(chosen == 0, operators, jnp.float32(1.0))
    second_weight = jnp.where(chosen == 1, operators, jnp.float32(1.0))
    environment = jnp.sum(first_weight[:, :, None, None, None] * squares[None], axis=1).astype(
        jnp.bfloat16
    )
    first_value = measure(environment, radius_rows[0])
    environment = advance(environment, tensors[1], source_rows[1], charges[1], second_weight)
    section_rows = [jnp.stack([first_value, measure(environment, radius_rows[1])])]
    unit_weight = jnp.ones_like(operators)
    environment = shifted(environment, "site", 1)
    measured = []
    for within in range(2):
        environment = advance(
            environment, tensors[within], source_rows[within], charges[within], unit_weight
        )
        measured.append(measure(environment, radius_rows[within]))
    section_rows.append(jnp.stack(measured))
    summed = lax.psum(jnp.stack(section_rows), "sec")
    return (environment[None], jnp.transpose(summed, (1, 0, 2)))


def solution(mesh):
    placed = (
        P(("grp", "site"), None, "sec", None, None),
        P("grp", None, None),
        P(),
        P(("grp", "site"), None),
        P("grp", "sec", None),
    )
    return jax.shard_map(
        shards,
        mesh=mesh,
        in_specs=placed,
        out_specs=(P(("grp", "site"), None, "sec", None, None), P(("grp", "site"), None, None)),
        check_vma=False,
    )
```

profile of v0, /device:TPU:17, one launch (start us, length us, event | category | flops | bytes accessed | tf_op | source)
XLA Modules:
  0.0 343.4 jit_solution(4997234047012776991)
XLA Ops:
  2.1 3.6 %broadcast_select_fusion = f32[2,10,256,256]{3,2,1,0:T(8,128)S(1)} fusion(pred[2,10]{1,0:T(4,128)(4,1)S(1)} %compare_bitcast_fusion.2, bf16[2,2,10,256,256]{4,3,2,1,0:T(8,128)(2,1)} %param.5), kind=kOutput, calls=%fused_computation.50 | convolution fusion | flops 672399360 | bytes 7864340 | tf_op jit(solution)/shard_map/srba,srbc->srac/dot_general | solution.py:76
  5.8 2.8 multiply_reduce_fusion
  8.6 3.0 copy.23
  13.9 3.9 %collective-permute-start.1 = (bf16[2,2,256,256]{2,3,0,1:T(8,128)(2,1)}, bf16[2,2,256,256]{2,3,0,1:T(8,128)(2,1)}, u32[]{:S(2)}, u32[]{:S(2)}) collective-permute-start(bf16[2,2,256,256]{2,3,0,1:T(8,128)(2,1)} %get-tuple-element.21), channel_id=1, source_target_pairs={{1,0},{3,2},{5,4},{7,6},{9,8},{11,10},{13,12},{15,14},{17,16},{19,... | collective-permute-start | bytes 1572872 | tf_op jit(solution)/shard_map/ppermute | solution.py:17
  17.8 1.5 fusion.138
  23.1 3.0 pad_maximum_fusion
  26.1 6.6 %fusion.12 = f32[10,2,256,256]{3,2,1,0:T(8,128)} fusion(bf16[2,14,256,256]{2,3,0,1:T(8,128)(2,1)} %pad_maximum_fusion, s32[]{:T(128)S(6)} %select_n.80, pred[10]{0:T(512)(128)(4,1)S(1)} %get-tuple-element.26, bf16[2,2,10,256,256]{4,3,2,1,0:T(8,128)(2,1)} %param.5), kind=kOutput, calls=%fused_computation.22 | convolution fusion | flops 1344798720 | bytes 10485774 | tf_op jit(solution)/shard_map/dot_general | solution.py:61
  32.7 7.6 %fusion = bf16[2,10,256,256]{2,3,0,1:T(8,128)(2,1)} fusion(f32[10,2,256,256]{3,2,1,0:T(8,128)} %fusion.12, f32[2]{0:T(128)S(1)} %get-tuple-element.15, f32[2]{0:T(128)S(1)} %get-tuple-element.14, bf16[2,14,256,256]{2,3,0,1:T(8,128)(2,1)} %pad_maximum_fusion, s32[]{:T(128)S(6)} %select_n.82, pred[10]{0:T(512)(128)(4,1)S(1)} %get-tuple-element.25, ...), kind=kOutput, calls=%fused_computation.10 | convolution fusion | flops 1350041600 | bytes 13107230 | tf_op jit(solution)/shard_map/dot_general | solution.py:61
  40.3 3.1 collective-permute-start.2
  43.4 57.5 %collective-permute-done.2 = bf16[2,10,256,256]{2,3,0,1:T(8,128)(2,1)S(1)} collective-permute-done((bf16[2,10,256,256]{2,3,0,1:T(8,128)(2,1)}, bf16[2,10,256,256]{2,3,0,1:T(8,128)(2,1)S(1)}, u32[]{:S(2)}, u32[]{:S(2)}) %collective-permute-start.2) | collective-permute-done | bytes 2621472 | tf_op jit(solution)/shard_map/ppermute | solution.py:27
  100.9 1.5 copy-done.1
  104.8 3.9 %collective-permute-start.4 = (bf16[2,2,256,256]{2,3,0,1:T(8,128)(2,1)}, bf16[2,2,256,256]{2,3,0,1:T(8,128)(2,1)S(1)}, u32[]{:S(2)}, u32[]{:S(2)}) collective-permute-start(bf16[2,2,256,256]{2,3,0,1:T(8,128)(2,1)} %get-tuple-element.18), channel_id=1, source_target_pairs={{1,0},{3,2},{5,4},{7,6},{9,8},{11,10},{13,12},{15,14},{17,16},{19,... | collective-permute-start | bytes 1572872 | tf_op jit(solution)/shard_map/ppermute | solution.py:17
  111.3 1.9 constant_dynamic-update-slice_fusion.2
  113.1 3.5 %constant_dynamic-update-slice_fusion.1 = bf16[2,14,256,256]{2,3,0,1:T(8,128)(2,1)} fusion(bf16[2,14,256,256]{2,3,0,1:T(8,128)(2,1)} %constant_dynamic-update-slice_fusion.2, bf16[2,10,256,256]{2,3,0,1:T(8,128)(2,1)} %copy-done.1), kind=kLoop, calls=%fused_computation.89 | loop fusion | bytes 5242880
  117.5 6.6 %fusion.6 = f32[10,2,256,256]{3,2,1,0:T(8,128)} fusion(bf16[2,14,256,256]{2,3,0,1:T(8,128)(2,1)} %constant_dynamic-update-slice_fusion, s32[]{:T(128)S(6)} %select_n.87, pred[10]{0:T(512)(128)(4,1)S(1)} %get-tuple-element.27, bf16[2,2,10,256,256]{4,3,2,1,0:T(8,128)(2,1)} %param.5), kind=kOutput, calls=%fused_computation.16 | convolution fusion | flops 1344798720 | bytes 10485774 | tf_op jit(solution)/shard_map/dot_general | solution.py:61
  124.1 7.3 %fusion.1 = bf16[2,10,256,256]{2,3,0,1:T(8,128)(2,1)} fusion(f32[10,2,256,256]{3,2,1,0:T(8,128)} %fusion.6, bf16[2,14,256,256]{2,3,0,1:T(8,128)(2,1)} %constant_dynamic-update-slice_fusion, s32[]{:T(128)S(6)} %select_n.85, pred[10]{0:T(512)(128)(4,1)S(1)} %get-tuple-element.24, bf16[2,2,10,256,256]{4,3,2,1,0:T(8,128)(2,1)} %param.5), kind=kOutput, calls=%fused_computation.11 | convolution fusion | flops 1347420160 | bytes 13107214 | tf_op jit(solution)/shard_map/dot_general | solution.py:61
  131.4 2.3 fusion.153
  134.9 3.9 %collective-permute-start.6 = (bf16[2,2,256,256]{2,3,0,1:T(8,128)(2,1)}, bf16[2,2,256,256]{2,3,0,1:T(8,128)(2,1)}, u32[]{:S(2)}, u32[]{:S(2)}) collective-permute-start(bf16[2,2,256,256]{2,3,0,1:T(8,128)(2,1)} %get-tuple-element.17), channel_id=1, source_target_pairs={{1,0},{3,2},{5,4},{7,6},{9,8},{11,10},{13,12},{15,14},{17,16},{19,... | collective-permute-start | bytes 1572872 | tf_op jit(solution)/shard_map/ppermute | solution.py:17
  139.8 41.1 %copy.36 = bf16[2,10,256,256]{1,0,3,2:T(2,128)(2,1)} copy(bf16[2,10,256,256]{2,3,0,1:T(8,128)(2,1)S(1)} %copy.23) | data formatting | bytes 5242880 | tf_op jit(solution)/shard_map/convert_element_type | solution.py:83
  181.2 3.1 gather_fusion
  184.3 45.7 %copy.39 = bf16[2,10,256,256]{1,0,3,2:T(2,128)(2,1)} copy(bf16[2,10,256,256]{2,3,0,1:T(8,128)(2,1)} %fusion) | data formatting | bytes 5242880 | tf_op jit(solution)/shard_map/convert_element_type | solution.py:70
  230.0 2.5 gather_fusion.1
  232.5 41.1 %copy.41 = bf16[2,10,256,256]{1,0,3,2:T(2,128)(2,1)} copy(bf16[2,10,256,256]{2,3,0,1:T(8,128)(2,1)S(1)} %copy-done) | data formatting | bytes 5242880 | tf_op jit(solution)/shard_map/convert_element_type | solution.py:70
  273.6 3.1 gather_fusion.2
  276.7 1.4 fusion.122
  278.2 3.0 pad_maximum_fusion.1
  281.2 6.6 %fusion.2 = f32[10,2,256,256]{3,2,1,0:T(8,128)} fusion(bf16[2,14,256,256]{2,3,0,1:T(8,128)(2,1)} %pad_maximum_fusion.1, s32[]{:T(128)S(6)} %select_n.82, pred[10]{0:T(512)(128)(4,1)S(1)} %copy-done.4, bf16[2,2,10,256,256]{4,3,2,1,0:T(8,128)(2,1)} %param.5), kind=kOutput, calls=%fused_computation.12 | convolution fusion | flops 1344798720 | bytes 10485774 | tf_op jit(solution)/shard_map/dot_general | solution.py:61
  287.8 5.8 %add_convert_fusion = bf16[10,2,256,256]{3,2,1,0:T(8,128)(2,1)S(1)} fusion(f32[10,2,256,256]{3,2,1,0:T(8,128)} %fusion.2, bf16[2,14,256,256]{2,3,0,1:T(8,128)(2,1)} %pad_maximum_fusion.1, s32[]{:T(128)S(6)} %select_n.80, pred[10]{0:T(512)(128)(4,1)S(1)} %get-tuple-element.26, bf16[2,2,10,256,256]{4,3,2,1,0:T(8,128)(2,1)} %param.5), kind=kOutput, calls=%fused_computation.5 | convolution fusion | flops 1347420160 | bytes 13107214 | tf_op jit(solution)/shard_map/dot_general | solution.py:61
  293.6 41.1 %copy.42 = bf16[2,10,256,256]{1,0,3,2:T(2,128)(2,1)} copy(bf16[2,10,256,256]{2,3,0,1:T(8,128)(2,1)S(1)} %bitcast.131) | data formatting | bytes 5242880 | tf_op jit(solution)/shard_map/convert_element_type | solution.py:70
  334.7 2.5 gather_fusion.3
  337.8 2.5 psum.7
  340.8 2.5 copy.43
  (37 shorter events, 11.7 us)
Async XLA Ops:
  2.1 3.7 %copy-start.2 = (f32[2,2]{1,0:T(2,128)S(1)}, f32[2,2]{1,0:T(2,128)}, u32[]{:S(2)}) copy-start(f32[2,2]{1,0:T(2,128)} %param.7) | copy-start | bytes 52
  12.6 10.4 %collective-permute-start = (bf16[2,2,256,256]{2,3,0,1:T(8,128)(2,1)}, bf16[2,2,256,256]{2,3,0,1:T(8,128)(2,1)S(1)}, u32[]{:S(2)}, u32[]{:S(2)}) collective-permute-start(bf16[2,2,256,256]{2,3,0,1:T(8,128)(2,1)} %get-tuple-element.20), channel_id=1, source_target_pairs={{0,1},{2,3},{4,5},{6,7},{8,9},{10,11},{12,13},{14,15},{16,17},{18,... | collective-permute-start | bytes 1572872 | tf_op jit(solution)/shard_map/ppermute | solution.py:15
  13.9 9.2 %collective-permute-start.1 = (bf16[2,2,256,256]{2,3,0,1:T(8,128)(2,1)}, bf16[2,2,256,256]{2,3,0,1:T(8,128)(2,1)}, u32[]{:S(2)}, u32[]{:S(2)}) collective-permute-start(bf16[2,2,256,256]{2,3,0,1:T(8,128)(2,1)} %get-tuple-element.21), channel_id=1, source_target_pairs={{1,0},{3,2},{5,4},{7,6},{9,8},{11,10},{13,12},{15,14},{17,16},{19,... | collective-permute-start | bytes 1572872 | tf_op jit(solution)/shard_map/ppermute | solution.py:17
  22.9 9.8 %copy-start.3 = (pred[10]{0:T(512)(128)(4,1)}, pred[10]{0:T(512)(128)(4,1)S(1)}, u32[]{:S(2)}) copy-start(pred[10]{0:T(512)(128)(4,1)S(1)} %get-tuple-element.25) | copy-start | bytes 34
  40.3 60.7 %collective-permute-start.2 = (bf16[2,10,256,256]{2,3,0,1:T(8,128)(2,1)}, bf16[2,10,256,256]{2,3,0,1:T(8,128)(2,1)S(1)}, u32[]{:S(2)}, u32[]{:S(2)}) collective-permute-start(bf16[2,10,256,256]{2,3,0,1:T(8,128)(2,1)} %fusion), channel_id=1, source_target_pairs={{0,2},{2,4},{4,6},{6,8},{8,10},{10,12},{12,14},{1,3},{3,5},{5,7},{... | collective-permute-start | bytes 7864328 | tf_op jit(solution)/shard_map/ppermute | solution.py:27
  100.9 1.5 copy-start.1
  103.5 7.8 %collective-permute-start.3 = (bf16[2,2,256,256]{2,3,0,1:T(8,128)(2,1)}, bf16[2,2,256,256]{2,3,0,1:T(8,128)(2,1)}, u32[]{:S(2)}, u32[]{:S(2)}) collective-permute-start(bf16[2,2,256,256]{2,3,0,1:T(8,128)(2,1)} %get-tuple-element.19), channel_id=1, source_target_pairs={{0,1},{2,3},{4,5},{6,7},{8,9},{10,11},{12,13},{14,15},{16,17},{18,... | collective-permute-start | bytes 1572872 | tf_op jit(solution)/shard_map/ppermute | solution.py:15
  104.8 11.8 %collective-permute-start.4 = (bf16[2,2,256,256]{2,3,0,1:T(8,128)(2,1)}, bf16[2,2,256,256]{2,3,0,1:T(8,128)(2,1)S(1)}, u32[]{:S(2)}, u32[]{:S(2)}) collective-permute-start(bf16[2,2,256,256]{2,3,0,1:T(8,128)(2,1)} %get-tuple-element.18), channel_id=1, source_target_pairs={{1,0},{3,2},{5,4},{7,6},{9,8},{11,10},{13,12},{15,14},{17,16},{19,... | collective-permute-start | bytes 1572872 | tf_op jit(solution)/shard_map/ppermute | solution.py:17
  133.7 144.5 %collective-permute-start.5 = (bf16[2,2,256,256]{2,3,0,1:T(8,128)(2,1)}, bf16[2,2,256,256]{2,3,0,1:T(8,128)(2,1)S(1)}, u32[]{:S(2)}, u32[]{:S(2)}) collective-permute-start(bf16[2,2,256,256]{2,3,0,1:T(8,128)(2,1)} %get-tuple-element.16), channel_id=1, source_target_pairs={{0,1},{2,3},{4,5},{6,7},{8,9},{10,11},{12,13},{14,15},{16,17},{18,... | collective-permute-start | bytes 1572872 | tf_op jit(solution)/shard_map/ppermute | solution.py:15
  134.9 143.2 %collective-permute-start.6 = (bf16[2,2,256,256]{2,3,0,1:T(8,128)(2,1)}, bf16[2,2,256,256]{2,3,0,1:T(8,128)(2,1)}, u32[]{:S(2)}, u32[]{:S(2)}) collective-permute-start(bf16[2,2,256,256]{2,3,0,1:T(8,128)(2,1)} %get-tuple-element.17), channel_id=1, source_target_pairs={{1,0},{3,2},{5,4},{7,6},{9,8},{11,10},{13,12},{15,14},{17,16},{19,... | collective-permute-start | bytes 1572872 | tf_op jit(solution)/shard_map/ppermute | solution.py:17
  184.3 48.2 %copy-start = (bf16[2,10,256,256]{2,3,0,1:T(8,128)(2,1)S(1)}, bf16[2,10,256,256]{2,3,0,1:T(8,128)(2,1)}, u32[]{:S(2)}) copy-start(bf16[2,10,256,256]{2,3,0,1:T(8,128)(2,1)} %fusion.1) | copy-start | bytes 7864324
  278.2 3.0 copy-start.4
where the time goes:
time: 348 us; the launch traced here: 343 us
  local copies, waits for them, and re-layouts  200 us (57%)
  waiting for transfers between devices  57.5 us (17%)
  matrix products  44.1 us (13%)
  starting transfers between devices  18.6 us (5%)
  other arithmetic  14.7 us (4%)
  between operations  6.18 us (2%)
    convert_element_type x3, local copies, waits for them, and re-layouts, advance(): return total.astype(jnp.bfloat16)  128 us
    ppermute x1, waiting for transfers between devices, shifted(): return lax.ppermute(block, axis, route)  57.5 us
    convert_element_type x1, local copies, waits for them, and re-layouts, shards(): jnp.sum(first_weight[:, :, None, None, None] * squares[None], axis=1)  41.1 us
    dot_general x6, matrix products, advance(): lax.dot_general(middle, blocks[state], (((2,), (1,)), ((1,), (0,))), pref...  40.4 us
    ppermute x3, starting transfers between devices, padded(): lax.ppermute(head, axis, [((i + 1) % count, i) for i in range(ends)])  11.6 us
    gather x4, local copies, waits for them, and re-layouts, measure(): diagonal = jnp.diagonal(environment, axis1=2, axis2=3).astype(jnp.float32)  11.2 us
    unnamed x14, local copies, waits for them, and re-layouts  10 us
  transfers between devices with their start and end apart: 7, of which 1 were waited for; matrix products, arithmetic and copies ran while one was open for 43% of the time, Pallas kernels for 0%

commit v1 on v0

v1 whole, which is shorter than its diff:
```python
import functools

import jax
import jax.numpy as jnp
from jax import lax
from jax.experimental import pallas as pl
from jax.experimental.pallas import tpu as pltpu
from jax.sharding import PartitionSpec as P

F32 = jnp.float32
BF16 = jnp.bfloat16
HALO = 2
RUNS = ((2, 5), (0, 2), (5, 8), (8, 10))


class Place:
    def __init__(self, sources, width):
        self.core = lax.axis_index("sec")
        self.pair = lax.axis_index("site")
        self.width = width
        middle = sources.shape[2] // 2
        sign = 2 * self.core - 1
        self.steps = []
        for site in range(2):
            charge = sources[2 * self.pair + site, 0, middle] - middle + 1
            self.steps.append([sign * (charge + 2 * state - 1) for state in range(2)])

    def local(self, b):
        return jnp.where(self.core == 0, self.width - 1 - b, b)


def dot(a, b):
    return jnp.dot(a, b, preferred_element_type=F32)


def dot_t(a, b):
    return lax.dot_general(a, b, (((0,), (0,)), ((), ())), preferred_element_type=F32)


def diagonal_row(block):
    half = block.shape[0] // 2
    row = lax.broadcasted_iota(jnp.int32, (half, half), 0)
    col = lax.broadcasted_iota(jnp.int32, (half, half), 1)
    parts = [
        jnp.sum(jnp.where(row == col, block[at : at + half, at : at + half], 0.0), axis=0, keepdims=True)
        for at in (0, half)
    ]
    return jnp.concatenate(parts, axis=1)


def pack(first, second):
    half = first.shape[0] // 2
    row = lax.broadcasted_iota(jnp.int32, (half, half), 0)
    col = lax.broadcasted_iota(jnp.int32, (half, half), 1)
    upper = row <= col

    def mixed(at):
        cut = slice(at, at + half)
        return jnp.where(upper, first[cut, cut], second[cut, cut])

    top = jnp.concatenate([mixed(0), first[:half, half:]], axis=1)
    bottom = jnp.concatenate([second[half:, :half], mixed(half)], axis=1)
    return jnp.concatenate([top, bottom], axis=0).astype(BF16)


def unpack(packed, diagonal, valid):
    half = packed.shape[0] // 2
    packed = jnp.where(valid, packed.astype(F32), 0.0)
    diagonal = jnp.where(valid, diagonal.astype(F32), 0.0)
    turned = packed.T
    row = lax.broadcasted_iota(jnp.int32, (half, half), 0)
    col = lax.broadcasted_iota(jnp.int32, (half, half), 1)

    def low(at):
        cut = slice(at, at + half)
        return jnp.where(row <= col, packed[cut, cut], turned[cut, cut])

    def high(at):
        cut = slice(at, at + half)
        mirrored = jnp.where(row < col, turned[cut, cut], packed[cut, cut])
        return jnp.where(row == col, diagonal[:, cut], mirrored)

    def whole(corner, ne, sw):
        top = jnp.concatenate([corner(0), ne], axis=1)
        bottom = jnp.concatenate([sw, corner(half)], axis=1)
        return jnp.concatenate([top, bottom], axis=0).astype(BF16)

    first = whole(low, packed[:half, half:], turned[half:, :half])
    second = whole(high, turned[:half, half:], packed[half:, :half])
    return first, second


def advance(pair_of, blocks, weight=None):
    size = blocks.shape[-1]
    middles = []
    for state in range(2):
        middle = dot(pair_of(state), blocks[state])
        halves = []
        for insert in range(2):
            part = middle[insert * size : (insert + 1) * size]
            if weight is not None:
                part = part * weight[insert][state]
            halves.append(part.astype(BF16))
        middles.append(jnp.concatenate(halves, axis=1))
    both = dot_t(blocks.reshape(2 * size, size), jnp.concatenate(middles, axis=0))
    return both[:, :size], both[:, size:]


def squares(place, blocks, weight, b):
    terms = [dot_t(blocks[state], blocks[state]) for state in range(2)]
    out = []
    for insert in range(2):
        total = 0.0
        for state in range(2):
            inside = b + place.steps[0][state] < place.width
            total = total + jnp.where(inside, weight[insert][state], 0.0) * terms[state]
        out.append(total)
    return out


def chosen_weights(operators, insert_at, which):
    return [
        [jnp.where(insert_at[0, k] == which, operators[k, s], 1.0) for s in range(2)] for k in range(2)
    ]


def trace_row(block, radius):
    return diagonal_row(block.astype(BF16).astype(F32)) * (radius * radius)


class Loads:
    def __init__(self):
        self.waiting = {}

    def start(self, key, source, target, sem):
        copy = pltpu.make_async_copy(source, target, sem)
        copy.start()
        self.waiting[key] = copy

    def wait(self, *keys):
        for key in keys:
            if key in self.waiting:
                self.waiting.pop(key).wait()


def first_kernel(width, run, sources, operators, insert_at, tensors, schmidt,
                 sent, boundary, traces, t0, t1, env, radius, sems):
    place = Place(sources, width)
    size = tensors.shape[-1]
    lo, hi = run
    count = hi - lo
    base = lo + jnp.minimum(place.steps[1][0], place.steps[1][1])
    loads = Loads()
    loads.start("radius", schmidt.at[pl.ds(2 * place.pair, 2)], radius, sems.at[0])
    needed = [base + i for i in range(count + 2)]
    for i, b in enumerate(needed + [0, 1]):
        loads.start(("t0", i), tensors.at[0, :, place.local(b)], t0.at[i], sems.at[1 + i])
    for i in range(count):
        loads.start(("t1", i), tensors.at[1, :, place.local(lo + i)], t1.at[i], sems.at[1 + count + 4 + i])
    u = chosen_weights(operators, insert_at, 0)
    v = chosen_weights(operators, insert_at, 1)
    traces[...] = jnp.zeros_like(traces)
    for i, b in enumerate(needed + [0, 1]):
        loads.wait(("t0", i))
        parts = squares(place, t0[i], u, b)
        for k in range(2):
            if i < count + 2:
                env[i, k * size : (k + 1) * size] = parts[k].astype(BF16)
            else:
                boundary[i - count - 2, k * size : (k + 1) * size] = parts[k].astype(BF16)
    loads.wait("radius")
    rows = []
    for i in range(count):
        loads.wait(("t1", i))
        parts = advance(lambda s: env[lo + i + place.steps[1][s] - base], t1[i], v)
        store_packed(sent, i, parts, rows)
        for k in range(2):
            row = radius[1, pl.ds(place.local(lo + i), 1)]
            traces[4 + k : 5 + k] += trace_row(parts[k], row)
    store_diagonals(sent, count, rows)


def store_packed(sent, i, parts, rows):
    size = parts[0].shape[0]
    sent[i * size : (i + 1) * size] = pack(*parts)
    rows.append(diagonal_row(parts[1]))


def store_diagonals(sent, count, rows):
    size = rows[0].shape[1]
    pad = jnp.zeros((16 - count, size), F32)
    sent[count * size : count * size + 16] = jnp.concatenate(rows + [pad], axis=0).astype(BF16)


def second_kernel(width, runs, sources, operators, insert_at, tensors, schmidt, halo, old_traces,
                  *rest):
    sents, rest = rest[: len(runs)], rest[len(runs) :]
    traces, t0, t1, env, radius, sems = rest
    place = Place(sources, width)
    size = tensors.shape[-1]
    loads = Loads()
    loads.start("radius", schmidt.at[pl.ds(2 * place.pair, 2)], radius, sems.at[0])
    for b in range(width):
        loads.start(("t0", b), tensors.at[0, :, place.local(b)], t0.at[b], sems.at[1 + b])
    loads.start("halo", halo, env.at[pl.ds(0, 2)], sems.at[1 + 2 * width])
    order = [b for lo, hi in runs for b in range(lo, hi)]
    for b in order:
        loads.start(("t1", b), tensors.at[1, :, place.local(b)], t1.at[b], sems.at[1 + width + b])
    u = chosen_weights(operators, insert_at, 0)
    v = chosen_weights(operators, insert_at, 1)
    env[HALO + width :] = jnp.zeros_like(env[HALO + width :])
    traces[...] = old_traces[...]
    loads.wait("radius")
    for b in range(width):
        loads.wait(("t0", b))
        parts = squares(place, t0[b], u, b)
        row = radius[0, pl.ds(place.local(b), 1)]
        for k in range(2):
            env[HALO + b, k * size : (k + 1) * size] = parts[k].astype(BF16)
            traces[k : k + 1] += trace_row(parts[k], row)
    loads.wait("halo")
    for (lo, hi), sent in zip(runs, sents):
        rows = []
        for b in range(lo, hi):
            loads.wait(("t1", b))
            parts = advance(lambda s: env[HALO + b + place.steps[1][s]], t1[b], v)
            store_packed(sent, b - lo, parts, rows)
            row = radius[1, pl.ds(place.local(b), 1)]
            for k in range(2):
                traces[4 + k : 5 + k] += trace_row(parts[k], row)
        store_diagonals(sent, hi - lo, rows)


def mirrored_halo(b):
    return HALO - 1 - b


def receive_kernel(width, runs, sources, tensors, schmidt, halo, old_traces, *rest):
    arrived, rest = rest[: len(runs)], rest[len(runs) :]
    out, traces, t0, env, radius, sems = rest
    place = Place(sources, width)
    size = tensors.shape[-1]
    valid = place.pair > 0
    loads = Loads()
    loads.start("radius", schmidt.at[pl.ds(2 * place.pair, 2)], radius, sems.at[0])
    for b in range(width):
        loads.start(("t0", b), tensors.at[0, :, place.local(b)], t0.at[b], sems.at[1 + b])
    traces[...] = old_traces[...]
    env[HALO + width :] = jnp.zeros_like(env[HALO + width :])

    def put(buffer, i, count, slot):
        parts = unpack(buffer[i * size : (i + 1) * size], buffer[count * size : count * size + 16][i : i + 1], valid)
        for k in range(2):
            env[slot, k * size : (k + 1) * size] = parts[k]

    for i in range(HALO):
        put(halo, i, HALO, HALO - 1 - i)
    for (lo, hi), buffer in zip(runs, arrived):
        for b in range(lo, hi):
            put(buffer, b - lo, hi - lo, HALO + b)
    loads.wait("radius")
    for b in range(width):
        loads.wait(("t0", b))
        parts = advance(lambda s: env[HALO + b + place.steps[0][s]], t0[b])
        row = radius[0, pl.ds(place.local(b), 1)]
        for k in range(2):
            out[b, k * size : (k + 1) * size] = parts[k].astype(BF16)
            traces[2 + k : 3 + k] += trace_row(parts[k], row)


def last_kernel(width, sources, tensors, schmidt, halo, middle, old_traces, out, traces, t1, env, stage, radius, sems):
    place = Place(sources, width)
    size = tensors.shape[-1]
    loads = Loads()
    loads.start("radius", schmidt.at[pl.ds(2 * place.pair, 2)], radius, sems.at[0])
    for b in range(width):
        loads.start(("t1", b), tensors.at[1, :, place.local(b)], t1.at[b], sems.at[1 + b])
    loads.start("halo", halo, env.at[pl.ds(0, 2)], sems.at[1 + width])
    loads.start("middle", middle, env.at[pl.ds(HALO, width)], sems.at[2 + width])
    traces[...] = old_traces[...]
    env[HALO + width :] = jnp.zeros_like(env[HALO + width :])
    loads.wait("radius", "halo", "middle")
    stores = Loads()
    for b in range(width):
        loads.wait(("t1", b))
        parts = advance(lambda s: env[HALO + b + place.steps[1][s]], t1[b])
        row = radius[1, pl.ds(place.local(b), 1)]
        for k in range(2):
            stage[b, k] = parts[k].astype(BF16)
            traces[6 + k : 7 + k] += trace_row(parts[k], row)
        stores.start(b, stage.at[b], out.at[0, :, place.local(b)], sems.at[3 + width + b])
    for b in range(width):
        stores.wait(b)


SMEM = pl.BlockSpec(memory_space=pltpu.SMEM)
VMEM = pl.BlockSpec(memory_space=pltpu.VMEM)
HBM = pl.BlockSpec(memory_space=pl.ANY)
PARAMS = pltpu.CompilerParams(vmem_limit_bytes=56 * 2**20)


def shards(tensors, sources, operators, insert_at, schmidt):
    width, size = tensors.shape[2], tensors.shape[-1]
    pairs = lax.axis_size("site")
    ring = [(i, (i + 1) % pairs) for i in range(pairs)]
    swap = [(0, 1), (1, 0)]

    def message(run):
        return jax.ShapeDtypeStruct(((run[1] - run[0]) * size + 16, size), BF16)

    trace_shape = jax.ShapeDtypeStruct((8, size), F32)
    edge_shape = jax.ShapeDtypeStruct((HALO, 2 * size, size), BF16)
    tensor_room = lambda n: pltpu.VMEM((n, 2, size, size), BF16)
    env_room = lambda n: pltpu.VMEM((n, 2 * size, size), BF16)
    radius_room = pltpu.VMEM((2,) + schmidt.shape[1:], F32)

    run = RUNS[0]
    count = run[1] - run[0]
    sent0, boundary, traces = pl.pallas_call(
        functools.partial(first_kernel, width, run),
        out_shape=(message(run), edge_shape, trace_shape),
        in_specs=[SMEM, SMEM, SMEM, HBM, HBM],
        out_specs=(VMEM, VMEM, VMEM),
        scratch_shapes=[tensor_room(count + 4), tensor_room(count), env_room(count + 2), radius_room,
                        pltpu.SemaphoreType.DMA((1 + 2 * count + 4,))],
        compiler_params=PARAMS,
    )(sources, operators, insert_at, tensors, schmidt)
    halo = lax.ppermute(boundary, "sec", swap)
    halo = halo[::-1]
    got = [lax.ppermute(sent0, "site", ring)]
    runs = RUNS[1:]
    *sents, traces = pl.pallas_call(
        functools.partial(second_kernel, width, runs),
        out_shape=tuple(message(r) for r in runs) + (trace_shape,),
        in_specs=[SMEM, SMEM, SMEM, HBM, HBM, HBM, VMEM],
        out_specs=(VMEM,) * (len(runs) + 1),
        scratch_shapes=[tensor_room(width), tensor_room(width), env_room(width + 2 * HALO), radius_room,
                        pltpu.SemaphoreType.DMA((2 + 2 * width,))],
        compiler_params=PARAMS,
    )(sources, operators, insert_at, tensors, schmidt, halo, traces)
    got += [lax.ppermute(s, "site", ring) for s in sents]
    halo = lax.ppermute(got[1], "sec", swap)
    middle, traces = pl.pallas_call(
        functools.partial(receive_kernel, width, RUNS),
        out_shape=(jax.ShapeDtypeStruct((width, 2 * size, size), BF16), trace_shape),
        in_specs=[SMEM, HBM, HBM, VMEM, VMEM] + [VMEM] * len(RUNS),
        out_specs=(VMEM, VMEM),
        scratch_shapes=[tensor_room(width), env_room(width + 2 * HALO), radius_room,
                        pltpu.SemaphoreType.DMA((1 + width,))],
        compiler_params=PARAMS,
    )(sources, tensors, schmidt, halo, traces, *got)
    halo = lax.ppermute(middle[:HALO], "sec", swap)[::-1]
    final, traces = pl.pallas_call(
        functools.partial(last_kernel, width),
        out_shape=(jax.ShapeDtypeStruct((1, 2, width, size, size), BF16), trace_shape),
        in_specs=[SMEM, HBM, HBM, HBM, HBM, VMEM],
        out_specs=(HBM, VMEM),
        scratch_shapes=[tensor_room(width), env_room(width + 2 * HALO), pltpu.VMEM((width, 2, size, size), BF16),
                        radius_room, pltpu.SemaphoreType.DMA((3 + 2 * width,))],
        compiler_params=PARAMS,
    )(sources, tensors, schmidt, halo, middle, traces)
    other = lax.ppermute(traces, "sec", swap)
    correlation = jnp.sum(traces + other, axis=1).reshape(2, 2, 2)
    return final, correlation


def solution(mesh):
    placed = (
        P(("grp", "site"), None, "sec", None, None),
        P("grp", None, None),
        P(),
        P(("grp", "site"), None),
        P("grp", "sec", None),
    )
    return jax.shard_map(
        shards,
        mesh=mesh,
        in_specs=placed,
        out_specs=(P(("grp", "site"), None, "sec", None, None), P(("grp", "site"), None, None)),
        check_vma=False,
    )
```

time: 348 us -> 86.7 us (0.25)
  the two profiles are of different devices: /device:TPU:17 before, /device:TPU:0 now
where the time goes in v1:
time: 86.7 us; the launch traced here: 86.3 us
  Pallas kernels  37 us (43%)
  waiting for transfers between devices  33.4 us (39%)
  starting transfers between devices  8.29 us (10%)
  local copies, waits for them, and re-layouts  6.02 us (7%)
    ppermute x3, waiting for transfers between devices, shards(): got += [lax.ppermute(s, 'site', ring) for s in sents]  19.9 us
    pallas_call x1, Pallas kernels, shards(): pl.pallas_call(functools.partial(last_kernel, width), out_shape=(jax.Shap...  10.9 us
    pallas_call x1, Pallas kernels, shards(): pl.pallas_call(functools.partial(second_kernel, width, runs), out_shape=t...  10.1 us
    pallas_call x1, Pallas kernels, shards(): pl.pallas_call(functools.partial(receive_kernel, width, RUNS), out_shape=...  9.69 us
    ppermute x1, waiting for transfers between devices, shards(): got = [lax.ppermute(sent0, 'site', ring)]  8.6 us
    pallas_call x1, Pallas kernels, shards(): pl.pallas_call(functools.partial(first_kernel, width, run), out_shape=(me...  6.42 us
    ppermute x3, starting transfers between devices, shards(): got += [lax.ppermute(s, 'site', ring) for s in sents]  5.98 us
    unnamed x13, local copies, waits for them, and re-layouts  2.6 us
  transfers between devices with their start and end apart: 8, of which 6 were waited for; matrix products, arithmetic and copies ran while one was open for 0% of the time, Pallas kernels for 0%

profile of v1, /device:TPU:0, one launch (start us, length us, event | category | flops | bytes accessed | tf_op | source)
XLA Modules:
  0.0 86.3 jit_solution(6586364831685405970)
XLA Ops:
  0.6 1.7 %copy.10.schmidt = f32[16,10,256]{2,1,0:T(8,128)} copy(f32[16,10,256]{2,0,1:T(8,128)} %param.9) | data formatting | bytes 327680 | tf_op args[4]
  2.3 6.4 %shard_map.68 = (bf16[784,256]{1,0:T(8,128)(2,1)}, bf16[2,512,256]{2,1,0:T(8,128)(2,1)}, f32[8,256]{1,0:T(8,128)}) custom-call(s32[16,2,20]{2,1,0:T(2,128)} %sources.7, f32[2,2]{1,0:T(2,128)} %operators.3, s32[1,2]{1,0:T(1,128)} %insert_at.3, bf16[2,2,10,256,256]{4,3,2,1,0:T(8,128)(2,1)} %tensors.7, f32[16,10,256]{2,1,0:T(8,128)} %copy.10.schmidt), custom_call_target="tpu_custom_call" | custom-call | tf_op jit(solution)/shard_map/pallas_call | solution.py:319
  8.8 0.5 collective-permute-start
  9.3 1.7 %collective-permute-done = bf16[2,512,256]{2,1,0:T(8,128)(2,1)S(1)} collective-permute-done((bf16[2,512,256]{2,1,0:T(8,128)(2,1)}, bf16[2,512,256]{2,1,0:T(8,128)(2,1)S(1)}, u32[]{:S(2)}, u32[]{:S(2)}) %collective-permute-start) | collective-permute-done | bytes 524320 | tf_op jit(solution)/shard_map/ppermute | solution.py:328
  11.0 0.8 rev.6.halo
  11.9 10.1 %shard_map.69 = (bf16[528,256]{1,0:T(8,128)(2,1)}, bf16[784,256]{1,0:T(8,128)(2,1)}, bf16[528,256]{1,0:T(8,128)(2,1)}, f32[8,256]{1,0:T(8,128)}) custom-call(s32[16,2,20]{2,1,0:T(2,128)} %sources.7, f32[2,2]{1,0:T(2,128)} %operators.3, s32[1,2]{1,0:T(1,128)} %insert_at.3, bf16[2,2,10,256,256]{4,3,2,1,0:T(8,128)(2,1)} %tensors.7, ...), custom_call_target="tpu_custom_call" | custom-call | tf_op jit(solution)/shard_map/pallas_call | solution.py:332
  21.9 2.9 %collective-permute-start.1 = (bf16[528,256]{1,0:T(8,128)(2,1)}, bf16[528,256]{1,0:T(8,128)(2,1)S(1)}, u32[]{:S(2)}, u32[]{:S(2)}) collective-permute-start(bf16[528,256]{1,0:T(8,128)(2,1)} %get-tuple-element.15), channel_id=1, source_target_pairs={{0,2},{2,4},{4,6},{6,8},{8,10},{10,12},{12,14},{14,0},{1,3},{3,5},... | collective-permute-start | bytes 811016 | tf_op jit(solution)/shard_map/ppermute | solution.py:341
  24.9 0.0 copy-done.5
  24.9 1.5 %collective-permute-start.3 = (bf16[784,256]{1,0:T(8,128)(2,1)S(1)}, bf16[784,256]{1,0:T(8,128)(2,1)S(1)}, u32[]{:S(2)}, u32[]{:S(2)}) collective-permute-start(bf16[784,256]{1,0:T(8,128)(2,1)S(1)} %copy-done.5), channel_id=1, source_target_pairs={{0,2},{2,4},{4,6},{6,8},{8,10},{10,12},{12,14},{14,0},{1,3},{3,5},... | collective-permute-start | bytes 1204232 | tf_op jit(solution)/shard_map/ppermute | solution.py:330
  26.4 1.5 %collective-permute-start.4 = (bf16[784,256]{1,0:T(8,128)(2,1)}, bf16[784,256]{1,0:T(8,128)(2,1)S(1)}, u32[]{:S(2)}, u32[]{:S(2)}) collective-permute-start(bf16[784,256]{1,0:T(8,128)(2,1)} %get-tuple-element.18), channel_id=1, source_target_pairs={{0,2},{2,4},{4,6},{6,8},{8,10},{10,12},{12,14},{14,0},{1,3},{3,5},... | collective-permute-start | bytes 1204232 | tf_op jit(solution)/shard_map/ppermute | solution.py:341
  27.9 1.5 %collective-permute-start.5 = (bf16[528,256]{1,0:T(8,128)(2,1)}, bf16[528,256]{1,0:T(8,128)(2,1)S(1)}, u32[]{:S(2)}, u32[]{:S(2)}) collective-permute-start(bf16[528,256]{1,0:T(8,128)(2,1)} %get-tuple-element.19), channel_id=1, source_target_pairs={{0,2},{2,4},{4,6},{6,8},{8,10},{10,12},{12,14},{14,0},{1,3},{3,5},... | collective-permute-start | bytes 811016 | tf_op jit(solution)/shard_map/ppermute | solution.py:341
  29.4 6.0 %collective-permute-done.1.rest_1_ = bf16[528,256]{1,0:T(8,128)(2,1)S(1)} collective-permute-done((bf16[528,256]{1,0:T(8,128)(2,1)}, bf16[528,256]{1,0:T(8,128)(2,1)S(1)}, u32[]{:S(2)}, u32[]{:S(2)}) %collective-permute-start.1) | collective-permute-done | bytes 270368 | tf_op jit(solution)/shard_map/ppermute | solution.py:341
  35.4 0.0 collective-permute-start.2
  35.4 8.6 %collective-permute-done.3.rest_0_ = bf16[784,256]{1,0:T(8,128)(2,1)S(1)} collective-permute-done((bf16[784,256]{1,0:T(8,128)(2,1)S(1)}, bf16[784,256]{1,0:T(8,128)(2,1)S(1)}, u32[]{:S(2)}, u32[]{:S(2)}) %collective-permute-start.3) | collective-permute-done | bytes 401440 | tf_op jit(solution)/shard_map/ppermute | solution.py:330
  44.0 13.9 %collective-permute-done.5.rest_3_ = bf16[528,256]{1,0:T(8,128)(2,1)S(1)} collective-permute-done((bf16[528,256]{1,0:T(8,128)(2,1)}, bf16[528,256]{1,0:T(8,128)(2,1)S(1)}, u32[]{:S(2)}, u32[]{:S(2)}) %collective-permute-start.5) | collective-permute-done | bytes 270368 | tf_op jit(solution)/shard_map/ppermute | solution.py:341
  57.9 0.0 collective-permute-done.4.rest_2_
  57.9 0.0 collective-permute-done.2.halo
  57.9 0.0 copy-start.4
  58.0 0.0 copy-done.2
  58.0 0.7 copy-done.3
  58.6 0.2 copy-done.1
  58.8 0.1 copy-done.4
  58.8 9.7 %shard_map.70 = (bf16[10,512,256]{2,1,0:T(8,128)(2,1)}, f32[8,256]{1,0:T(8,128)}) custom-call(s32[16,2,20]{2,1,0:T(2,128)} %sources.7, bf16[2,2,10,256,256]{4,3,2,1,0:T(8,128)(2,1)} %tensors.7, f32[16,10,256]{2,1,0:T(8,128)} %copy.10.schmidt, bf16[528,256]{1,0:T(8,128)(2,1)} %copy-done.4, f32[8,256]{1,0:T(8,128)} %get-tuple-element.16.old_traces, ...), custom_call_target="tpu_custom_call" | custom-call | tf_op jit(solution)/shard_map/pallas_call | solution.py:343
  68.5 1.1 %slice.3 = bf16[2,512,256]{2,1,0:T(8,128)(2,1)S(1)} slice(bf16[10,512,256]{2,1,0:T(8,128)(2,1)} %get-tuple-element.20.middle), slice={[0:2], [0:512], [0:256]} | slice | bytes 1048576 | tf_op jit(solution)/shard_map/slice | solution.py:352
  69.6 0.1 collective-permute-start.6
  69.7 1.9 %collective-permute-done.6 = bf16[2,512,256]{2,1,0:T(8,128)(2,1)S(1)} collective-permute-done((bf16[2,512,256]{2,1,0:T(8,128)(2,1)S(1)}, bf16[2,512,256]{2,1,0:T(8,128)(2,1)S(1)}, u32[]{:S(2)}, u32[]{:S(2)}) %collective-permute-start.6) | collective-permute-done | bytes 524320 | tf_op jit(solution)/shard_map/ppermute | solution.py:352
  71.6 0.8 rev.7.halo
  72.4 10.9 %shard_map.71 = (bf16[1,2,10,256,256]{4,3,2,1,0:T(8,128)(2,1)}, f32[8,256]{1,0:T(8,128)}) custom-call(s32[16,2,20]{2,1,0:T(2,128)} %sources.7, bf16[2,2,10,256,256]{4,3,2,1,0:T(8,128)(2,1)} %tensors.7, f32[16,10,256]{2,1,0:T(8,128)} %copy.10.schmidt, bf16[2,512,256]{2,1,0:T(8,128)(2,1)} %rev.7.halo, bf16[10,512,256]{2,1,0:T(8,128)(2,1)} %get-tuple-element.20.middle, ...), custom_call_target="tpu_custom_call" | custom-call | tf_op jit(solution)/shard_map/pallas_call | solution.py:353
  83.3 0.2 collective-permute-start.7
  83.5 1.3 %collective-permute-done.7 = f32[8,256]{1,0:T(8,128)S(1)} collective-permute-done((f32[8,256]{1,0:T(8,128)}, f32[8,256]{1,0:T(8,128)S(1)}, u32[]{:S(2)}, u32[]{:S(2)}) %collective-permute-start.7) | collective-permute-done | bytes 8224 | tf_op jit(solution)/shard_map/ppermute | solution.py:362
  84.8 0.8 add_reduce_fusion
  85.6 0.7 reshape.7
  (6 shorter events, 0.0 us)
Async XLA Ops:
  8.8 2.3 %collective-permute-start = (bf16[2,512,256]{2,1,0:T(8,128)(2,1)}, bf16[2,512,256]{2,1,0:T(8,128)(2,1)S(1)}, u32[]{:S(2)}, u32[]{:S(2)}) collective-permute-start(bf16[2,512,256]{2,1,0:T(8,128)(2,1)} %get-tuple-element.13), channel_id=1, source_target_pairs={{0,1},{1,0},{2,3},{3,2},{4,5},{5,4},{6,7},{7,6},{8,9},{9,8},{10,11... | collective-permute-start | bytes 1572872 | tf_op jit(solution)/shard_map/ppermute | solution.py:328
  11.9 13.0 %copy-start.5 = (bf16[784,256]{1,0:T(8,128)(2,1)S(1)}, bf16[784,256]{1,0:T(8,128)(2,1)}, u32[]{:S(2)}) copy-start(bf16[784,256]{1,0:T(8,128)(2,1)} %get-tuple-element.17) | copy-start | bytes 1204228
  21.9 13.5 %collective-permute-start.1 = (bf16[528,256]{1,0:T(8,128)(2,1)}, bf16[528,256]{1,0:T(8,128)(2,1)S(1)}, u32[]{:S(2)}, u32[]{:S(2)}) collective-permute-start(bf16[528,256]{1,0:T(8,128)(2,1)} %get-tuple-element.15), channel_id=1, source_target_pairs={{0,2},{2,4},{4,6},{6,8},{8,10},{10,12},{12,14},{14,0},{1,3},{3,5},... | collective-permute-start | bytes 811016 | tf_op jit(solution)/shard_map/ppermute | solution.py:341
  24.9 19.1 %collective-permute-start.3 = (bf16[784,256]{1,0:T(8,128)(2,1)S(1)}, bf16[784,256]{1,0:T(8,128)(2,1)S(1)}, u32[]{:S(2)}, u32[]{:S(2)}) collective-permute-start(bf16[784,256]{1,0:T(8,128)(2,1)S(1)} %copy-done.5), channel_id=1, source_target_pairs={{0,2},{2,4},{4,6},{6,8},{8,10},{10,12},{12,14},{14,0},{1,3},{3,5},... | collective-permute-start | bytes 1204232 | tf_op jit(solution)/shard_map/ppermute | solution.py:330
  26.4 31.5 %collective-permute-start.4 = (bf16[784,256]{1,0:T(8,128)(2,1)}, bf16[784,256]{1,0:T(8,128)(2,1)S(1)}, u32[]{:S(2)}, u32[]{:S(2)}) collective-permute-start(bf16[784,256]{1,0:T(8,128)(2,1)} %get-tuple-element.18), channel_id=1, source_target_pairs={{0,2},{2,4},{4,6},{6,8},{8,10},{10,12},{12,14},{14,0},{1,3},{3,5},... | collective-permute-start | bytes 1204232 | tf_op jit(solution)/shard_map/ppermute | solution.py:341
  27.9 30.0 %collective-permute-start.5 = (bf16[528,256]{1,0:T(8,128)(2,1)}, bf16[528,256]{1,0:T(8,128)(2,1)S(1)}, u32[]{:S(2)}, u32[]{:S(2)}) collective-permute-start(bf16[528,256]{1,0:T(8,128)(2,1)} %get-tuple-element.19), channel_id=1, source_target_pairs={{0,2},{2,4},{4,6},{6,8},{8,10},{10,12},{12,14},{14,0},{1,3},{3,5},... | collective-permute-start | bytes 811016 | tf_op jit(solution)/shard_map/ppermute | solution.py:341
  35.4 22.6 %copy-start.2 = (bf16[528,256]{1,0:T(8,128)(2,1)}, bf16[528,256]{1,0:T(8,128)(2,1)S(1)}, u32[]{:S(2)}) copy-start(bf16[528,256]{1,0:T(8,128)(2,1)S(1)} %collective-permute-done.1.rest_1_) | copy-start | bytes 811012
  35.4 22.5 %collective-permute-start.2 = (bf16[528,256]{1,0:T(8,128)(2,1)S(1)}, bf16[528,256]{1,0:T(8,128)(2,1)S(1)}, u32[]{:S(2)}, u32[]{:S(2)}) collective-permute-start(bf16[528,256]{1,0:T(8,128)(2,1)S(1)} %collective-permute-done.1.rest_1_), channel_id=1, source_target_pairs={{0,1},{1,0},{2,3},{3,2},{4,5},{5,4},{6,7},{7,6},{8,9},{9,8},{10,11... | collective-permute-start | bytes 811016 | tf_op jit(solution)/shard_map/ppermute | solution.py:342
  44.0 14.0 %copy-start = (bf16[784,256]{1,0:T(8,128)(2,1)}, bf16[784,256]{1,0:T(8,128)(2,1)S(1)}, u32[]{:S(2)}) copy-start(bf16[784,256]{1,0:T(8,128)(2,1)S(1)} %collective-permute-done.3.rest_0_) | copy-start | bytes 1204228
  57.9 0.7 copy-start.3
  57.9 0.8 copy-start.1
  57.9 0.9 %copy-start.4 = (bf16[528,256]{1,0:T(8,128)(2,1)}, bf16[528,256]{1,0:T(8,128)(2,1)S(1)}, u32[]{:S(2)}) copy-start(bf16[528,256]{1,0:T(8,128)(2,1)S(1)} %collective-permute-done.2.halo) | copy-start | bytes 811012
  69.6 2.0 %collective-permute-start.6 = (bf16[2,512,256]{2,1,0:T(8,128)(2,1)S(1)}, bf16[2,512,256]{2,1,0:T(8,128)(2,1)S(1)}, u32[]{:S(2)}, u32[]{:S(2)}) collective-permute-start(bf16[2,512,256]{2,1,0:T(8,128)(2,1)S(1)} %slice.3), channel_id=1, source_target_pairs={{0,1},{1,0},{2,3},{3,2},{4,5},{5,4},{6,7},{7,6},{8,9},{9,8},{10,11... | collective-permute-start | bytes 1572872 | tf_op jit(solution)/shard_map/ppermute | solution.py:352
  83.3 1.4 %collective-permute-start.7 = (f32[8,256]{1,0:T(8,128)}, f32[8,256]{1,0:T(8,128)S(1)}, u32[]{:S(2)}, u32[]{:S(2)}) collective-permute-start(f32[8,256]{1,0:T(8,128)} %get-tuple-element.23), channel_id=1, source_target_pairs={{0,1},{1,0},{2,3},{3,2},{4,5},{5,4},{6,7},{7,6},{8,9},{9,8},{10,11... | collective-permute-start | bytes 24584 | tf_op jit(solution)/shard_map/ppermute | solution.py:362

commit v2 on v0

v2 whole, which is shorter than its diff:
```python
import functools

import jax
import jax.numpy as jnp
from jax import lax
from jax.experimental import pallas as pl
from jax.experimental.pallas import tpu as pltpu
from jax.sharding import PartitionSpec as P

F32 = jnp.float32
BF16 = jnp.bfloat16
REACH = 4
HALO = 2
class Place:
    def __init__(self, sources, width):
        self.core = lax.axis_index("sec")
        self.pair = lax.axis_index("site")
        self.width = width
        middle = sources.shape[2] // 2
        sign = 2 * self.core - 1
        self.steps = []
        for site in range(2):
            charge = sources[2 * self.pair + site, 0, middle] - middle + 1
            self.steps.append([sign * (charge + 2 * state - 1) for state in range(2)])

    def local(self, b):
        return jnp.where(self.core == 0, self.width - 1 - b, b)


def dot(a, b):
    return jnp.dot(a, b, preferred_element_type=F32)


def dot_t(a, b):
    return lax.dot_general(a, b, (((0,), (0,)), ((), ())), preferred_element_type=F32)


def diagonal_row(block):
    half = block.shape[0] // 2
    row = lax.broadcasted_iota(jnp.int32, (half, half), 0)
    col = lax.broadcasted_iota(jnp.int32, (half, half), 1)
    parts = [
        jnp.sum(jnp.where(row == col, block[at : at + half, at : at + half], 0.0), axis=0, keepdims=True)
        for at in (0, half)
    ]
    return jnp.concatenate(parts, axis=1)


def pack(first, second):
    half = first.shape[0] // 2
    row = lax.broadcasted_iota(jnp.int32, (half, half), 0)
    col = lax.broadcasted_iota(jnp.int32, (half, half), 1)
    upper = row <= col

    def mixed(at):
        cut = slice(at, at + half)
        return jnp.where(upper, first[cut, cut], second[cut, cut])

    top = jnp.concatenate([mixed(0), first[:half, half:]], axis=1)
    bottom = jnp.concatenate([second[half:, :half], mixed(half)], axis=1)
    return jnp.concatenate([top, bottom], axis=0).astype(BF16)


def unpack(packed, diagonal, valid):
    half = packed.shape[0] // 2
    packed = jnp.where(valid, packed, jnp.zeros_like(packed))
    diagonal = jnp.where(valid, diagonal.astype(F32), 0.0)
    turned = packed.T
    row = lax.broadcasted_iota(jnp.int32, (half, half), 0)
    col = lax.broadcasted_iota(jnp.int32, (half, half), 1)

    def corners(at):
        cut = slice(at, at + half)
        straight, mirrored = packed[cut, cut].astype(F32), turned[cut, cut].astype(F32)
        low = jnp.where(row <= col, straight, mirrored)
        high = jnp.where(row == col, diagonal[:, cut], jnp.where(row < col, mirrored, straight))
        return low.astype(BF16), high.astype(BF16)

    def whole(north, ne, sw, south):
        top = jnp.concatenate([north, ne], axis=1)
        bottom = jnp.concatenate([sw, south], axis=1)
        return jnp.concatenate([top, bottom], axis=0)

    north, south = corners(0), corners(half)
    first = whole(north[0], packed[:half, half:], turned[half:, :half], south[0])
    second = whole(north[1], turned[:half, half:], packed[half:, :half], south[1])
    return first, second


def advance(env, slots, blocks, weight=None):
    size = blocks.shape[-1]
    middles = []
    for state in range(2):
        turned = blocks[state].T
        halves = []
        for insert in range(2):
            part = dot(turned, env[slots[state], insert * size : (insert + 1) * size])
            if weight is not None:
                part = part * weight[insert][state]
            halves.append(part.astype(BF16))
        middles.append(jnp.concatenate(halves, axis=0))
    both = dot(jnp.concatenate(middles, axis=1), blocks.reshape(2 * size, size))
    return both[:size], both[size:]


def squares(place, blocks, weight, b):
    terms = [dot(blocks[state].T, blocks[state]) for state in range(2)]
    out = []
    for insert in range(2):
        total = 0.0
        for state in range(2):
            inside = b + place.steps[0][state] < place.width
            total = total + jnp.where(inside, weight[insert][state], 0.0) * terms[state]
        out.append(total)
    return out


def chosen_weights(operators, insert_at, which):
    return [
        [jnp.where(insert_at[0, k] == which, operators[k, s], 1.0) for s in range(2)] for k in range(2)
    ]


def add_traces(place, traces, at, site, b, parts, radius):
    row = radius[place.local(b), pl.ds(2 * place.pair + site, 1)]
    for k in range(2):
        traces[at + k : at + k + 1] += diagonal_row(parts[k].astype(BF16).astype(F32)) * (row * row)


def slots_of(place, site, b):
    return [REACH + b + place.steps[site][state] for state in range(2)]


def store_env(env, slot, parts):
    size = parts[0].shape[0]
    for k in range(2):
        env[slot, k * size : (k + 1) * size] = parts[k].astype(BF16)


def send(place, env, t1, weight, traces, radius, sent, run):
    rows = []
    lo, hi = run
    for b in range(lo, hi):
        parts = advance(env, slots_of(place, 1, b), t1[b], weight)
        size = parts[0].shape[0]
        sent[(b - lo) * size : (b - lo + 1) * size] = pack(*parts)
        rows.append(diagonal_row(parts[1]))
        add_traces(place, traces, 4, 1, b, parts, radius)
    rows.append(jnp.zeros((16 - len(rows), size), F32))
    sent[(hi - lo) * size : (hi - lo) * size + 16] = jnp.concatenate(rows, axis=0).astype(BF16)


def take(place, buffer, i, count, env, slot):
    size = buffer.shape[1]
    diagonal = buffer[count * size : count * size + 16][i : i + 1]
    store_env(env, slot, unpack(buffer[i * size : (i + 1) * size], diagonal, place.pair > 0))


class Loads:
    def __init__(self):
        self.waiting = {}

    def start(self, key, source, target, sem):
        copy = pltpu.make_async_copy(source, target, sem)
        copy.start()
        self.waiting[key] = copy

    def wait(self, *keys):
        for key in keys:
            if key in self.waiting:
                self.waiting.pop(key).wait()


def first_kernel(width, run, sources, operators, insert_at, tensors, schmidt,
                 sent, edge, env, t0, t1, radius, traces, sems):
    place = Place(sources, width)
    lo, hi = run
    loads = Loads()
    ends = list(range(lo, width)) + list(range(lo))
    near = [b for b in ends if lo - HALO <= b < hi + HALO]
    for b in near:
        loads.start(("t0", b), tensors.at[0, :, place.local(b)], t0.at[b], sems.at[0, b])
    for b in range(lo, hi):
        loads.start(("t1", b), tensors.at[1, :, place.local(b)], t1.at[b], sems.at[1, b])
    loads.start("radius", schmidt, radius, sems.at[0, width])
    for b in ends:
        if b not in near:
            loads.start(("t0", b), tensors.at[0, :, place.local(b)], t0.at[b], sems.at[0, b])
    for b in ends:
        if not lo <= b < hi:
            loads.start(("t1", b), tensors.at[1, :, place.local(b)], t1.at[b], sems.at[1, b])
    u = chosen_weights(operators, insert_at, 0)
    v = chosen_weights(operators, insert_at, 1)
    traces[...] = jnp.zeros_like(traces)
    env[REACH + width :] = jnp.zeros_like(env[REACH + width :])
    for b in near:
        loads.wait(("t0", b))
        parts = squares(place, t0[b], u, b)
        store_env(env, REACH + b, parts)
        if b < HALO:
            store_env(edge, HALO - 1 - b, parts)
            edge[2 * HALO - 1 - b] = t0[b].reshape(edge.shape[1:])
    for b in range(lo, hi):
        loads.wait(("t1", b))
    loads.wait("radius")
    send(place, env, t1, v, traces, radius, sent, run)
    for b in ends:
        loads.wait(("t0", b), ("t1", b))


def second_kernel(width, first_run, runs, sources, operators, insert_at, old_env, halo, t0, t1, radius, old_traces, *rest):
    env, sents, traces = rest[0], rest[1:-1], rest[-1]
    place = Place(sources, width)
    size = t0.shape[-1]
    u = chosen_weights(operators, insert_at, 0)
    v = chosen_weights(operators, insert_at, 1)
    traces[...] = old_traces[...]
    for i in range(HALO):
        env[REACH - HALO + i] = halo[i]
    lo, hi = first_run
    for b in range(width):
        if not lo - HALO <= b < hi + HALO:
            parts = squares(place, t0[b], u, b)
            store_env(env, REACH + b, parts)
        else:
            parts = [env[REACH + b, k * size : (k + 1) * size] for k in range(2)]
        add_traces(place, traces, 0, 0, b, parts, radius)
    for run, sent in zip(runs, sents):
        send(place, env, t1, v, traces, radius, sent, run)


def open_kernel(width, run, sources, buffer, env, piece):
    place = Place(sources, width)
    env[REACH + width :] = jnp.zeros_like(env[REACH + width :])
    lo, hi = run
    size = buffer.shape[1]
    for b in range(lo, hi):
        take(place, buffer, b - lo, hi - lo, env, REACH + b)
    piece[: HALO * size] = buffer[: HALO * size]
    piece[HALO * size :] = buffer[(hi - lo) * size :]


def middle_blocks(place, todo, env, middle, t0, traces, radius):
    for b in range(*todo):
        parts = advance(env, slots_of(place, 0, b), t0[b])
        store_env(middle, REACH + b, parts)
        add_traces(place, traces, 2, 0, b, parts, radius)


def final_blocks(place, todo, middle, t1, traces, radius, stage, out, sems):
    stores = Loads()
    for b in range(*todo):
        parts = advance(middle, slots_of(place, 1, b), t1[b])
        for k in range(2):
            stage[b, k] = parts[k].astype(BF16)
        stores.start(b, stage.at[b], out.at[0, :, place.local(b)], sems.at[b])
        add_traces(place, traces, 6, 1, b, parts, radius)
    return stores


def edge_kernel(width, known, sources, t0, t1, halo, radius, old_traces, old_env, ours, *rest):
    beyond, (out, env, middle, traces, stage, sems) = rest[:2], rest[2:]
    place = Place(sources, width)
    traces[...] = old_traces[...]
    middle[REACH + width :] = jnp.zeros_like(middle[REACH + width :])
    for i in range(HALO):
        take(place, ours, i, HALO, env, REACH + i)
        for j in range(2):
            take(place, beyond[j], i, HALO, env, REACH - 1 - i - HALO * j)
    for i in range(HALO):
        blocks = halo[HALO + i].reshape(t0.shape[1:])
        store_env(middle, REACH - HALO + i, advance(env, slots_of(place, 0, i - HALO), blocks))
    middle_blocks(place, (0, known - HALO), env, middle, t0, traces, radius)
    last = (0, known - 2 * HALO)
    final_blocks(place, last, middle, t1, traces, radius, stage, out, sems).wait(*range(*last))


def next_kernel(width, run, sources, t0, t1, radius, old_traces, buffer, old_env, old_middle, old_out,
                out, env, middle, traces, *rest):
    totals, (stage, sems) = rest[:-2], rest[-2:]
    place = Place(sources, width)
    lo, hi = run
    upto = (width, width) if hi == width else (hi - HALO, hi - 2 * HALO)
    for b in range(lo, hi):
        take(place, buffer, b - lo, hi - lo, env, REACH + b)
    traces[...] = old_traces[...]
    middle_blocks(place, (lo - HALO, upto[0]), env, middle, t0, traces, radius)
    last = (lo - 2 * HALO, upto[1])
    stores = final_blocks(place, last, middle, t1, traces, radius, stage, out, sems)
    for total in totals:
        sums = jnp.sum(traces[...], axis=1, keepdims=True)
        for j in range(2):
            for t in range(2):
                at = 4 * j + 2 * t
                total[j, t : t + 1] = jnp.concatenate([sums[at : at + 1], sums[at + 1 : at + 2]], axis=1)
    stores.wait(*range(*last))


SMEM = pl.BlockSpec(memory_space=pltpu.SMEM)
VMEM = pl.BlockSpec(memory_space=pltpu.VMEM)
HBM = pl.BlockSpec(memory_space=pl.ANY)
PARAMS = pltpu.CompilerParams(vmem_limit_bytes=28 * 2**20)
RUNS = ((2, 6), (0, 2), (6, 10))


def held(array, near):
    return pltpu.with_memory_space_constraint(array, pltpu.VMEM if near else pltpu.HBM)


def call(kernel, name, scalars, arrays, outs, scratch=(), aliases=None):
    return pl.pallas_call(
        kernel,
        out_shape=tuple((pltpu.VMEM if near else pltpu.HBM)(s, d) for s, d, near in outs),
        in_specs=[SMEM] * len(scalars) + [VMEM if near else HBM for _, near in arrays],
        out_specs=tuple(VMEM if near else HBM for _, _, near in outs),
        scratch_shapes=list(scratch),
        compiler_params=PARAMS,
        input_output_aliases={} if aliases is None else aliases,
        name=name,
    )(*[held(a, False) for a in scalars], *[held(a, near) for a, near in arrays])


def shards(tensors, sources, operators, insert_at, schmidt):
    width, size = tensors.shape[2], tensors.shape[-1]
    pairs = lax.axis_size("site")
    ring = [(i, (i + 1) % pairs) for i in range(pairs)]
    swap = [(0, 1), (1, 0)]
    schmidt = jnp.swapaxes(schmidt, 0, 1)

    def message(run):
        return ((run[1] - run[0]) * size + 16, size), BF16, True

    trace_shape = ((8, size), F32, True)
    env_shape = ((width + REACH + HALO, 2 * size, size), BF16, True)
    tensor_shape = ((width, 2, size, size), BF16, True)
    radius_shape = (schmidt.shape, F32, True)
    out_shape = ((1, 2, width, size, size), BF16, False)
    stage = [pltpu.VMEM((width, 2, size, size), BF16), pltpu.SemaphoreType.DMA((width,))]

    def across(array):
        return lax.ppermute(array, "sec", swap)

    sent, edge, env, t0, t1, radius, traces = call(
        functools.partial(first_kernel, width, RUNS[0]),
        "anchor",
        (sources, operators, insert_at),
        ((tensors, False), (schmidt, False)),
        (
            message(RUNS[0]),
            ((2 * HALO, 2 * size, size), BF16, True),
            env_shape,
            tensor_shape,
            tensor_shape,
            radius_shape,
            trace_shape,
        ),
        [pltpu.SemaphoreType.DMA((2, width + 1))],
    )
    halo = across(edge)
    got = [lax.ppermute(sent, "site", ring)]
    env, *sents, traces = call(
        functools.partial(second_kernel, width, RUNS[0], RUNS[1:]),
        "anchor_rest",
        (sources, operators, insert_at),
        ((env, True), (halo, True), (t0, True), (t1, True), (radius, True), (traces, True)),
        (env_shape,) + tuple(message(r) for r in RUNS[1:]) + (trace_shape,),
        aliases={3: 0},
    )
    got += [lax.ppermute(s, "site", ring) for s in sents]
    env, piece = call(
        functools.partial(open_kernel, width, RUNS[0]),
        "first_run",
        (sources,),
        ((got[0], True),),
        (env_shape, message(RUNS[1])),
    )
    ours, env = lax.optimization_barrier((got[1], env))
    final, env, middle, traces = call(
        functools.partial(edge_kernel, width, RUNS[0][1]),
        "edge",
        (sources,),
        tuple((a, True) for a in (t0, t1, halo, radius, traces, env, ours, across(ours), across(piece))),
        (out_shape, env_shape, env_shape, trace_shape),
        stage,
        {6: 1},
    )
    for run, buffer in zip(RUNS[2:], got[2:]):
        outs = (out_shape, env_shape, env_shape, trace_shape)
        if run[1] == width:
            outs += (((2, 2, 2), F32, True),)
        final, env, middle, traces, *totals = call(
            functools.partial(next_kernel, width, run),
            "run_%d" % run[0],
            (sources,),
            tuple((a, True) for a in (t0, t1, radius, traces, buffer, env, middle)) + ((final, False),),
            outs,
            stage,
            {6: 1, 7: 2, 8: 0},
        )
    return final, totals[0] + across(totals[0])


def solution(mesh):
    placed = (
        P(("grp", "site"), None, "sec", None, None),
        P("grp", None, None),
        P(),
        P(("grp", "site"), None),
        P("grp", "sec", None),
    )
    return jax.shard_map(
        shards,
        mesh=mesh,
        in_specs=placed,
        out_specs=(P(("grp", "site"), None, "sec", None, None), P(("grp", "site"), None, None)),
        check_vma=False,
    )
```

time: 348 us -> 51.9 us (0.15)
  the two profiles are of different devices: /device:TPU:17 before, /device:TPU:0 now
where the time goes in v2:
time: 51.9 us; the launch traced here: 51.4 us
  Pallas kernels  22.5 us (43%)
  waiting for transfers between devices  20.2 us (39%)
  starting transfers between devices  7.41 us (14%)
  between operations  0.69 us (1%)
  other arithmetic  0.58 us (1%)
    pallas_call x5, Pallas kernels, call(): pl.pallas_call(kernel, out_shape=tuple(((pltpu.VMEM if near else pltpu.HB...  22.5 us
    ppermute x2, waiting for transfers between devices, shards(): got += [lax.ppermute(s, 'site', ring) for s in sents]  9.11 us
    ppermute x1, waiting for transfers between devices, shards(): got = [lax.ppermute(sent, 'site', ring)]  8.43 us
    ppermute x2, starting transfers between devices, shards(): got += [lax.ppermute(s, 'site', ring) for s in sents]  4.17 us
    ppermute x4, waiting for transfers between devices, across(): return lax.ppermute(array, 'sec', swap)  2.69 us
    ppermute x1, starting transfers between devices, shards(): got = [lax.ppermute(sent, 'site', ring)]  2.58 us
  transfers between devices with their start and end apart: 7, of which 5 were waited for; matrix products, arithmetic and copies ran while one was open for 0% of the time, Pallas kernels for 19%

profile of v2, /device:TPU:0, one launch (start us, length us, event | category | flops | bytes accessed | tf_op | source)
XLA Modules:
  0.0 51.4 jit_solution(15718983094796813523)
XLA Ops:
  0.6 5.8 %anchor.1 = (bf16[1040,256]{1,0:T(8,128)(2,1)S(1)}, bf16[4,512,256]{2,1,0:T(8,128)(2,1)S(1)}, bf16[16,512,256]{2,1,0:T(8,128)(2,1)S(1)}, bf16[10,2,256,256]{3,2,...) custom-call(s32[16,2,20]{2,1,0:T(2,128)} %sources.9, ...), custom_call_target="tpu_custom_call" | custom-call | tf_op jit(solution)/shard_map/anchor/pallas_call | solution.py:311
  6.5 0.5 %collective-permute-start = (bf16[4,512,256]{2,1,0:T(8,128)(2,1)S(1)}, bf16[4,512,256]{2,1,0:T(8,128)(2,1)S(1)}, u32[]{:S(2)}, u32[]{:S(2)}) collective-permute-start(bf16[4,512,256]{2,1,0:T(8,128)(2,1)S(1)} %get-tuple-element.25), channel_id=1, source_target_pairs={{0,1},{1,0},{2,3},{3,2},{4,5},{5,4},{6,7},{7,6},{8,9},{9,8},{10,11... | collective-permute-start | bytes 3145736 | tf_op jit(solution)/shard_map/ppermute | solution.py:341
  7.0 2.6 %collective-permute-start.2 = (bf16[1040,256]{1,0:T(8,128)(2,1)S(1)}, bf16[1040,256]{1,0:T(8,128)(2,1)S(1)}, u32[]{:S(2)}, u32[]{:S(2)}) collective-permute-start(bf16[1040,256]{1,0:T(8,128)(2,1)S(1)} %get-tuple-element.30), channel_id=1, source_target_pairs={{0,2},{2,4},{4,6},{6,8},{8,10},{10,12},{12,14},{14,0},{1,3},{3,5},... | collective-permute-start | bytes 1597448 | tf_op jit(solution)/shard_map/ppermute | solution.py:360
  9.6 0.0 collective-permute-done.halo
  9.6 3.4 %anchor_rest.1 = (bf16[16,512,256]{2,1,0:T(8,128)(2,1)S(1)}, bf16[528,256]{1,0:T(8,128)(2,1)S(1)}, bf16[1040,256]{1,0:T(8,128)(2,1)S(1)}, f32[8,256]{1,0:T(8,128)S(1)}) custom-call(s32[16,2,20]{2,1,0:T(2,128)} %sources.9, f32[2,2]{1,0:T(2,128)} %operators.3, s32[1,2]{1,0:T(1,128)} %insert_at.3, ...), custom_call_target="tpu_custom_call", output_to_operand_aliasing={{0}: (3, {})} | custom-call | tf_op jit(solution)/shard_map/anchor_rest/pallas_call | solution.py:311
  13.0 2.6 %collective-permute-start.1 = (bf16[528,256]{1,0:T(8,128)(2,1)S(1)}, bf16[528,256]{1,0:T(8,128)(2,1)S(1)}, u32[]{:S(2)}, u32[]{:S(2)}) collective-permute-start(bf16[528,256]{1,0:T(8,128)(2,1)S(1)} %get-tuple-element.29), channel_id=1, source_target_pairs={{0,2},{2,4},{4,6},{6,8},{8,10},{10,12},{12,14},{14,0},{1,3},{3,5},... | collective-permute-start | bytes 811016 | tf_op jit(solution)/shard_map/ppermute | solution.py:369
  15.6 1.5 %collective-permute-start.5 = (bf16[1040,256]{1,0:T(8,128)(2,1)S(1)}, bf16[1040,256]{1,0:T(8,128)(2,1)S(1)}, u32[]{:S(2)}, u32[]{:S(2)}) collective-permute-start(bf16[1040,256]{1,0:T(8,128)(2,1)S(1)} %get-tuple-element.36), channel_id=1, source_target_pairs={{0,2},{2,4},{4,6},{6,8},{8,10},{10,12},{12,14},{14,0},{1,3},{3,5},... | collective-permute-start | bytes 1597448 | tf_op jit(solution)/shard_map/ppermute | solution.py:369
  17.1 8.4 %collective-permute-done.2.buffer = bf16[1040,256]{1,0:T(8,128)(2,1)S(1)} collective-permute-done((bf16[1040,256]{1,0:T(8,128)(2,1)S(1)}, bf16[1040,256]{1,0:T(8,128)(2,1)S(1)}, u32[]{:S(2)}, u32[]{:S(2)}) %collective-permute-start.2) | collective-permute-done | bytes 532512 | tf_op jit(solution)/shard_map/ppermute | solution.py:360
  25.6 1.3 %first_run.1 = (bf16[16,512,256]{2,1,0:T(8,128)(2,1)S(1)}, bf16[528,256]{1,0:T(8,128)(2,1)S(1)}) custom-call(s32[16,2,20]{2,1,0:T(2,128)} %sources.9, bf16[1040,256]{1,0:T(8,128)(2,1)S(1)} %collective-permute-done.2.buffer), custom_call_target="tpu_custom_call" | custom-call | tf_op jit(solution)/shard_map/first_run/pallas_call | solution.py:311
  26.8 0.1 collective-permute-start.4
  26.9 4.4 %collective-permute-done.1.ours = bf16[528,256]{1,0:T(8,128)(2,1)S(1)} collective-permute-done((bf16[528,256]{1,0:T(8,128)(2,1)S(1)}, bf16[528,256]{1,0:T(8,128)(2,1)S(1)}, u32[]{:S(2)}, u32[]{:S(2)}) %collective-permute-start.1) | collective-permute-done | bytes 270368 | tf_op jit(solution)/shard_map/ppermute | solution.py:369
  31.4 0.0 collective-permute-start.3
  31.4 0.0 collective-permute-done.4.rest_1_
  31.4 1.5 %collective-permute-done.3.rest_0_ = bf16[528,256]{1,0:T(8,128)(2,1)S(1)} collective-permute-done((bf16[528,256]{1,0:T(8,128)(2,1)S(1)}, bf16[528,256]{1,0:T(8,128)(2,1)S(1)}, u32[]{:S(2)}, u32[]{:S(2)}) %collective-permute-start.3) | collective-permute-done | bytes 270368 | tf_op jit(solution)/shard_map/ppermute | solution.py:341
  32.9 4.9 %edge.1 = (bf16[1,2,10,256,256]{4,3,2,1,0:T(8,128)(2,1)}, bf16[16,512,256]{2,1,0:T(8,128)(2,1)S(1)}, bf16[16,512,256]{2,1,0:T(8,128)(2,1)S(1)}, f32[8,256]{1,0:T(8,128)S(1)}) custom-call(s32[16,2,20]{2,1,0:T(2,128)} %sources.9, bf16[10,2,256,256]{3,2,1,0:T(8,128)(2,1)S(1)} %get-tuple-element.22.t0, ...), custom_call_target="tpu_custom_call", output_to_operand_aliasing={{1}: (6, {})} | custom-call | tf_op jit(solution)/shard_map/edge/pallas_call | solution.py:311
  37.9 4.7 %collective-permute-done.5.buffer = bf16[1040,256]{1,0:T(8,128)(2,1)S(1)} collective-permute-done((bf16[1040,256]{1,0:T(8,128)(2,1)S(1)}, bf16[1040,256]{1,0:T(8,128)(2,1)S(1)}, u32[]{:S(2)}, u32[]{:S(2)}) %collective-permute-start.5) | collective-permute-done | bytes 532512 | tf_op jit(solution)/shard_map/ppermute | solution.py:369
  42.5 7.1 %run_6.1 = (bf16[1,2,10,256,256]{4,3,2,1,0:T(8,128)(2,1)}, bf16[16,512,256]{2,1,0:T(8,128)(2,1)S(1)}, bf16[16,512,256]{2,1,0:T(8,128)(2,1)S(1)}, f32[8,256]{1,0:T(8,128)}, f32[2,2,2]{2,1,0:T(2,128)S(1)}) custom-call(s32[16,2,20]{2,1,0:T(2,128)} %sources.9, ...), custom_call_target="tpu_custom_call", output_to_operand_aliasing={{1}: (6, {}), {2}: (7, {}), {0}: (8, {})} | custom-call | tf_op jit(solution)/shard_map/run_6/pallas_call | solution.py:311
  49.6 0.1 collective-permute-start.6
  49.7 1.1 %collective-permute-done.6 = f32[2,2,2]{2,1,0:T(2,128)S(1)} collective-permute-done((f32[2,2,2]{2,1,0:T(2,128)S(1)}, f32[2,2,2]{2,1,0:T(2,128)S(1)}, u32[]{:S(2)}, u32[]{:S(2)}) %collective-permute-start.6) | collective-permute-done | bytes 64 | tf_op jit(solution)/shard_map/ppermute | solution.py:341
  50.8 0.6 %add.3 = f32[2,2,2]{2,1,0:T(2,128)} add(f32[2,2,2]{2,1,0:T(2,128)S(1)} %get-tuple-element.41, f32[2,2,2]{2,1,0:T(2,128)S(1)} %collective-permute-done.6) | non-fusion elementwise | flops 8 | bytes 96 | tf_op jit(solution)/shard_map/add | solution.py:400
Async XLA Ops:
  6.5 3.1 %collective-permute-start = (bf16[4,512,256]{2,1,0:T(8,128)(2,1)S(1)}, bf16[4,512,256]{2,1,0:T(8,128)(2,1)S(1)}, u32[]{:S(2)}, u32[]{:S(2)}) collective-permute-start(bf16[4,512,256]{2,1,0:T(8,128)(2,1)S(1)} %get-tuple-element.25), channel_id=1, source_target_pairs={{0,1},{1,0},{2,3},{3,2},{4,5},{5,4},{6,7},{7,6},{8,9},{9,8},{10,11... | collective-permute-start | bytes 3145736 | tf_op jit(solution)/shard_map/ppermute | solution.py:341
  7.0 18.6 %collective-permute-start.2 = (bf16[1040,256]{1,0:T(8,128)(2,1)S(1)}, bf16[1040,256]{1,0:T(8,128)(2,1)S(1)}, u32[]{:S(2)}, u32[]{:S(2)}) collective-permute-start(bf16[1040,256]{1,0:T(8,128)(2,1)S(1)} %get-tuple-element.30), channel_id=1, source_target_pairs={{0,2},{2,4},{4,6},{6,8},{8,10},{10,12},{12,14},{14,0},{1,3},{3,5},... | collective-permute-start | bytes 1597448 | tf_op jit(solution)/shard_map/ppermute | solution.py:360
  13.0 18.4 %collective-permute-start.1 = (bf16[528,256]{1,0:T(8,128)(2,1)S(1)}, bf16[528,256]{1,0:T(8,128)(2,1)S(1)}, u32[]{:S(2)}, u32[]{:S(2)}) collective-permute-start(bf16[528,256]{1,0:T(8,128)(2,1)S(1)} %get-tuple-element.29), channel_id=1, source_target_pairs={{0,2},{2,4},{4,6},{6,8},{8,10},{10,12},{12,14},{14,0},{1,3},{3,5},... | collective-permute-start | bytes 811016 | tf_op jit(solution)/shard_map/ppermute | solution.py:369
  15.6 26.9 %collective-permute-start.5 = (bf16[1040,256]{1,0:T(8,128)(2,1)S(1)}, bf16[1040,256]{1,0:T(8,128)(2,1)S(1)}, u32[]{:S(2)}, u32[]{:S(2)}) collective-permute-start(bf16[1040,256]{1,0:T(8,128)(2,1)S(1)} %get-tuple-element.36), channel_id=1, source_target_pairs={{0,2},{2,4},{4,6},{6,8},{8,10},{10,12},{12,14},{14,0},{1,3},{3,5},... | collective-permute-start | bytes 1597448 | tf_op jit(solution)/shard_map/ppermute | solution.py:369
  26.8 4.5 %collective-permute-start.4 = (bf16[528,256]{1,0:T(8,128)(2,1)S(1)}, bf16[528,256]{1,0:T(8,128)(2,1)S(1)}, u32[]{:S(2)}, u32[]{:S(2)}) collective-permute-start(bf16[528,256]{1,0:T(8,128)(2,1)S(1)} %get-tuple-element.34), channel_id=1, source_target_pairs={{0,1},{1,0},{2,3},{3,2},{4,5},{5,4},{6,7},{7,6},{8,9},{9,8},{10,11... | collective-permute-start | bytes 811016 | tf_op jit(solution)/shard_map/ppermute | solution.py:341
  31.4 1.5 %collective-permute-start.3 = (bf16[528,256]{1,0:T(8,128)(2,1)S(1)}, bf16[528,256]{1,0:T(8,128)(2,1)S(1)}, u32[]{:S(2)}, u32[]{:S(2)}) collective-permute-start(bf16[528,256]{1,0:T(8,128)(2,1)S(1)} %collective-permute-done.1.ours), channel_id=1, source_target_pairs={{0,1},{1,0},{2,3},{3,2},{4,5},{5,4},{6,7},{7,6},{8,9},{9,8},{10,11... | collective-permute-start | bytes 811016 | tf_op jit(solution)/shard_map/ppermute | solution.py:341
  49.6 1.2 %collective-permute-start.6 = (f32[2,2,2]{2,1,0:T(2,128)S(1)}, f32[2,2,2]{2,1,0:T(2,128)S(1)}, u32[]{:S(2)}, u32[]{:S(2)}) collective-permute-start(f32[2,2,2]{2,1,0:T(2,128)S(1)} %get-tuple-element.41), channel_id=1, source_target_pairs={{0,1},{1,0},{2,3},{3,2},{4,5},{5,4},{6,7},{7,6},{8,9},{9,8},{10,11... | collective-permute-start | bytes 104 | tf_op jit(solution)/shard_map/ppermute | solution.py:341

commit v3 on v2

--- a/solution.py
+++ b/solution.py
@@ -12,16 +12,11 @@
 REACH = 4
 HALO = 2
 class Place:
-    def __init__(self, sources, width):
+    def __init__(self, width, steps):
         self.core = lax.axis_index("sec")
         self.pair = lax.axis_index("site")
         self.width = width
-        middle = sources.shape[2] // 2
-        sign = 2 * self.core - 1
-        self.steps = []
-        for site in range(2):
-            charge = sources[2 * self.pair + site, 0, middle] - middle + 1
-            self.steps.append([sign * (charge + 2 * state - 1) for state in range(2)])
+        self.steps = steps
 
     def local(self, b):
         return jnp.where(self.core == 0, self.width - 1 - b, b)
@@ -109,16 +104,29 @@
     for insert in range(2):
         total = 0.0
         for state in range(2):
-            inside = b + place.steps[0][state] < place.width
+            inside = b + place.steps[state] < place.width
             total = total + jnp.where(inside, weight[insert][state], 0.0) * terms[state]
         out.append(total)
     return out
 
 
-def chosen_weights(operators, insert_at, which):
-    return [
-        [jnp.where(insert_at[0, k] == which, operators[k, s], 1.0) for s in range(2)] for k in range(2)
-    ]
+def fill_steps(place, sources, steps):
+    middle = sources.shape[2] // 2
+    for site in range(2):
+        charge = sources[2 * place.pair + site, 0, middle] - middle + 1
+        for state in range(2):
+            steps[2 * site + state] = (2 * place.core - 1) * (charge + 2 * state - 1)
+
+
+def fill_weights(operators, insert_at, weights):
+    for which in range(2):
+        for k in range(2):
+            for s in range(2):
+                weights[which, 2 * k + s] = jnp.where(insert_at[0, k] == which, operators[k, s], 1.0)
+
+
+def weights_at(weights, which):
+    return [[weights[which, 2 * k + s] for s in range(2)] for k in range(2)]
 
 
 def add_traces(place, traces, at, site, b, parts, radius):
@@ -128,7 +136,7 @@
 
 
 def slots_of(place, site, b):
-    return [REACH + b + place.steps[site][state] for state in range(2)]
+    return [REACH + b + place.steps[2 * site + state] for state in range(2)]
 
 
 def store_env(env, slot, parts):
@@ -137,17 +145,22 @@
         env[slot, k * size : (k + 1) * size] = parts[k].astype(BF16)
 
 
+def send_one(place, env, t1, weight, traces, radius, sent, lo, b):
+    parts = advance(env, slots_of(place, 1, b), t1[b], weight)
+    size = parts[0].shape[0]
+    sent[(b - lo) * size : (b - lo + 1) * size] = pack(*parts)
+    add_traces(place, traces, 4, 1, b, parts, radius)
+    return diagonal_row(parts[1])
+
+
+def send_rows(sent, rows):
+    count, size = len(rows), rows[0].shape[1]
+    rows = rows + [jnp.zeros((16 - count, size), F32)]
+    sent[count * size : count * size + 16] = jnp.concatenate(rows, axis=0).astype(BF16)
+
+
 def send(place, env, t1, weight, traces, radius, sent, run):
-    rows = []
-    lo, hi = run
-    for b in range(lo, hi):
-        parts = advance(env, slots_of(place, 1, b), t1[b], weight)
-        size = parts[0].shape[0]
-        sent[(b - lo) * size : (b - lo + 1) * size] = pack(*parts)
-        rows.append(diagonal_row(parts[1]))
-        add_traces(place, traces, 4, 1, b, parts, radius)
-    rows.append(jnp.zeros((16 - len(rows), size), F32))
-    sent[(hi - lo) * size : (hi - lo) * size + 16] = jnp.concatenate(rows, axis=0).astype(BF16)
+    send_rows(sent, [send_one(place, env, t1, weight, traces, radius, sent, run[0], b) for b in range(*run)])
 
 
 def take(place, buffer, i, count, env, slot):
@@ -172,72 +185,81 @@
 
 
 def first_kernel(width, run, sources, operators, insert_at, tensors, schmidt,
-                 sent, edge, env, t0, t1, radius, traces, sems):
-    place = Place(sources, width)
+                 sent, edge, env, t0, t1, radius, traces, steps, weights, sources_here, operators_here, inserts_here, sems):
+    place = Place(width, steps)
     lo, hi = run
     loads = Loads()
-    ends = list(range(lo, width)) + list(range(lo))
-    near = [b for b in ends if lo - HALO <= b < hi + HALO]
+    loads.start("sources", sources, sources_here, sems.at[1, 0])
+    loads.start("operators", operators, operators_here, sems.at[1, 1])
+    loads.start("insert_at", insert_at, inserts_here, sems.at[1, width])
+    near = list(range(hi + HALO))
     for b in near:
         loads.start(("t0", b), tensors.at[0, :, place.local(b)], t0.at[b], sems.at[0, b])
     for b in range(lo, hi):
         loads.start(("t1", b), tensors.at[1, :, place.local(b)], t1.at[b], sems.at[1, b])
     loads.start("radius", schmidt, radius, sems.at[0, width])
-    for b in ends:
-        if b not in near:
-            loads.start(("t0", b), tensors.at[0, :, place.local(b)], t0.at[b], sems.at[0, b])
-    for b in ends:
-        if not lo <= b < hi:
-            loads.start(("t1", b), tensors.at[1, :, place.local(b)], t1.at[b], sems.at[1, b])
-    u = chosen_weights(operators, insert_at, 0)
-    v = chosen_weights(operators, insert_at, 1)
     traces[...] = jnp.zeros_like(traces)
     env[REACH + width :] = jnp.zeros_like(env[REACH + width :])
-    for b in near:
-        loads.wait(("t0", b))
-        parts = squares(place, t0[b], u, b)
-        store_env(env, REACH + b, parts)
-        if b < HALO:
-            store_env(edge, HALO - 1 - b, parts)
-            edge[2 * HALO - 1 - b] = t0[b].reshape(edge.shape[1:])
+    loads.wait("sources", "operators", "insert_at")
+    fill_steps(place, sources_here, steps)
+    fill_weights(operators_here, inserts_here, weights)
+    u, v = weights_at(weights, 0), weights_at(weights, 1)
+    for group in [near]:
+        for b in group:
+            loads.wait(("t0", b))
+        for b in group:
+            parts = squares(place, t0[b], u, b)
+            store_env(env, REACH + b, parts)
+            if b < HALO:
+                store_env(edge, HALO - 1 - b, parts)
+                edge[2 * HALO - 1 - b] = t0[b].reshape(edge.shape[1:])
     for b in range(lo, hi):
         loads.wait(("t1", b))
     loads.wait("radius")
     send(place, env, t1, v, traces, radius, sent, run)
-    for b in ends:
-        loads.wait(("t0", b), ("t1", b))
-
-
-def second_kernel(width, first_run, runs, sources, operators, insert_at, old_env, halo, t0, t1, radius, old_traces, *rest):
-    env, sents, traces = rest[0], rest[1:-1], rest[-1]
-    place = Place(sources, width)
+
+
+def second_kernel(width, first_run, runs, steps, weights, tensors, old_env, halo, old_t0, old_t1, radius,
+                  old_traces, *rest):
+    env, t0, t1, sents, (traces, sems) = *rest[:3], rest[3:-2], rest[-2:]
+    place = Place(width, steps)
     size = t0.shape[-1]
-    u = chosen_weights(operators, insert_at, 0)
-    v = chosen_weights(operators, insert_at, 1)
+    lo, hi = first_run
+    late = [b for b in range(width) if not lo - HALO <= b < hi + HALO]
+    order = [b for run in runs for b in range(*run)]
+    loads = Loads()
+    for b in late:
+        loads.start(("t0", b), tensors.at[0, :, place.local(b)], t0.at[b], sems.at[0, b])
+    for b in order:
+        loads.start(("t1", b), tensors.at[1, :, place.local(b)], t1.at[b], sems.at[1, b])
+    u, v = weights_at(weights, 0), weights_at(weights, 1)
     traces[...] = old_traces[...]
     for i in range(HALO):
         env[REACH - HALO + i] = halo[i]
-    lo, hi = first_run
     for b in range(width):
-        if not lo - HALO <= b < hi + HALO:
+        if b in late:
+            loads.wait(("t0", b))
             parts = squares(place, t0[b], u, b)
             store_env(env, REACH + b, parts)
         else:
             parts = [env[REACH + b, k * size : (k + 1) * size] for k in range(2)]
         add_traces(place, traces, 0, 0, b, parts, radius)
+    for b in order:
+        loads.wait(("t1", b))
     for run, sent in zip(runs, sents):
         send(place, env, t1, v, traces, radius, sent, run)
 
 
-def open_kernel(width, run, sources, buffer, env, piece):
-    place = Place(sources, width)
+def open_kernel(width, runs, steps, *rest):
+    buffers, (env, piece) = rest[: len(runs)], rest[len(runs) :]
+    place = Place(width, steps)
     env[REACH + width :] = jnp.zeros_like(env[REACH + width :])
-    lo, hi = run
-    size = buffer.shape[1]
-    for b in range(lo, hi):
-        take(place, buffer, b - lo, hi - lo, env, REACH + b)
-    piece[: HALO * size] = buffer[: HALO * size]
-    piece[HALO * size :] = buffer[(hi - lo) * size :]
+    for (lo, hi), buffer in zip(runs, buffers):
+        for b in range(lo, hi):
+            take(place, buffer, b - lo, hi - lo, env, REACH + b)
+    size = buffers[0].shape[1]
+    piece[: HALO * size] = buffers[0][: HALO * size]
+    piece[HALO * size :] = buffers[0][(runs[0][1] - runs[0][0]) * size :]
 
 
 def middle_blocks(place, todo, env, middle, t0, traces, radius):
@@ -258,9 +280,9 @@
     return stores
 
 
-def edge_kernel(width, known, sources, t0, t1, halo, radius, old_traces, old_env, ours, *rest):
+def edge_kernel(width, known, steps, t0, t1, halo, radius, old_traces, old_env, ours, *rest):
     beyond, (out, env, middle, traces, stage, sems) = rest[:2], rest[2:]
-    place = Place(sources, width)
+    place = Place(width, steps)
     traces[...] = old_traces[...]
     middle[REACH + width :] = jnp.zeros_like(middle[REACH + width :])
     for i in range(HALO):
@@ -275,10 +297,10 @@
     final_blocks(place, last, middle, t1, traces, radius, stage, out, sems).wait(*range(*last))
 
 
-def next_kernel(width, run, sources, t0, t1, radius, old_traces, buffer, old_env, old_middle, old_out,
+def next_kernel(width, run, steps, t0, t1, radius, old_traces, buffer, old_env, old_middle, old_out,
                 out, env, middle, traces, *rest):
     totals, (stage, sems) = rest[:-2], rest[-2:]
-    place = Place(sources, width)
+    place = Place(width, steps)
     lo, hi = run
     upto = (width, width) if hi == width else (hi - HALO, hi - 2 * HALO)
     for b in range(lo, hi):
@@ -300,24 +322,24 @@
 VMEM = pl.BlockSpec(memory_space=pltpu.VMEM)
 HBM = pl.BlockSpec(memory_space=pl.ANY)
 PARAMS = pltpu.CompilerParams(vmem_limit_bytes=28 * 2**20)
-RUNS = ((2, 6), (0, 2), (6, 10))
-
-
-def held(array, near):
-    return pltpu.with_memory_space_constraint(array, pltpu.VMEM if near else pltpu.HBM)
+RUNS = ((2, 5), (5, 7), (0, 2), (7, 10))
+OPENED = 2
 
 
 def call(kernel, name, scalars, arrays, outs, scratch=(), aliases=None):
+    specs = {pltpu.VMEM: VMEM, pltpu.SMEM: SMEM, pltpu.HBM: HBM}
+    where = [pltpu.SMEM] * len(scalars) + [pltpu.VMEM if near else pltpu.HBM for _, near in arrays]
+    values = [*scalars, *[a for a, _ in arrays]]
     return pl.pallas_call(
         kernel,
-        out_shape=tuple((pltpu.VMEM if near else pltpu.HBM)(s, d) for s, d, near in outs),
-        in_specs=[SMEM] * len(scalars) + [VMEM if near else HBM for _, near in arrays],
-        out_specs=tuple(VMEM if near else HBM for _, _, near in outs),
+        out_shape=tuple(memory(s, d) for s, d, memory in outs),
+        in_specs=[specs[w] for w in where],
+        out_specs=tuple(specs[memory] for _, _, memory in outs),
         scratch_shapes=list(scratch),
         compiler_params=PARAMS,
         input_output_aliases={} if aliases is None else aliases,
         name=name,
-    )(*[held(a, False) for a in scalars], *[held(a, near) for a, near in arrays])
+    )(*[pltpu.with_memory_space_constraint(a, w) for a, w in zip(values, where)])
 
 
 def shards(tensors, sources, operators, insert_at, schmidt):
@@ -328,70 +350,73 @@
     schmidt = jnp.swapaxes(schmidt, 0, 1)
 
     def message(run):
-        return ((run[1] - run[0]) * size + 16, size), BF16, True
-
-    trace_shape = ((8, size), F32, True)
-    env_shape = ((width + REACH + HALO, 2 * size, size), BF16, True)
-    tensor_shape = ((width, 2, size, size), BF16, True)
-    radius_shape = (schmidt.shape, F32, True)
-    out_shape = ((1, 2, width, size, size), BF16, False)
+        return ((run[1] - run[0]) * size + 16, size), BF16, pltpu.VMEM
+
+    trace_shape = ((8, size), F32, pltpu.VMEM)
+    env_shape = ((width + REACH + HALO, 2 * size, size), BF16, pltpu.VMEM)
+    tensor_shape = ((width, 2, size, size), BF16, pltpu.VMEM)
+    radius_shape = (schmidt.shape, F32, pltpu.VMEM)
+    out_shape = ((1, 2, width, size, size), BF16, pltpu.HBM)
     stage = [pltpu.VMEM((width, 2, size, size), BF16), pltpu.SemaphoreType.DMA((width,))]
 
     def across(array):
         return lax.ppermute(array, "sec", swap)
 
-    sent, edge, env, t0, t1, radius, traces = call(
+    sent, edge, env, t0, t1, radius, traces, steps, weights = call(
         functools.partial(first_kernel, width, RUNS[0]),
         "anchor",
-        (sources, operators, insert_at),
-        ((tensors, False), (schmidt, False)),
+        (),
+        tuple((a, False) for a in (sources, operators, insert_at, tensors, schmidt)),
         (
             message(RUNS[0]),
-            ((2 * HALO, 2 * size, size), BF16, True),
+            ((2 * HALO, 2 * size, size), BF16, pltpu.VMEM),
             env_shape,
             tensor_shape,
             tensor_shape,
             radius_shape,
             trace_shape,
+            ((4,), jnp.int32, pltpu.SMEM),
+            ((2, 4), F32, pltpu.SMEM),
         ),
-        [pltpu.SemaphoreType.DMA((2, width + 1))],
+        [pltpu.SMEM(a.shape, a.dtype) for a in (sources, operators, insert_at)] + [pltpu.SemaphoreType.DMA((2, width + 1))],
     )
     halo = across(edge)
     got = [lax.ppermute(sent, "site", ring)]
-    env, *sents, traces = call(
+    env, t0, t1, *sents, traces = call(
         functools.partial(second_kernel, width, RUNS[0], RUNS[1:]),
         "anchor_rest",
-        (sources, operators, insert_at),
-        ((env, True), (halo, True), (t0, True), (t1, True), (radius, True), (traces, True)),
-        (env_shape,) + tuple(message(r) for r in RUNS[1:]) + (trace_shape,),
-        aliases={3: 0},
+        (steps, weights),
+        ((tensors, False),) + tuple((a, True) for a in (env, halo, t0, t1, radius, traces)),
+        (env_shape, tensor_shape, tensor_shape) + tuple(message(r) for r in RUNS[1:]) + (trace_shape,),
+        [pltpu.SemaphoreType.DMA((2, width))],
+        {3: 0, 5: 1, 6: 2},
     )
     got += [lax.ppermute(s, "site", ring) for s in sents]
     env, piece = call(
-        functools.partial(open_kernel, width, RUNS[0]),
-        "first_run",
-        (sources,),
-        ((got[0], True),),
-        (env_shape, message(RUNS[1])),
-    )
-    ours, env = lax.optimization_barrier((got[1], env))
+        functools.partial(open_kernel, width, RUNS[:OPENED]),
+        "first_runs",
+        (steps,),
+        tuple((a, True) for a in got[:OPENED]),
+        (env_shape, message(RUNS[OPENED])),
+    )
+    ours, env = lax.optimization_barrier((got[OPENED], env))
     final, env, middle, traces = call(
-        functools.partial(edge_kernel, width, RUNS[0][1]),
+        functools.partial(edge_kernel, width, RUNS[OPENED - 1][1]),
         "edge",
-        (sources,),
+        (steps,),
         tuple((a, True) for a in (t0, t1, halo, radius, traces, env, ours, across(ours), across(piece))),
         (out_shape, env_shape, env_shape, trace_shape),
         stage,
         {6: 1},
     )
-    for run, buffer in zip(RUNS[2:], got[2:]):
+    for run, buffer in zip(RUNS[OPENED + 1 :], got[OPENED + 1 :]):
         outs = (out_shape, env_shape, env_shape, trace_shape)
         if run[1] == width:
-            outs += (((2, 2, 2), F32, True),)
+            outs += (((2, 2, 2), F32, pltpu.VMEM),)
         final, env, middle, traces, *totals = call(
             functools.partial(next_kernel, width, run),
             "run_%d" % run[0],
-            (sources,),
+            (steps,),
             tuple((a, True) for a in (t0, t1, radius, traces, buffer, env, middle)) + ((final, False),),
             outs,
             stage,

time: 51.9 us -> 48 us (0.925)
  Pallas kernels: 22.5 us -> 18.4 us
  starting transfers between devices: 7.41 us -> 9.36 us
  waiting for transfers between devices: 20.2 us -> 18.7 us
    ppermute x1, waiting for transfers between devices: 8.43 us -> 3.11 us  [shards(): got = [lax.ppermute(sent, 'site', ring)]]
    pallas_call x5, Pallas kernels: 22.5 us -> 18.4 us  [call(): pl.pallas_call(kernel, out_shape=tuple((memory(s, d) for s, d, memory in...]
    ppermute x2 -> x3, waiting for transfers between devices: 9.11 us -> 13.1 us  [shards(): got += [lax.ppermute(s, 'site', ring) for s in sents]]
    ppermute x2 -> x3, starting transfers between devices: 4.17 us -> 5.68 us  [shards(): got += [lax.ppermute(s, 'site', ring) for s in sents]]
  transfers between devices with their start and end apart: 7 -> 8, of which waited for: 5 -> 7; matrix products, arithmetic and copies ran while one was open for 0% -> 0% of each run, Pallas kernels for 19% -> 20%
where the time goes in v3:
time: 48 us; the launch traced here: 47.7 us
  waiting for transfers between devices  18.7 us (39%)
  Pallas kernels  18.4 us (38%)
  starting transfers between devices  9.36 us (20%)
  between operations  0.69 us (1%)
  other arithmetic  0.58 us (1%)
    pallas_call x5, Pallas kernels, call(): pl.pallas_call(kernel, out_shape=tuple((memory(s, d) for s, d, memory in...  18.4 us
    ppermute x3, waiting for transfers between devices, shards(): got += [lax.ppermute(s, 'site', ring) for s in sents]  13.1 us
    ppermute x3, starting transfers between devices, shards(): got += [lax.ppermute(s, 'site', ring) for s in sents]  5.68 us
    ppermute x1, waiting for transfers between devices, shards(): got = [lax.ppermute(sent, 'site', ring)]  3.11 us
    ppermute x1, starting transfers between devices, shards(): got = [lax.ppermute(sent, 'site', ring)]  2.58 us
    ppermute x4, waiting for transfers between devices, across(): return lax.ppermute(array, 'sec', swap)  2.57 us
    ppermute x4, starting transfers between devices, across(): return lax.ppermute(array, 'sec', swap)  1.1 us
  transfers between devices with their start and end apart: 8, of which 7 were waited for; matrix products, arithmetic and copies ran while one was open for 0% of the time, Pallas kernels for 20%

profile of v3, /device:TPU:0, one launch (start us, length us, event | category | flops | bytes accessed | tf_op | source)
XLA Modules:
  0.0 47.7 jit_solution(6967263515633337788)
XLA Ops:
  0.6 3.6 %anchor.1 = (bf16[784,256]{1,0:T(8,128)(2,1)S(1)}, bf16[4,512,256]{2,1,0:T(8,128)(2,1)S(1)}, bf16[16,512,256]{2,1,0:T(8,128)(2,1)S(1)}, bf16[10,2,256,256]{3,2,1...) custom-call(s32[16,2,20]{2,1,0:T(2,128)} %sources.1, ...), custom_call_target="tpu_custom_call" | custom-call | tf_op jit(solution)/shard_map/anchor/pallas_call | solution.py:333
  4.2 0.5 %collective-permute-start = (bf16[4,512,256]{2,1,0:T(8,128)(2,1)S(1)}, bf16[4,512,256]{2,1,0:T(8,128)(2,1)S(1)}, u32[]{:S(2)}, u32[]{:S(2)}) collective-permute-start(bf16[4,512,256]{2,1,0:T(8,128)(2,1)S(1)} %get-tuple-element.30), channel_id=1, source_target_pairs={{0,1},{1,0},{2,3},{3,2},{4,5},{5,4},{6,7},{7,6},{8,9},{9,8},{10,11... | collective-permute-start | bytes 3145736 | tf_op jit(solution)/shard_map/ppermute | solution.py:363
  4.7 2.6 %collective-permute-start.2 = (bf16[784,256]{1,0:T(8,128)(2,1)S(1)}, bf16[784,256]{1,0:T(8,128)(2,1)S(1)}, u32[]{:S(2)}, u32[]{:S(2)}) collective-permute-start(bf16[784,256]{1,0:T(8,128)(2,1)S(1)} %get-tuple-element.39), channel_id=1, source_target_pairs={{0,2},{2,4},{4,6},{6,8},{8,10},{10,12},{12,14},{14,0},{1,3},{3,5},... | collective-permute-start | bytes 1204232 | tf_op jit(solution)/shard_map/ppermute | solution.py:384
  7.3 0.0 collective-permute-done.halo
  7.3 4.4 %anchor_rest.1 = (bf16[16,512,256]{2,1,0:T(8,128)(2,1)S(1)}, bf16[10,2,256,256]{3,2,1,0:T(8,128)(2,1)S(1)}, bf16[10,2,256,256]{3,2,1,0:T(8,128)(2,1)S(1)}, bf16[...) custom-call(s32[4]{0:T(128)S(4)} %get-tuple-element.27.steps, ...), custom_call_target="tpu_custom_call", output_to_operand_aliasing={{0}: (3, {}), {1}: (5, {}), {2}: (6, {})} | custom-call | tf_op jit(solution)/shard_map/anchor_rest/pallas_call | solution.py:333
  11.7 2.6 %collective-permute-start.3 = (bf16[528,256]{1,0:T(8,128)(2,1)S(1)}, bf16[528,256]{1,0:T(8,128)(2,1)S(1)}, u32[]{:S(2)}, u32[]{:S(2)}) collective-permute-start(bf16[528,256]{1,0:T(8,128)(2,1)S(1)} %get-tuple-element.40), channel_id=1, source_target_pairs={{0,2},{2,4},{4,6},{6,8},{8,10},{10,12},{12,14},{14,0},{1,3},{3,5},... | collective-permute-start | bytes 811016 | tf_op jit(solution)/shard_map/ppermute | solution.py:394
  14.3 1.5 %collective-permute-start.1 = (bf16[528,256]{1,0:T(8,128)(2,1)S(1)}, bf16[528,256]{1,0:T(8,128)(2,1)S(1)}, u32[]{:S(2)}, u32[]{:S(2)}) collective-permute-start(bf16[528,256]{1,0:T(8,128)(2,1)S(1)} %get-tuple-element.38), channel_id=1, source_target_pairs={{0,2},{2,4},{4,6},{6,8},{8,10},{10,12},{12,14},{14,0},{1,3},{3,5},... | collective-permute-start | bytes 811016 | tf_op jit(solution)/shard_map/ppermute | solution.py:394
  15.8 1.5 %collective-permute-start.6 = (bf16[784,256]{1,0:T(8,128)(2,1)S(1)}, bf16[784,256]{1,0:T(8,128)(2,1)S(1)}, u32[]{:S(2)}, u32[]{:S(2)}) collective-permute-start(bf16[784,256]{1,0:T(8,128)(2,1)S(1)} %get-tuple-element.46), channel_id=1, source_target_pairs={{0,2},{2,4},{4,6},{6,8},{8,10},{10,12},{12,14},{14,0},{1,3},{3,5},... | collective-permute-start | bytes 1204232 | tf_op jit(solution)/shard_map/ppermute | solution.py:394
  17.4 3.1 %collective-permute-done.2.rest_0_ = bf16[784,256]{1,0:T(8,128)(2,1)S(1)} collective-permute-done((bf16[784,256]{1,0:T(8,128)(2,1)S(1)}, bf16[784,256]{1,0:T(8,128)(2,1)S(1)}, u32[]{:S(2)}, u32[]{:S(2)}) %collective-permute-start.2) | collective-permute-done | bytes 401440 | tf_op jit(solution)/shard_map/ppermute | solution.py:384
  20.5 5.8 %collective-permute-done.3.rest_1_ = bf16[528,256]{1,0:T(8,128)(2,1)S(1)} collective-permute-done((bf16[528,256]{1,0:T(8,128)(2,1)S(1)}, bf16[528,256]{1,0:T(8,128)(2,1)S(1)}, u32[]{:S(2)}, u32[]{:S(2)}) %collective-permute-start.3) | collective-permute-done | bytes 270368 | tf_op jit(solution)/shard_map/ppermute | solution.py:394
  26.3 0.4 first_runs.1
  26.7 5.4 %collective-permute-done.1.ours = bf16[528,256]{1,0:T(8,128)(2,1)S(1)} collective-permute-done((bf16[528,256]{1,0:T(8,128)(2,1)S(1)}, bf16[528,256]{1,0:T(8,128)(2,1)S(1)}, u32[]{:S(2)}, u32[]{:S(2)}) %collective-permute-start.1) | collective-permute-done | bytes 270368 | tf_op jit(solution)/shard_map/ppermute | solution.py:394
  32.1 0.0 collective-permute-start.4
  32.1 0.5 %collective-permute-start.5 = (bf16[528,256]{1,0:T(8,128)(2,1)S(1)}, bf16[528,256]{1,0:T(8,128)(2,1)S(1)}, u32[]{:S(2)}, u32[]{:S(2)}) collective-permute-start(bf16[528,256]{1,0:T(8,128)(2,1)S(1)} %get-tuple-element.44), channel_id=1, source_target_pairs={{0,1},{1,0},{2,3},{3,2},{4,5},{5,4},{6,7},{7,6},{8,9},{9,8},{10,11... | collective-permute-start | bytes 811016 | tf_op jit(solution)/shard_map/ppermute | solution.py:363
  32.6 1.0 %collective-permute-done.4.rest_0_ = bf16[528,256]{1,0:T(8,128)(2,1)S(1)} collective-permute-done((bf16[528,256]{1,0:T(8,128)(2,1)S(1)}, bf16[528,256]{1,0:T(8,128)(2,1)S(1)}, u32[]{:S(2)}, u32[]{:S(2)}) %collective-permute-start.4) | collective-permute-done | bytes 270368 | tf_op jit(solution)/shard_map/ppermute | solution.py:363
  33.6 0.4 collective-permute-done.5.rest_1_
  34.0 4.6 %edge.1 = (bf16[1,2,10,256,256]{4,3,2,1,0:T(8,128)(2,1)}, bf16[16,512,256]{2,1,0:T(8,128)(2,1)S(1)}, bf16[16,512,256]{2,1,0:T(8,128)(2,1)S(1)}, f32[8,256]{1,0:T(8,128)S(1)}) custom-call(s32[4]{0:T(128)S(4)} %get-tuple-element.27.steps, bf16[10,2,256,256]{3,2,1,0:T(8,128)(2,1)S(1)} %get-tuple-element.35.t0, ...), custom_call_target="tpu_custom_call", output_to_operand_aliasing={{1}: (6, {})} | custom-call | tf_op jit(solution)/shard_map/edge/pallas_call | solution.py:333
  38.6 1.9 %collective-permute-done.6.buffer = bf16[784,256]{1,0:T(8,128)(2,1)S(1)} collective-permute-done((bf16[784,256]{1,0:T(8,128)(2,1)S(1)}, bf16[784,256]{1,0:T(8,128)(2,1)S(1)}, u32[]{:S(2)}, u32[]{:S(2)}) %collective-permute-start.6) | collective-permute-done | bytes 401440 | tf_op jit(solution)/shard_map/ppermute | solution.py:394
  40.4 5.5 %run_7.1 = (bf16[1,2,10,256,256]{4,3,2,1,0:T(8,128)(2,1)}, bf16[16,512,256]{2,1,0:T(8,128)(2,1)S(1)}, bf16[16,512,256]{2,1,0:T(8,128)(2,1)S(1)}, f32[8,256]{1,0:T(8,128)}, f32[2,2,2]{2,1,0:T(2,128)S(1)}) custom-call(s32[4]{0:T(128)S(4)} %get-tuple-element.27.steps, ...), custom_call_target="tpu_custom_call", output_to_operand_aliasing={{1}: (6, {}), {2}: (7, {}), {0}: (8, {})} | custom-call | tf_op jit(solution)/shard_map/run_7/pallas_call | solution.py:333
  45.9 0.1 collective-permute-start.7
  46.0 1.1 %collective-permute-done.7 = f32[2,2,2]{2,1,0:T(2,128)S(1)} collective-permute-done((f32[2,2,2]{2,1,0:T(2,128)S(1)}, f32[2,2,2]{2,1,0:T(2,128)S(1)}, u32[]{:S(2)}, u32[]{:S(2)}) %collective-permute-start.7) | collective-permute-done | bytes 64 | tf_op jit(solution)/shard_map/ppermute | solution.py:363
  47.1 0.6 %add.3 = f32[2,2,2]{2,1,0:T(2,128)} add(f32[2,2,2]{2,1,0:T(2,128)S(1)} %get-tuple-element.51, f32[2,2,2]{2,1,0:T(2,128)S(1)} %collective-permute-done.7) | non-fusion elementwise | flops 8 | bytes 96 | tf_op jit(solution)/shard_map/add | solution.py:425
Async XLA Ops:
  4.2 3.1 %collective-permute-start = (bf16[4,512,256]{2,1,0:T(8,128)(2,1)S(1)}, bf16[4,512,256]{2,1,0:T(8,128)(2,1)S(1)}, u32[]{:S(2)}, u32[]{:S(2)}) collective-permute-start(bf16[4,512,256]{2,1,0:T(8,128)(2,1)S(1)} %get-tuple-element.30), channel_id=1, source_target_pairs={{0,1},{1,0},{2,3},{3,2},{4,5},{5,4},{6,7},{7,6},{8,9},{9,8},{10,11... | collective-permute-start | bytes 3145736 | tf_op jit(solution)/shard_map/ppermute | solution.py:363
  4.7 15.8 %collective-permute-start.2 = (bf16[784,256]{1,0:T(8,128)(2,1)S(1)}, bf16[784,256]{1,0:T(8,128)(2,1)S(1)}, u32[]{:S(2)}, u32[]{:S(2)}) collective-permute-start(bf16[784,256]{1,0:T(8,128)(2,1)S(1)} %get-tuple-element.39), channel_id=1, source_target_pairs={{0,2},{2,4},{4,6},{6,8},{8,10},{10,12},{12,14},{14,0},{1,3},{3,5},... | collective-permute-start | bytes 1204232 | tf_op jit(solution)/shard_map/ppermute | solution.py:384
  11.7 14.6 %collective-permute-start.3 = (bf16[528,256]{1,0:T(8,128)(2,1)S(1)}, bf16[528,256]{1,0:T(8,128)(2,1)S(1)}, u32[]{:S(2)}, u32[]{:S(2)}) collective-permute-start(bf16[528,256]{1,0:T(8,128)(2,1)S(1)} %get-tuple-element.40), channel_id=1, source_target_pairs={{0,2},{2,4},{4,6},{6,8},{8,10},{10,12},{12,14},{14,0},{1,3},{3,5},... | collective-permute-start | bytes 811016 | tf_op jit(solution)/shard_map/ppermute | solution.py:394
  14.3 17.7 %collective-permute-start.1 = (bf16[528,256]{1,0:T(8,128)(2,1)S(1)}, bf16[528,256]{1,0:T(8,128)(2,1)S(1)}, u32[]{:S(2)}, u32[]{:S(2)}) collective-permute-start(bf16[528,256]{1,0:T(8,128)(2,1)S(1)} %get-tuple-element.38), channel_id=1, source_target_pairs={{0,2},{2,4},{4,6},{6,8},{8,10},{10,12},{12,14},{14,0},{1,3},{3,5},... | collective-permute-start | bytes 811016 | tf_op jit(solution)/shard_map/ppermute | solution.py:394
  15.8 24.6 %collective-permute-start.6 = (bf16[784,256]{1,0:T(8,128)(2,1)S(1)}, bf16[784,256]{1,0:T(8,128)(2,1)S(1)}, u32[]{:S(2)}, u32[]{:S(2)}) collective-permute-start(bf16[784,256]{1,0:T(8,128)(2,1)S(1)} %get-tuple-element.46), channel_id=1, source_target_pairs={{0,2},{2,4},{4,6},{6,8},{8,10},{10,12},{12,14},{14,0},{1,3},{3,5},... | collective-permute-start | bytes 1204232 | tf_op jit(solution)/shard_map/ppermute | solution.py:394
  32.1 1.5 %collective-permute-start.4 = (bf16[528,256]{1,0:T(8,128)(2,1)S(1)}, bf16[528,256]{1,0:T(8,128)(2,1)S(1)}, u32[]{:S(2)}, u32[]{:S(2)}) collective-permute-start(bf16[528,256]{1,0:T(8,128)(2,1)S(1)} %collective-permute-done.1.ours), channel_id=1, source_target_pairs={{0,1},{1,0},{2,3},{3,2},{4,5},{5,4},{6,7},{7,6},{8,9},{9,8},{10,11... | collective-permute-start | bytes 811016 | tf_op jit(solution)/shard_map/ppermute | solution.py:363
  32.1 1.9 %collective-permute-start.5 = (bf16[528,256]{1,0:T(8,128)(2,1)S(1)}, bf16[528,256]{1,0:T(8,128)(2,1)S(1)}, u32[]{:S(2)}, u32[]{:S(2)}) collective-permute-start(bf16[528,256]{1,0:T(8,128)(2,1)S(1)} %get-tuple-element.44), channel_id=1, source_target_pairs={{0,1},{1,0},{2,3},{3,2},{4,5},{5,4},{6,7},{7,6},{8,9},{9,8},{10,11... | collective-permute-start | bytes 811016 | tf_op jit(solution)/shard_map/ppermute | solution.py:363
  45.9 1.2 %collective-permute-start.7 = (f32[2,2,2]{2,1,0:T(2,128)S(1)}, f32[2,2,2]{2,1,0:T(2,128)S(1)}, u32[]{:S(2)}, u32[]{:S(2)}) collective-permute-start(f32[2,2,2]{2,1,0:T(2,128)S(1)} %get-tuple-element.51), channel_id=1, source_target_pairs={{0,1},{1,0},{2,3},{3,2},{4,5},{5,4},{6,7},{7,6},{8,9},{9,8},{10,11... | collective-permute-start | bytes 104 | tf_op jit(solution)/shard_map/ppermute | solution.py:363

commit v4 on v3

--- a/solution.py
+++ b/solution.py
@@ -391,7 +391,7 @@
         [pltpu.SemaphoreType.DMA((2, width))],
         {3: 0, 5: 1, 6: 2},
     )
-    got += [lax.ppermute(s, "site", ring) for s in sents]
+    got += [lax.ppermute(s, "site", ring[:-1]) for s in sents]
     env, piece = call(
         functools.partial(open_kernel, width, RUNS[:OPENED]),
         "first_runs",

time: 48 us -> 45 us (0.938)
  the two profiles are of different devices: /device:TPU:0 before, /device:TPU:17 now
where the time goes in v4:
time: 45 us; the launch traced here: 44.7 us
  Pallas kernels  18.4 us (41%)
  starting transfers between devices  14.8 us (33%)
  waiting for transfers between devices  10.2 us (23%)
  between operations  0.71 us (2%)
  other arithmetic  0.58 us (1%)
    pallas_call x5, Pallas kernels, call(): pl.pallas_call(kernel, out_shape=tuple((memory(s, d) for s, d, memory in...  18.4 us
    ppermute x3, starting transfers between devices, shards(): got += [lax.ppermute(s, 'site', ring[:-1]) for s in sents]  9.62 us
    ppermute x3, waiting for transfers between devices, shards(): got += [lax.ppermute(s, 'site', ring[:-1]) for s in sents]  6.81 us
    ppermute x4, starting transfers between devices, across(): return lax.ppermute(array, 'sec', swap)  3.89 us
    ppermute x4, waiting for transfers between devices, across(): return lax.ppermute(array, 'sec', swap)  3.42 us
    ppermute x1, starting transfers between devices, shards(): got = [lax.ppermute(sent, 'site', ring)]  1.24 us
  transfers between devices with their start and end apart: 8, of which 7 were waited for; matrix products, arithmetic and copies ran while one was open for 0% of the time, Pallas kernels for 21%

profile of v4, /device:TPU:17, one launch (start us, length us, event | category | flops | bytes accessed | tf_op | source)
XLA Modules:
  0.0 44.7 jit_solution(5298460635389728338)
XLA Ops:
  0.6 3.6 %anchor.1 = (bf16[784,256]{1,0:T(8,128)(2,1)S(1)}, bf16[4,512,256]{2,1,0:T(8,128)(2,1)S(1)}, bf16[16,512,256]{2,1,0:T(8,128)(2,1)S(1)}, bf16[10,2,256,256]{3,2,1...) custom-call(s32[16,2,20]{2,1,0:T(2,128)} %sources.1, ...), custom_call_target="tpu_custom_call" | custom-call | tf_op jit(solution)/shard_map/anchor/pallas_call | solution.py:333
  4.2 0.7 %collective-permute-start = (bf16[4,512,256]{2,1,0:T(8,128)(2,1)S(1)}, bf16[4,512,256]{2,1,0:T(8,128)(2,1)S(1)}, u32[]{:S(2)}, u32[]{:S(2)}) collective-permute-start(bf16[4,512,256]{2,1,0:T(8,128)(2,1)S(1)} %get-tuple-element.30), channel_id=1, source_target_pairs={{0,1},{1,0},{2,3},{3,2},{4,5},{5,4},{6,7},{7,6},{8,9},{9,8},{10,11... | collective-permute-start | bytes 3145736 | tf_op jit(solution)/shard_map/ppermute | solution.py:363
  4.9 1.2 %collective-permute-start.2 = (bf16[784,256]{1,0:T(8,128)(2,1)S(1)}, bf16[784,256]{1,0:T(8,128)(2,1)S(1)}, u32[]{:S(2)}, u32[]{:S(2)}) collective-permute-start(bf16[784,256]{1,0:T(8,128)(2,1)S(1)} %get-tuple-element.39), channel_id=1, source_target_pairs={{0,2},{2,4},{4,6},{6,8},{8,10},{10,12},{12,14},{14,0},{1,3},{3,5},... | collective-permute-start | bytes 1204232 | tf_op jit(solution)/shard_map/ppermute | solution.py:384
  6.2 1.0 %collective-permute-done.halo = bf16[4,512,256]{2,1,0:T(8,128)(2,1)S(1)} collective-permute-done((bf16[4,512,256]{2,1,0:T(8,128)(2,1)S(1)}, bf16[4,512,256]{2,1,0:T(8,128)(2,1)S(1)}, u32[]{:S(2)}, u32[]{:S(2)}) %collective-permute-start) | collective-permute-done | bytes 1048608 | tf_op jit(solution)/shard_map/ppermute | solution.py:363
  7.2 4.4 %anchor_rest.1 = (bf16[16,512,256]{2,1,0:T(8,128)(2,1)S(1)}, bf16[10,2,256,256]{3,2,1,0:T(8,128)(2,1)S(1)}, bf16[10,2,256,256]{3,2,1,0:T(8,128)(2,1)S(1)}, bf16[...) custom-call(s32[4]{0:T(128)S(4)} %get-tuple-element.27.steps, ...), custom_call_target="tpu_custom_call", output_to_operand_aliasing={{0}: (3, {}), {1}: (5, {}), {2}: (6, {})} | custom-call | tf_op jit(solution)/shard_map/anchor_rest/pallas_call | solution.py:333
  11.6 3.1 %collective-permute-start.3 = (bf16[528,256]{1,0:T(8,128)(2,1)S(1)}, bf16[528,256]{1,0:T(8,128)(2,1)S(1)}, u32[]{:S(2)}, u32[]{:S(2)}) collective-permute-start(bf16[528,256]{1,0:T(8,128)(2,1)S(1)} %get-tuple-element.40), channel_id=1, source_target_pairs={{0,2},{2,4},{4,6},{6,8},{8,10},{10,12},{12,14},{1,3},{3,5},{5,7},{... | collective-permute-start | bytes 811016 | tf_op jit(solution)/shard_map/ppermute | solution.py:394
  14.8 3.2 %collective-permute-start.1 = (bf16[528,256]{1,0:T(8,128)(2,1)S(1)}, bf16[528,256]{1,0:T(8,128)(2,1)S(1)}, u32[]{:S(2)}, u32[]{:S(2)}) collective-permute-start(bf16[528,256]{1,0:T(8,128)(2,1)S(1)} %get-tuple-element.38), channel_id=1, source_target_pairs={{0,2},{2,4},{4,6},{6,8},{8,10},{10,12},{12,14},{1,3},{3,5},{5,7},{... | collective-permute-start | bytes 811016 | tf_op jit(solution)/shard_map/ppermute | solution.py:394
  17.9 3.3 %collective-permute-start.6 = (bf16[784,256]{1,0:T(8,128)(2,1)S(1)}, bf16[784,256]{1,0:T(8,128)(2,1)S(1)}, u32[]{:S(2)}, u32[]{:S(2)}) collective-permute-start(bf16[784,256]{1,0:T(8,128)(2,1)S(1)} %get-tuple-element.46), channel_id=1, source_target_pairs={{0,2},{2,4},{4,6},{6,8},{8,10},{10,12},{12,14},{1,3},{3,5},{5,7},{... | collective-permute-start | bytes 1204232 | tf_op jit(solution)/shard_map/ppermute | solution.py:394
  21.3 0.0 collective-permute-done.2.rest_0_
  21.3 0.9 %collective-permute-done.3.rest_1_ = bf16[528,256]{1,0:T(8,128)(2,1)S(1)} collective-permute-done((bf16[528,256]{1,0:T(8,128)(2,1)S(1)}, bf16[528,256]{1,0:T(8,128)(2,1)S(1)}, u32[]{:S(2)}, u32[]{:S(2)}) %collective-permute-start.3) | collective-permute-done | bytes 270368 | tf_op jit(solution)/shard_map/ppermute | solution.py:394
  22.2 0.4 first_runs.1
  22.6 5.4 %collective-permute-done.1.ours = bf16[528,256]{1,0:T(8,128)(2,1)S(1)} collective-permute-done((bf16[528,256]{1,0:T(8,128)(2,1)S(1)}, bf16[528,256]{1,0:T(8,128)(2,1)S(1)}, u32[]{:S(2)}, u32[]{:S(2)}) %collective-permute-start.1) | collective-permute-done | bytes 270368 | tf_op jit(solution)/shard_map/ppermute | solution.py:394
  28.0 1.9 %collective-permute-start.4 = (bf16[528,256]{1,0:T(8,128)(2,1)S(1)}, bf16[528,256]{1,0:T(8,128)(2,1)S(1)}, u32[]{:S(2)}, u32[]{:S(2)}) collective-permute-start(bf16[528,256]{1,0:T(8,128)(2,1)S(1)} %collective-permute-done.1.ours), channel_id=1, source_target_pairs={{0,1},{1,0},{2,3},{3,2},{4,5},{5,4},{6,7},{7,6},{8,9},{9,8},{10,11... | collective-permute-start | bytes 811016 | tf_op jit(solution)/shard_map/ppermute | solution.py:363
  29.9 0.0 collective-permute-start.5
  29.9 1.2 %collective-permute-done.4.rest_0_ = bf16[528,256]{1,0:T(8,128)(2,1)S(1)} collective-permute-done((bf16[528,256]{1,0:T(8,128)(2,1)S(1)}, bf16[528,256]{1,0:T(8,128)(2,1)S(1)}, u32[]{:S(2)}, u32[]{:S(2)}) %collective-permute-start.4) | collective-permute-done | bytes 270368 | tf_op jit(solution)/shard_map/ppermute | solution.py:363
  31.1 0.4 collective-permute-done.5.rest_1_
  31.5 4.6 %edge.1 = (bf16[1,2,10,256,256]{4,3,2,1,0:T(8,128)(2,1)}, bf16[16,512,256]{2,1,0:T(8,128)(2,1)S(1)}, bf16[16,512,256]{2,1,0:T(8,128)(2,1)S(1)}, f32[8,256]{1,0:T(8,128)S(1)}) custom-call(s32[4]{0:T(128)S(4)} %get-tuple-element.27.steps, bf16[10,2,256,256]{3,2,1,0:T(8,128)(2,1)S(1)} %get-tuple-element.35.t0, ...), custom_call_target="tpu_custom_call", output_to_operand_aliasing={{1}: (6, {})} | custom-call | tf_op jit(solution)/shard_map/edge/pallas_call | solution.py:333
  36.0 0.5 %collective-permute-done.6.buffer = bf16[784,256]{1,0:T(8,128)(2,1)S(1)} collective-permute-done((bf16[784,256]{1,0:T(8,128)(2,1)S(1)}, bf16[784,256]{1,0:T(8,128)(2,1)S(1)}, u32[]{:S(2)}, u32[]{:S(2)}) %collective-permute-start.6) | collective-permute-done | bytes 401440 | tf_op jit(solution)/shard_map/ppermute | solution.py:394
  36.6 5.5 %run_7.1 = (bf16[1,2,10,256,256]{4,3,2,1,0:T(8,128)(2,1)}, bf16[16,512,256]{2,1,0:T(8,128)(2,1)S(1)}, bf16[16,512,256]{2,1,0:T(8,128)(2,1)S(1)}, f32[8,256]{1,0:T(8,128)}, f32[2,2,2]{2,1,0:T(2,128)S(1)}) custom-call(s32[4]{0:T(128)S(4)} %get-tuple-element.27.steps, ...), custom_call_target="tpu_custom_call", output_to_operand_aliasing={{1}: (6, {}), {2}: (7, {}), {0}: (8, {})} | custom-call | tf_op jit(solution)/shard_map/run_7/pallas_call | solution.py:333
  42.1 1.2 %collective-permute-start.7 = (f32[2,2,2]{2,1,0:T(2,128)S(1)}, f32[2,2,2]{2,1,0:T(2,128)S(1)}, u32[]{:S(2)}, u32[]{:S(2)}) collective-permute-start(f32[2,2,2]{2,1,0:T(2,128)S(1)} %get-tuple-element.51), channel_id=1, source_target_pairs={{0,1},{1,0},{2,3},{3,2},{4,5},{5,4},{6,7},{7,6},{8,9},{9,8},{10,11... | collective-permute-start | bytes 104 | tf_op jit(solution)/shard_map/ppermute | solution.py:363
  43.3 0.8 %collective-permute-done.7 = f32[2,2,2]{2,1,0:T(2,128)S(1)} collective-permute-done((f32[2,2,2]{2,1,0:T(2,128)S(1)}, f32[2,2,2]{2,1,0:T(2,128)S(1)}, u32[]{:S(2)}, u32[]{:S(2)}) %collective-permute-start.7) | collective-permute-done | bytes 64 | tf_op jit(solution)/shard_map/ppermute | solution.py:363
  44.1 0.6 %add.3 = f32[2,2,2]{2,1,0:T(2,128)} add(f32[2,2,2]{2,1,0:T(2,128)S(1)} %get-tuple-element.51, f32[2,2,2]{2,1,0:T(2,128)S(1)} %collective-permute-done.7) | non-fusion elementwise | flops 8 | bytes 96 | tf_op jit(solution)/shard_map/add | solution.py:425
Async XLA Ops:
  4.2 3.0 %collective-permute-start = (bf16[4,512,256]{2,1,0:T(8,128)(2,1)S(1)}, bf16[4,512,256]{2,1,0:T(8,128)(2,1)S(1)}, u32[]{:S(2)}, u32[]{:S(2)}) collective-permute-start(bf16[4,512,256]{2,1,0:T(8,128)(2,1)S(1)} %get-tuple-element.30), channel_id=1, source_target_pairs={{0,1},{1,0},{2,3},{3,2},{4,5},{5,4},{6,7},{7,6},{8,9},{9,8},{10,11... | collective-permute-start | bytes 3145736 | tf_op jit(solution)/shard_map/ppermute | solution.py:363
  4.9 16.3 %collective-permute-start.2 = (bf16[784,256]{1,0:T(8,128)(2,1)S(1)}, bf16[784,256]{1,0:T(8,128)(2,1)S(1)}, u32[]{:S(2)}, u32[]{:S(2)}) collective-permute-start(bf16[784,256]{1,0:T(8,128)(2,1)S(1)} %get-tuple-element.39), channel_id=1, source_target_pairs={{0,2},{2,4},{4,6},{6,8},{8,10},{10,12},{12,14},{14,0},{1,3},{3,5},... | collective-permute-start | bytes 1204232 | tf_op jit(solution)/shard_map/ppermute | solution.py:384
  11.6 10.6 %collective-permute-start.3 = (bf16[528,256]{1,0:T(8,128)(2,1)S(1)}, bf16[528,256]{1,0:T(8,128)(2,1)S(1)}, u32[]{:S(2)}, u32[]{:S(2)}) collective-permute-start(bf16[528,256]{1,0:T(8,128)(2,1)S(1)} %get-tuple-element.40), channel_id=1, source_target_pairs={{0,2},{2,4},{4,6},{6,8},{8,10},{10,12},{12,14},{1,3},{3,5},{5,7},{... | collective-permute-start | bytes 811016 | tf_op jit(solution)/shard_map/ppermute | solution.py:394
  14.8 13.2 %collective-permute-start.1 = (bf16[528,256]{1,0:T(8,128)(2,1)S(1)}, bf16[528,256]{1,0:T(8,128)(2,1)S(1)}, u32[]{:S(2)}, u32[]{:S(2)}) collective-permute-start(bf16[528,256]{1,0:T(8,128)(2,1)S(1)} %get-tuple-element.38), channel_id=1, source_target_pairs={{0,2},{2,4},{4,6},{6,8},{8,10},{10,12},{12,14},{1,3},{3,5},{5,7},{... | collective-permute-start | bytes 811016 | tf_op jit(solution)/shard_map/ppermute | solution.py:394
  17.9 18.6 %collective-permute-start.6 = (bf16[784,256]{1,0:T(8,128)(2,1)S(1)}, bf16[784,256]{1,0:T(8,128)(2,1)S(1)}, u32[]{:S(2)}, u32[]{:S(2)}) collective-permute-start(bf16[784,256]{1,0:T(8,128)(2,1)S(1)} %get-tuple-element.46), channel_id=1, source_target_pairs={{0,2},{2,4},{4,6},{6,8},{8,10},{10,12},{12,14},{1,3},{3,5},{5,7},{... | collective-permute-start | bytes 1204232 | tf_op jit(solution)/shard_map/ppermute | solution.py:394
  28.0 3.1 %collective-permute-start.4 = (bf16[528,256]{1,0:T(8,128)(2,1)S(1)}, bf16[528,256]{1,0:T(8,128)(2,1)S(1)}, u32[]{:S(2)}, u32[]{:S(2)}) collective-permute-start(bf16[528,256]{1,0:T(8,128)(2,1)S(1)} %collective-permute-done.1.ours), channel_id=1, source_target_pairs={{0,1},{1,0},{2,3},{3,2},{4,5},{5,4},{6,7},{7,6},{8,9},{9,8},{10,11... | collective-permute-start | bytes 811016 | tf_op jit(solution)/shard_map/ppermute | solution.py:363
  29.9 1.6 %collective-permute-start.5 = (bf16[528,256]{1,0:T(8,128)(2,1)S(1)}, bf16[528,256]{1,0:T(8,128)(2,1)S(1)}, u32[]{:S(2)}, u32[]{:S(2)}) collective-permute-start(bf16[528,256]{1,0:T(8,128)(2,1)S(1)} %get-tuple-element.44), channel_id=1, source_target_pairs={{0,1},{1,0},{2,3},{3,2},{4,5},{5,4},{6,7},{7,6},{8,9},{9,8},{10,11... | collective-permute-start | bytes 811016 | tf_op jit(solution)/shard_map/ppermute | solution.py:363
  42.1 2.0 %collective-permute-start.7 = (f32[2,2,2]{2,1,0:T(2,128)S(1)}, f32[2,2,2]{2,1,0:T(2,128)S(1)}, u32[]{:S(2)}, u32[]{:S(2)}) collective-permute-start(f32[2,2,2]{2,1,0:T(2,128)S(1)} %get-tuple-element.51), channel_id=1, source_target_pairs={{0,1},{1,0},{2,3},{3,2},{4,5},{5,4},{6,7},{7,6},{8,9},{9,8},{10,11... | collective-permute-start | bytes 104 | tf_op jit(solution)/shard_map/ppermute | solution.py:363

commit v5 on v4

v5 whole, which is shorter than its diff:
```python
import functools

import jax
import jax.numpy as jnp
from jax import lax
from jax.experimental import pallas as pl
from jax.experimental.pallas import tpu as pltpu
from jax.sharding import PartitionSpec as P

F32 = jnp.float32
BF16 = jnp.bfloat16
REACH = 4
HALO = 2
EXTRA = 16
class Place:
    def __init__(self, width, steps):
        self.core = lax.axis_index("sec")
        self.pair = lax.axis_index("site")
        self.width = width
        self.steps = steps

    def local(self, b):
        return jnp.where(self.core == 0, self.width - 1 - b, b)


def dot(a, b):
    return jnp.dot(a, b, preferred_element_type=F32)


def dot_t(a, b):
    return lax.dot_general(a, b, (((0,), (0,)), ((), ())), preferred_element_type=F32)


def diagonal_row(block):
    half = block.shape[0] // 2
    row = lax.broadcasted_iota(jnp.int32, (half, half), 0)
    col = lax.broadcasted_iota(jnp.int32, (half, half), 1)
    parts = [
        jnp.sum(jnp.where(row == col, block[at : at + half, at : at + half], 0.0), axis=0, keepdims=True)
        for at in (0, half)
    ]
    return jnp.concatenate(parts, axis=1)


def pack(first, second):
    half = first.shape[0] // 2
    row = lax.broadcasted_iota(jnp.int32, (half, half), 0)
    col = lax.broadcasted_iota(jnp.int32, (half, half), 1)
    upper = row <= col

    def mixed(at):
        cut = slice(at, at + half)
        return jnp.where(upper, first[cut, cut], second[cut, cut])

    top = jnp.concatenate([mixed(0), first[:half, half:]], axis=1)
    bottom = jnp.concatenate([second[half:, :half], mixed(half)], axis=1)
    return jnp.concatenate([top, bottom], axis=0).astype(BF16)


def unpack(packed, diagonal, valid):
    half = packed.shape[0] // 2
    packed = jnp.where(valid, packed, jnp.zeros_like(packed))
    diagonal = jnp.where(valid, diagonal.astype(F32), 0.0)
    turned = packed.T
    row = lax.broadcasted_iota(jnp.int32, (half, half), 0)
    col = lax.broadcasted_iota(jnp.int32, (half, half), 1)

    def corners(at):
        cut = slice(at, at + half)
        straight, mirrored = packed[cut, cut].astype(F32), turned[cut, cut].astype(F32)
        low = jnp.where(row <= col, straight, mirrored)
        high = jnp.where(row == col, diagonal[:, cut], jnp.where(row < col, mirrored, straight))
        return low.astype(BF16), high.astype(BF16)

    def whole(north, ne, sw, south):
        top = jnp.concatenate([north, ne], axis=1)
        bottom = jnp.concatenate([sw, south], axis=1)
        return jnp.concatenate([top, bottom], axis=0)

    north, south = corners(0), corners(half)
    first = whole(north[0], packed[:half, half:], turned[half:, :half], south[0])
    second = whole(north[1], turned[:half, half:], packed[half:, :half], south[1])
    return first, second


def advance(env, slots, blocks, weight=None):
    size = blocks[0].shape[-1]
    middles = []
    for state in range(2):
        turned = blocks[state].T
        halves = []
        for insert in range(2):
            part = dot(turned, env[slots[state], insert * size : (insert + 1) * size])
            if weight is not None:
                part = part * weight[insert][state]
            halves.append(part.astype(BF16))
        middles.append(jnp.concatenate(halves, axis=0))
    both = dot(jnp.concatenate(middles, axis=1), jnp.concatenate(blocks, axis=0))
    return both[:size], both[size:]


def one_state(place, env, site, state, tensors, b):
    size = env.shape[-1]
    block = tensors[state, place.local(b)]
    slot = REACH + b + place.steps[2 * site + state]
    turned = block.T
    halves = [dot(turned, env[slot, k * size : (k + 1) * size]).astype(BF16) for k in range(2)]
    return dot(jnp.concatenate(halves, axis=0), block)


def begin(place, todo, env, site, tensors, partial):
    for i, b in enumerate(range(*todo)):
        partial[i] = one_state(place, env, site, 1 - place.core, tensors, b)


def complete(place, i, b, env, site, tensors, partial):
    both = partial[i] + one_state(place, env, site, place.core, tensors, b)
    size = env.shape[-1]
    return both[:size], both[size:]


def squares(place, blocks, weight, b):
    terms = [dot(blocks[state].T, blocks[state]) for state in range(2)]
    out = []
    for insert in range(2):
        total = 0.0
        for state in range(2):
            inside = b + place.steps[state] < place.width
            total = total + jnp.where(inside, weight[insert][state], 0.0) * terms[state]
        out.append(total)
    return out


def fill_steps(place, sources, steps):
    middle = sources.shape[2] // 2
    for site in range(2):
        charge = sources[2 * place.pair + site, 0, middle] - middle + 1
        for state in range(2):
            steps[2 * site + state] = (2 * place.core - 1) * (charge + 2 * state - 1)


def fill_weights(operators, insert_at, weights):
    for which in range(2):
        for k in range(2):
            for s in range(2):
                weights[which, 2 * k + s] = jnp.where(insert_at[0, k] == which, operators[k, s], 1.0)


def weights_at(weights, which):
    return [[weights[which, 2 * k + s] for s in range(2)] for k in range(2)]


def add_traces(place, traces, at, site, b, parts, radius):
    row = radius[place.local(b), pl.ds(2 * place.pair + site, 1)]
    for k in range(2):
        traces[at + k : at + k + 1] += diagonal_row(parts[k].astype(BF16).astype(F32)) * (row * row)


def slots_of(place, site, b):
    return [REACH + b + place.steps[2 * site + state] for state in range(2)]


def store_env(env, slot, parts):
    size = parts[0].shape[0]
    for k in range(2):
        env[slot, k * size : (k + 1) * size] = parts[k].astype(BF16)


def blocks_of(place, tensors, b):
    return [tensors[state, place.local(b)] for state in range(2)]


def send(place, env, t1, weight, traces, radius, sent, run):
    rows = []
    for b in range(*run):
        parts = advance(env, slots_of(place, 1, b), blocks_of(place, t1, b), weight)
        size = parts[0].shape[0]
        sent[(b - run[0]) * size : (b - run[0] + 1) * size] = pack(*parts)
        add_traces(place, traces, 4, 1, b, parts, radius)
        rows.append(diagonal_row(parts[1]))
    return rows


def send_rows(sent, rows):
    rows = jnp.concatenate(rows, axis=0)
    rows = jnp.concatenate([rows, jnp.zeros((EXTRA - rows.shape[0], rows.shape[1]), F32)], axis=0)
    sent[sent.shape[0] - EXTRA :] = rows.astype(BF16)


def below(buffer):
    return buffer[buffer.shape[0] - EXTRA :]


def take(place, buffer, i, diagonals, row, env, slot):
    size = buffer.shape[1]
    store_env(env, slot, unpack(buffer[i * size : (i + 1) * size], diagonals[row : row + 1], place.pair > 0))


class Loads:
    def __init__(self):
        self.waiting = {}

    def start(self, key, source, target, sem):
        copy = pltpu.make_async_copy(source, target, sem)
        copy.start()
        self.waiting[key] = copy

    def tensors(self, place, source, target, site, lo, hi, sem):
        at = pl.ds(jnp.where(place.core == 0, place.width - hi, lo), hi - lo)
        self.start((site, lo), source.at[site, :, at], target.at[:, at], sem)

    def wait(self, *keys):
        for key in keys:
            if key in self.waiting:
                self.waiting.pop(key).wait()


def first_kernel(width, run, sources, operators, insert_at, tensors, schmidt,
                 sent, edge, env, t0, t1, radius, traces, steps, weights, sources_here, operators_here, inserts_here, sems):
    place = Place(width, steps)
    lo, hi = run
    loads = Loads()
    loads.start("sources", sources, sources_here, sems.at[0])
    loads.start("operators", operators, operators_here, sems.at[1])
    loads.start("insert_at", insert_at, inserts_here, sems.at[2])
    near = hi + HALO
    loads.tensors(place, tensors, t0, 0, 0, near, sems.at[3])
    loads.tensors(place, tensors, t1, 1, lo, hi, sems.at[4])
    loads.start("radius", schmidt, radius, sems.at[5])
    traces[...] = jnp.zeros_like(traces)
    env[REACH + width :] = jnp.zeros_like(env[REACH + width :])
    loads.wait("sources", "operators", "insert_at")
    fill_steps(place, sources_here, steps)
    fill_weights(operators_here, inserts_here, weights)
    u, v = weights_at(weights, 0), weights_at(weights, 1)
    loads.wait((0, 0))
    for b in range(near):
        blocks = blocks_of(place, t0, b)
        parts = squares(place, blocks, u, b)
        store_env(env, REACH + b, parts)
        if b < HALO:
            store_env(edge, HALO - 1 - b, parts)
            edge[2 * HALO - 1 - b] = jnp.concatenate(blocks, axis=0)
    loads.wait((1, lo), "radius")
    send_rows(sent, send(place, env, t1, v, traces, radius, sent, run))


def second_kernel(width, first_run, runs, steps, weights, tensors, old_env, halo, old_t0, old_t1, radius,
                  old_traces, *rest):
    env, t0, t1, sents, (traces, sems) = *rest[:3], rest[3:-2], rest[-2:]
    place = Place(width, steps)
    size = t0.shape[-1]
    lo, hi = first_run
    known = hi + HALO
    loads = Loads()
    loads.tensors(place, tensors, t0, 0, known, width, sems.at[0])
    loads.tensors(place, tensors, t1, 1, hi, width, sems.at[1])
    loads.tensors(place, tensors, t1, 1, 0, lo, sems.at[2])
    u, v = weights_at(weights, 0), weights_at(weights, 1)
    traces[...] = old_traces[...]
    for i in range(HALO):
        env[REACH - HALO + i] = halo[i]
    for b in range(known):
        parts = [env[REACH + b, k * size : (k + 1) * size] for k in range(2)]
        add_traces(place, traces, 0, 0, b, parts, radius)
    loads.wait((0, known))
    for b in range(known, width):
        parts = squares(place, blocks_of(place, t0, b), u, b)
        store_env(env, REACH + b, parts)
        add_traces(place, traces, 0, 0, b, parts, radius)
    loads.wait((1, hi), (1, 0))
    rows = []
    for run, sent in zip(runs, sents):
        rows += send(place, env, t1, v, traces, radius, sent, run)
    send_rows(sents[0], rows)


def middle_blocks(place, todo, env, middle, t0, traces, radius, partial=None):
    for i, b in enumerate(range(*todo)):
        if partial is not None and i < HALO:
            parts = complete(place, i, b, env, 0, t0, partial)
        else:
            parts = advance(env, slots_of(place, 0, b), blocks_of(place, t0, b))
        store_env(middle, REACH + b, parts)
        add_traces(place, traces, 2, 0, b, parts, radius)


def open_kernel(width, run, steps, first, env, middle, piece):
    place = Place(width, steps)
    size = first.shape[1]
    for array in (env, middle):
        array[REACH + width :] = jnp.zeros_like(array[REACH + width :])
    lo, hi = run
    for b in range(lo, hi):
        take(place, first, b - lo, below(first), b - lo, env, REACH + b)
    piece[: HALO * size] = first[: HALO * size]
    piece[HALO * size :] = below(first)


def final_blocks(place, todo, middle, t1, traces, radius, stage, out, sems, partial=None):
    stores = Loads()
    for i, b in enumerate(range(*todo)):
        if partial is not None and i < HALO:
            parts = complete(place, i, b, middle, 1, t1, partial)
        else:
            parts = advance(middle, slots_of(place, 1, b), blocks_of(place, t1, b))
        for k in range(2):
            stage[b, k] = parts[k].astype(BF16)
        stores.start(b, stage.at[b], out.at[0, :, place.local(b)], sems.at[b])
        add_traces(place, traces, 6, 1, b, parts, radius)
    return stores


def edge_kernel(width, known, steps, t0, t1, halo, radius, old_traces, old_env, old_middle, ours, near, far,
                out, env, middle, traces, partial0, partial1, stage, sems):
    place = Place(width, steps)
    size = t0.shape[-1]
    traces[...] = old_traces[...]
    for i in range(HALO):
        take(place, ours, i, below(ours), i, env, REACH + i)
        take(place, near, i, below(near), i, env, REACH - 1 - i)
        take(place, far, i, below(far), i, env, REACH - 1 - HALO - i)
    for i in range(HALO):
        blocks = [halo[HALO + i, state * size : (state + 1) * size] for state in range(2)]
        store_env(middle, REACH - HALO + i, advance(env, slots_of(place, 0, i - HALO), blocks))
    middle_blocks(place, (0, known - HALO), env, middle, t0, traces, radius)
    last = (0, known - 2 * HALO)
    stores = final_blocks(place, last, middle, t1, traces, radius, stage, out, sems)
    begin(place, (known - HALO, known), env, 0, t0, partial0)
    begin(place, (last[1], last[1] + HALO), middle, 1, t1, partial1)
    stores.wait(*range(*last))


def next_kernel(width, run, row, steps, t0, t1, radius, old_traces, ours, buffer, old_partial0, old_partial1, old_env, old_middle,
                old_out, out, env, middle, traces, *rest):
    results, (stage, sems) = rest[:-2], rest[-2:]
    place = Place(width, steps)
    lo, hi = run
    for b in range(lo, hi):
        take(place, buffer, b - lo, below(ours), row + b - lo, env, REACH + b)
    traces[...] = old_traces[...]
    ends = hi == width
    upto = width if ends else hi - HALO
    middle_blocks(place, (lo - HALO, upto), env, middle, t0, traces, radius, old_partial0)
    last = (lo - 2 * HALO, width if ends else upto - HALO)
    stores = final_blocks(place, last, middle, t1, traces, radius, stage, out, sems, old_partial1)
    if ends:
        (totals,) = results
        sums = jnp.sum(traces[...], axis=1, keepdims=True)
        for j in range(2):
            for t in range(2):
                at = 4 * j + 2 * t
                totals[j, t : t + 1] = jnp.concatenate([sums[at : at + 1], sums[at + 1 : at + 2]], axis=1)
    else:
        begin(place, (upto, hi), env, 0, t0, results[0])
        begin(place, (last[1], upto), middle, 1, t1, results[1])
    stores.wait(*range(*last))


SMEM = pl.BlockSpec(memory_space=pltpu.SMEM)
VMEM = pl.BlockSpec(memory_space=pltpu.VMEM)
HBM = pl.BlockSpec(memory_space=pl.ANY)
PARAMS = pltpu.CompilerParams(vmem_limit_bytes=28 * 2**20)
RUNS = ((2, 5), (0, 2), (5, 8), (8, 10))


def call(kernel, name, scalars, arrays, outs, scratch=(), aliases=None):
    specs = {pltpu.VMEM: VMEM, pltpu.SMEM: SMEM, pltpu.HBM: HBM}
    where = [pltpu.SMEM] * len(scalars) + [pltpu.VMEM if near else pltpu.HBM for _, near in arrays]
    values = [*scalars, *[a for a, _ in arrays]]
    return pl.pallas_call(
        kernel,
        out_shape=tuple(memory(s, d) for s, d, memory in outs),
        in_specs=[specs[w] for w in where],
        out_specs=tuple(specs[memory] for _, _, memory in outs),
        scratch_shapes=list(scratch),
        compiler_params=PARAMS,
        input_output_aliases={} if aliases is None else aliases,
        name=name,
    )(*[pltpu.with_memory_space_constraint(a, w) for a, w in zip(values, where)])


def shards(tensors, sources, operators, insert_at, schmidt):
    width, size = tensors.shape[2], tensors.shape[-1]
    pairs = lax.axis_size("site")
    ring = [(i, (i + 1) % pairs) for i in range(pairs)]
    swap = [(0, 1), (1, 0)]
    schmidt = jnp.swapaxes(schmidt, 0, 1)

    def message(run, extra=EXTRA):
        return ((run[1] - run[0]) * size + extra, size), BF16, pltpu.VMEM

    trace_shape = ((8, size), F32, pltpu.VMEM)
    env_shape = ((width + REACH + HALO, 2 * size, size), BF16, pltpu.VMEM)
    tensor_shape = ((2, width, size, size), BF16, pltpu.VMEM)
    partial_shape = ((HALO, 2 * size, size), F32, pltpu.VMEM)
    radius_shape = (schmidt.shape, F32, pltpu.VMEM)
    out_shape = ((1, 2, width, size, size), BF16, pltpu.HBM)
    stage = [pltpu.VMEM((width, 2, size, size), BF16), pltpu.SemaphoreType.DMA((width,))]

    def across(array):
        return lax.ppermute(array, "sec", swap)

    sent, edge, env, t0, t1, radius, traces, steps, weights = call(
        functools.partial(first_kernel, width, RUNS[0]),
        "anchor",
        (),
        tuple((a, False) for a in (sources, operators, insert_at, tensors, schmidt)),
        (
            message(RUNS[0]),
            ((2 * HALO, 2 * size, size), BF16, pltpu.VMEM),
            env_shape,
            tensor_shape,
            tensor_shape,
            radius_shape,
            trace_shape,
            ((4,), jnp.int32, pltpu.SMEM),
            ((2, 4), F32, pltpu.SMEM),
        ),
        [pltpu.SMEM(a.shape, a.dtype) for a in (sources, operators, insert_at)] + [pltpu.SemaphoreType.DMA((6,))],
    )
    halo = across(edge)
    got = [lax.ppermute(sent, "site", ring)]
    env, t0, t1, *sents, traces = call(
        functools.partial(second_kernel, width, RUNS[0], RUNS[1:]),
        "anchor_rest",
        (steps, weights),
        ((tensors, False),) + tuple((a, True) for a in (env, halo, t0, t1, radius, traces)),
        (env_shape, tensor_shape, tensor_shape) + (message(RUNS[1]), message(RUNS[2], 0), message(RUNS[3], 0)) + (trace_shape,),
        [pltpu.SemaphoreType.DMA((3,))],
        {3: 0, 5: 1, 6: 2},
    )
    got += [lax.ppermute(s, "site", ring[:-1]) for s in sents]
    env, middle, piece = call(
        functools.partial(open_kernel, width, RUNS[0]),
        "first_run",
        (steps,),
        ((got[0], True),),
        (env_shape, env_shape, message(RUNS[1])),
    )
    ours, env = lax.optimization_barrier((got[1], env))
    final, env, middle, traces, *partials = call(
        functools.partial(edge_kernel, width, RUNS[0][1]),
        "edge",
        (steps,),
        tuple((a, True) for a in (t0, t1, halo, radius, traces, env, middle, ours, across(ours), across(piece))),
        (out_shape, env_shape, env_shape, trace_shape, partial_shape, partial_shape),
        stage,
        {6: 1, 7: 2},
    )
    row = RUNS[1][1] - RUNS[1][0]
    for run, buffer in zip(RUNS[2:], got[2:]):
        results = (partial_shape, partial_shape) if run[1] < width else (((2, 2, 2), F32, pltpu.VMEM),)
        final, env, middle, traces, *partials = call(
            functools.partial(next_kernel, width, run, row),
            "run_%d" % run[0],
            (steps,),
            tuple((a, True) for a in (t0, t1, radius, traces, ours, buffer, *partials, env, middle)) + ((final, False),),
            (out_shape, env_shape, env_shape, trace_shape) + results,
            stage,
            {9: 1, 10: 2, 11: 0},
        )
        row += run[1] - run[0]
    (totals,) = partials
    return final, totals + across(totals)


def solution(mesh):
    placed = (
        P(("grp", "site"), None, "sec", None, None),
        P("grp", None, None),
        P(),
        P(("grp", "site"), None),
        P("grp", "sec", None),
    )
    return jax.shard_map(
        shards,
        mesh=mesh,
        in_specs=placed,
        out_specs=(P(("grp", "site"), None, "sec", None, None), P(("grp", "site"), None, None)),
        check_vma=False,
    )
```

time: 45 us -> 43.8 us (0.973)
  starting transfers between devices: 14.8 us -> 13.7 us
  waiting for transfers between devices: 10.2 us -> 9.39 us
  Pallas kernels: 18.4 us -> 19.1 us
    ppermute x4, waiting for transfers between devices: 3.42 us -> 1.87 us  [across(): return lax.ppermute(array, 'sec', swap)]
    ppermute x3, starting transfers between devices: 9.62 us -> 8.71 us  [shards(): got += [lax.ppermute(s, 'site', ring[:-1]) for s in sents]]
    ppermute x3, waiting for transfers between devices: 6.81 us -> 7.52 us  [shards(): got += [lax.ppermute(s, 'site', ring[:-1]) for s in sents]]
    pallas_call x5 -> x6, Pallas kernels: 18.4 us -> 19.1 us  [call(): pl.pallas_call(kernel, out_shape=tuple((memory(s, d) for s, d, memory in...]
  transfers between devices with their start and end apart: 8 -> 8, of which waited for: 7 -> 5; matrix products, arithmetic and copies ran while one was open for 0% -> 0% of each run, Pallas kernels for 21% -> 25%
where the time goes in v5:
time: 43.8 us; the launch traced here: 43.5 us
  Pallas kernels  19.1 us (44%)
  starting transfers between devices  13.7 us (31%)
  waiting for transfers between devices  9.39 us (21%)
  between operations  0.73 us (2%)
  other arithmetic  0.58 us (1%)
    pallas_call x6, Pallas kernels, call(): pl.pallas_call(kernel, out_shape=tuple((memory(s, d) for s, d, memory in...  19.1 us
    ppermute x3, starting transfers between devices, shards(): got += [lax.ppermute(s, 'site', ring[:-1]) for s in sents]  8.71 us
    ppermute x3, waiting for transfers between devices, shards(): got += [lax.ppermute(s, 'site', ring[:-1]) for s in sents]  7.52 us
    ppermute x4, starting transfers between devices, across(): return lax.ppermute(array, 'sec', swap)  3.76 us
    ppermute x4, waiting for transfers between devices, across(): return lax.ppermute(array, 'sec', swap)  1.87 us
    ppermute x1, starting transfers between devices, shards(): got = [lax.ppermute(sent, 'site', ring)]  1.24 us
  transfers between devices with their start and end apart: 8, of which 5 were waited for; matrix products, arithmetic and copies ran while one was open for 0% of the time, Pallas kernels for 25%

profile of v5, /device:TPU:17, one launch (start us, length us, event | category | flops | bytes accessed | tf_op | source)
XLA Modules:
  0.0 43.5 jit_solution(11907486134296206855)
XLA Ops:
  0.6 3.5 %anchor.1 = (bf16[784,256]{1,0:T(8,128)(2,1)S(1)}, bf16[4,512,256]{2,1,0:T(8,128)(2,1)S(1)}, bf16[16,512,256]{2,1,0:T(8,128)(2,1)S(1)}, bf16[2,10,256,256]{3,2,1...) custom-call(s32[16,2,20]{2,1,0:T(2,128)} %sources.1, ...), custom_call_target="tpu_custom_call" | custom-call | tf_op jit(solution)/shard_map/anchor/pallas_call | solution.py:371
  4.1 0.7 %collective-permute-start = (bf16[4,512,256]{2,1,0:T(8,128)(2,1)S(1)}, bf16[4,512,256]{2,1,0:T(8,128)(2,1)S(1)}, u32[]{:S(2)}, u32[]{:S(2)}) collective-permute-start(bf16[4,512,256]{2,1,0:T(8,128)(2,1)S(1)} %get-tuple-element.39), channel_id=1, source_target_pairs={{0,1},{1,0},{2,3},{3,2},{4,5},{5,4},{6,7},{7,6},{8,9},{9,8},{10,11... | collective-permute-start | bytes 3145736 | tf_op jit(solution)/shard_map/ppermute | solution.py:402
  4.9 1.2 %collective-permute-start.2 = (bf16[784,256]{1,0:T(8,128)(2,1)S(1)}, bf16[784,256]{1,0:T(8,128)(2,1)S(1)}, u32[]{:S(2)}, u32[]{:S(2)}) collective-permute-start(bf16[784,256]{1,0:T(8,128)(2,1)S(1)} %get-tuple-element.48), channel_id=1, source_target_pairs={{0,2},{2,4},{4,6},{6,8},{8,10},{10,12},{12,14},{14,0},{1,3},{3,5},... | collective-permute-start | bytes 1204232 | tf_op jit(solution)/shard_map/ppermute | solution.py:423
  6.1 1.0 %collective-permute-done.halo = bf16[4,512,256]{2,1,0:T(8,128)(2,1)S(1)} collective-permute-done((bf16[4,512,256]{2,1,0:T(8,128)(2,1)S(1)}, bf16[4,512,256]{2,1,0:T(8,128)(2,1)S(1)}, u32[]{:S(2)}, u32[]{:S(2)}) %collective-permute-start) | collective-permute-done | bytes 1048608 | tf_op jit(solution)/shard_map/ppermute | solution.py:402
  7.2 4.0 %anchor_rest.1 = (bf16[16,512,256]{2,1,0:T(8,128)(2,1)S(1)}, bf16[2,10,256,256]{3,2,1,0:T(8,128)(2,1)S(1)}, bf16[2,10,256,256]{3,2,1,0:T(8,128)(2,1)S(1)}, bf16[...) custom-call(s32[4]{0:T(128)S(4)} %get-tuple-element.36.steps, ...), custom_call_target="tpu_custom_call", output_to_operand_aliasing={{0}: (3, {}), {1}: (5, {}), {2}: (6, {})} | custom-call | tf_op jit(solution)/shard_map/anchor_rest/pallas_call | solution.py:371
  11.2 3.1 %collective-permute-start.1 = (bf16[528,256]{1,0:T(8,128)(2,1)S(1)}, bf16[528,256]{1,0:T(8,128)(2,1)S(1)}, u32[]{:S(2)}, u32[]{:S(2)}) collective-permute-start(bf16[528,256]{1,0:T(8,128)(2,1)S(1)} %get-tuple-element.47), channel_id=1, source_target_pairs={{0,2},{2,4},{4,6},{6,8},{8,10},{10,12},{12,14},{1,3},{3,5},{5,7},{... | collective-permute-start | bytes 811016 | tf_op jit(solution)/shard_map/ppermute | solution.py:433
  14.3 3.1 %collective-permute-start.5 = (bf16[768,256]{1,0:T(8,128)(2,1)S(1)}, bf16[768,256]{1,0:T(8,128)(2,1)S(1)}, u32[]{:S(2)}, u32[]{:S(2)}) collective-permute-start(bf16[768,256]{1,0:T(8,128)(2,1)S(1)} %get-tuple-element.55), channel_id=1, source_target_pairs={{0,2},{2,4},{4,6},{6,8},{8,10},{10,12},{12,14},{1,3},{3,5},{5,7},{... | collective-permute-start | bytes 1179656 | tf_op jit(solution)/shard_map/ppermute | solution.py:433
  17.5 0.0 collective-permute-done.2.first
  17.5 0.3 first_run.1
  17.8 1.0 %collective-permute-start.4 = (bf16[528,256]{1,0:T(8,128)(2,1)S(1)}, bf16[528,256]{1,0:T(8,128)(2,1)S(1)}, u32[]{:S(2)}, u32[]{:S(2)}) collective-permute-start(bf16[528,256]{1,0:T(8,128)(2,1)S(1)} %get-tuple-element.53), channel_id=1, source_target_pairs={{0,1},{1,0},{2,3},{3,2},{4,5},{5,4},{6,7},{7,6},{8,9},{9,8},{10,11... | collective-permute-start | bytes 811016 | tf_op jit(solution)/shard_map/ppermute | solution.py:402
  18.8 3.7 %collective-permute-done.1.ours = bf16[528,256]{1,0:T(8,128)(2,1)S(1)} collective-permute-done((bf16[528,256]{1,0:T(8,128)(2,1)S(1)}, bf16[528,256]{1,0:T(8,128)(2,1)S(1)}, u32[]{:S(2)}, u32[]{:S(2)}) %collective-permute-start.1) | collective-permute-done | bytes 270368 | tf_op jit(solution)/shard_map/ppermute | solution.py:433
  22.5 1.2 %collective-permute-start.3 = (bf16[528,256]{1,0:T(8,128)(2,1)S(1)}, bf16[528,256]{1,0:T(8,128)(2,1)S(1)}, u32[]{:S(2)}, u32[]{:S(2)}) collective-permute-start(bf16[528,256]{1,0:T(8,128)(2,1)S(1)} %collective-permute-done.1.ours), channel_id=1, source_target_pairs={{0,1},{1,0},{2,3},{3,2},{4,5},{5,4},{6,7},{7,6},{8,9},{9,8},{10,11... | collective-permute-start | bytes 811016 | tf_op jit(solution)/shard_map/ppermute | solution.py:402
  23.7 2.4 %collective-permute-start.6 = (bf16[512,256]{1,0:T(8,128)(2,1)S(1)}, bf16[512,256]{1,0:T(8,128)(2,1)S(1)}, u32[]{:S(2)}, u32[]{:S(2)}) collective-permute-start(bf16[512,256]{1,0:T(8,128)(2,1)S(1)} %get-tuple-element.62), channel_id=1, source_target_pairs={{0,2},{2,4},{4,6},{6,8},{8,10},{10,12},{12,14},{1,3},{3,5},{5,7},{... | collective-permute-start | bytes 786440 | tf_op jit(solution)/shard_map/ppermute | solution.py:433
  26.1 0.0 collective-permute-done.4.far
  26.1 0.0 collective-permute-done.3.near
  26.1 3.6 %edge.1 = (bf16[1,2,10,256,256]{4,3,2,1,0:T(8,128)(2,1)}, bf16[16,512,256]{2,1,0:T(8,128)(2,1)S(1)}, bf16[16,512,256]{2,1,0:T(8,128)(2,1)S(1)}, f32[8,256]{1,0:T...) custom-call(s32[4]{0:T(128)S(4)} %get-tuple-element.36.steps, ...), custom_call_target="tpu_custom_call", output_to_operand_aliasing={{1}: (6, {}), {2}: (7, {})} | custom-call | tf_op jit(solution)/shard_map/edge/pallas_call | solution.py:371
  29.7 1.2 %collective-permute-done.5.buffer = bf16[768,256]{1,0:T(8,128)(2,1)S(1)} collective-permute-done((bf16[768,256]{1,0:T(8,128)(2,1)S(1)}, bf16[768,256]{1,0:T(8,128)(2,1)S(1)}, u32[]{:S(2)}, u32[]{:S(2)}) %collective-permute-start.5) | collective-permute-done | bytes 393248 | tf_op jit(solution)/shard_map/ppermute | solution.py:433
  30.9 3.0 %run_5.1 = (bf16[1,2,10,256,256]{4,3,2,1,0:T(8,128)(2,1)}, bf16[16,512,256]{2,1,0:T(8,128)(2,1)S(1)}, bf16[16,512,256]{2,1,0:T(8,128)(2,1)S(1)}, f32[8,256]{1,0:...) custom-call(s32[4]{0:T(128)S(4)} %get-tuple-element.36.steps, ...), custom_call_target="tpu_custom_call", output_to_operand_aliasing={{1}: (9, {}), {2}: (10, {}), {0}: (11, {})} | custom-call | tf_op jit(solution)/shard_map/run_5/pallas_call | solution.py:371
  34.0 2.6 %collective-permute-done.6.buffer = bf16[512,256]{1,0:T(8,128)(2,1)S(1)} collective-permute-done((bf16[512,256]{1,0:T(8,128)(2,1)S(1)}, bf16[512,256]{1,0:T(8,128)(2,1)S(1)}, u32[]{:S(2)}, u32[]{:S(2)}) %collective-permute-start.6) | collective-permute-done | bytes 262176 | tf_op jit(solution)/shard_map/ppermute | solution.py:433
  36.5 4.7 %run_8.1 = (bf16[1,2,10,256,256]{4,3,2,1,0:T(8,128)(2,1)}, bf16[16,512,256]{2,1,0:T(8,128)(2,1)S(1)}, bf16[16,512,256]{2,1,0:T(8,128)(2,1)S(1)}, f32[8,256]{1,0:T(8,128)}, f32[2,2,2]{2,1,0:T(2,128)S(1)}) custom-call(s32[4]{0:T(128)S(4)} %get-tuple-element.36.steps, ...), custom_call_target="tpu_custom_call", output_to_operand_aliasing={{1}: (9, {}), {2}: (10, {}), {0}: (11, {})} | custom-call | tf_op jit(solution)/shard_map/run_8/pallas_call | solution.py:371
  41.3 0.9 %collective-permute-start.7 = (f32[2,2,2]{2,1,0:T(2,128)S(1)}, f32[2,2,2]{2,1,0:T(2,128)S(1)}, u32[]{:S(2)}, u32[]{:S(2)}) collective-permute-start(f32[2,2,2]{2,1,0:T(2,128)S(1)} %get-tuple-element.69), channel_id=1, source_target_pairs={{0,1},{1,0},{2,3},{3,2},{4,5},{5,4},{6,7},{7,6},{8,9},{9,8},{10,11... | collective-permute-start | bytes 104 | tf_op jit(solution)/shard_map/ppermute | solution.py:402
  42.1 0.8 %collective-permute-done.7 = f32[2,2,2]{2,1,0:T(2,128)S(1)} collective-permute-done((f32[2,2,2]{2,1,0:T(2,128)S(1)}, f32[2,2,2]{2,1,0:T(2,128)S(1)}, u32[]{:S(2)}, u32[]{:S(2)}) %collective-permute-start.7) | collective-permute-done | bytes 64 | tf_op jit(solution)/shard_map/ppermute | solution.py:402
  43.0 0.6 %add.3 = f32[2,2,2]{2,1,0:T(2,128)} add(f32[2,2,2]{2,1,0:T(2,128)S(1)} %get-tuple-element.69, f32[2,2,2]{2,1,0:T(2,128)S(1)} %collective-permute-done.7) | non-fusion elementwise | flops 8 | bytes 96 | tf_op jit(solution)/shard_map/add | solution.py:465
Async XLA Ops:
  4.1 3.0 %collective-permute-start = (bf16[4,512,256]{2,1,0:T(8,128)(2,1)S(1)}, bf16[4,512,256]{2,1,0:T(8,128)(2,1)S(1)}, u32[]{:S(2)}, u32[]{:S(2)}) collective-permute-start(bf16[4,512,256]{2,1,0:T(8,128)(2,1)S(1)} %get-tuple-element.39), channel_id=1, source_target_pairs={{0,1},{1,0},{2,3},{3,2},{4,5},{5,4},{6,7},{7,6},{8,9},{9,8},{10,11... | collective-permute-start | bytes 3145736 | tf_op jit(solution)/shard_map/ppermute | solution.py:402
  4.9 12.6 %collective-permute-start.2 = (bf16[784,256]{1,0:T(8,128)(2,1)S(1)}, bf16[784,256]{1,0:T(8,128)(2,1)S(1)}, u32[]{:S(2)}, u32[]{:S(2)}) collective-permute-start(bf16[784,256]{1,0:T(8,128)(2,1)S(1)} %get-tuple-element.48), channel_id=1, source_target_pairs={{0,2},{2,4},{4,6},{6,8},{8,10},{10,12},{12,14},{14,0},{1,3},{3,5},... | collective-permute-start | bytes 1204232 | tf_op jit(solution)/shard_map/ppermute | solution.py:423
  11.2 11.3 %collective-permute-start.1 = (bf16[528,256]{1,0:T(8,128)(2,1)S(1)}, bf16[528,256]{1,0:T(8,128)(2,1)S(1)}, u32[]{:S(2)}, u32[]{:S(2)}) collective-permute-start(bf16[528,256]{1,0:T(8,128)(2,1)S(1)} %get-tuple-element.47), channel_id=1, source_target_pairs={{0,2},{2,4},{4,6},{6,8},{8,10},{10,12},{12,14},{1,3},{3,5},{5,7},{... | collective-permute-start | bytes 811016 | tf_op jit(solution)/shard_map/ppermute | solution.py:433
  14.3 16.6 %collective-permute-start.5 = (bf16[768,256]{1,0:T(8,128)(2,1)S(1)}, bf16[768,256]{1,0:T(8,128)(2,1)S(1)}, u32[]{:S(2)}, u32[]{:S(2)}) collective-permute-start(bf16[768,256]{1,0:T(8,128)(2,1)S(1)} %get-tuple-element.55), channel_id=1, source_target_pairs={{0,2},{2,4},{4,6},{6,8},{8,10},{10,12},{12,14},{1,3},{3,5},{5,7},{... | collective-permute-start | bytes 1179656 | tf_op jit(solution)/shard_map/ppermute | solution.py:433
  17.8 8.3 %collective-permute-start.4 = (bf16[528,256]{1,0:T(8,128)(2,1)S(1)}, bf16[528,256]{1,0:T(8,128)(2,1)S(1)}, u32[]{:S(2)}, u32[]{:S(2)}) collective-permute-start(bf16[528,256]{1,0:T(8,128)(2,1)S(1)} %get-tuple-element.53), channel_id=1, source_target_pairs={{0,1},{1,0},{2,3},{3,2},{4,5},{5,4},{6,7},{7,6},{8,9},{9,8},{10,11... | collective-permute-start | bytes 811016 | tf_op jit(solution)/shard_map/ppermute | solution.py:402
  22.5 3.6 %collective-permute-start.3 = (bf16[528,256]{1,0:T(8,128)(2,1)S(1)}, bf16[528,256]{1,0:T(8,128)(2,1)S(1)}, u32[]{:S(2)}, u32[]{:S(2)}) collective-permute-start(bf16[528,256]{1,0:T(8,128)(2,1)S(1)} %collective-permute-done.1.ours), channel_id=1, source_target_pairs={{0,1},{1,0},{2,3},{3,2},{4,5},{5,4},{6,7},{7,6},{8,9},{9,8},{10,11... | collective-permute-start | bytes 811016 | tf_op jit(solution)/shard_map/ppermute | solution.py:402
  23.7 12.9 %collective-permute-start.6 = (bf16[512,256]{1,0:T(8,128)(2,1)S(1)}, bf16[512,256]{1,0:T(8,128)(2,1)S(1)}, u32[]{:S(2)}, u32[]{:S(2)}) collective-permute-start(bf16[512,256]{1,0:T(8,128)(2,1)S(1)} %get-tuple-element.62), channel_id=1, source_target_pairs={{0,2},{2,4},{4,6},{6,8},{8,10},{10,12},{12,14},{1,3},{3,5},{5,7},{... | collective-permute-start | bytes 786440 | tf_op jit(solution)/shard_map/ppermute | solution.py:433
  41.3 1.7 %collective-permute-start.7 = (f32[2,2,2]{2,1,0:T(2,128)S(1)}, f32[2,2,2]{2,1,0:T(2,128)S(1)}, u32[]{:S(2)}, u32[]{:S(2)}) collective-permute-start(f32[2,2,2]{2,1,0:T(2,128)S(1)} %get-tuple-element.69), channel_id=1, source_target_pairs={{0,1},{1,0},{2,3},{3,2},{4,5},{5,4},{6,7},{7,6},{8,9},{9,8},{10,11... | collective-permute-start | bytes 104 | tf_op jit(solution)/shard_map/ppermute | solution.py:402

commit v6 on v5

--- a/solution.py
+++ b/solution.py
@@ -108,13 +108,18 @@
     return dot(jnp.concatenate(halves, axis=0), block)
 
 
-def begin(place, todo, env, site, tensors, partial):
+def early_state(place, site, b, known):
+    nearer = 1 - place.core
+    return jnp.where(b + place.steps[2 * site + nearer] < known, nearer, 1 - nearer)
+
+
+def begin(place, todo, known, env, site, tensors, partial):
     for i, b in enumerate(range(*todo)):
-        partial[i] = one_state(place, env, site, 1 - place.core, tensors, b)
-
-
-def complete(place, i, b, env, site, tensors, partial):
-    both = partial[i] + one_state(place, env, site, place.core, tensors, b)
+        partial[i] = one_state(place, env, site, early_state(place, site, b, known), tensors, b)
+
+
+def complete(place, i, b, known, env, site, tensors, partial):
+    both = partial[i] + one_state(place, env, site, 1 - early_state(place, site, b, known), tensors, b)
     size = env.shape[-1]
     return both[:size], both[size:]
 
@@ -275,10 +280,10 @@
     send_rows(sents[0], rows)
 
 
-def middle_blocks(place, todo, env, middle, t0, traces, radius, partial=None):
+def middle_blocks(place, todo, env, middle, t0, traces, radius, partial=None, known=0):
     for i, b in enumerate(range(*todo)):
-        if partial is not None and i < HALO:
-            parts = complete(place, i, b, env, 0, t0, partial)
+        if partial is not None and i < partial.shape[0]:
+            parts = complete(place, i, b, known, env, 0, t0, partial)
         else:
             parts = advance(env, slots_of(place, 0, b), blocks_of(place, t0, b))
         store_env(middle, REACH + b, parts)
@@ -297,11 +302,11 @@
     piece[HALO * size :] = below(first)
 
 
-def final_blocks(place, todo, middle, t1, traces, radius, stage, out, sems, partial=None):
+def final_blocks(place, todo, middle, t1, traces, radius, stage, out, sems, partial=None, known=0):
     stores = Loads()
     for i, b in enumerate(range(*todo)):
-        if partial is not None and i < HALO:
-            parts = complete(place, i, b, middle, 1, t1, partial)
+        if partial is not None and i < partial.shape[0]:
+            parts = complete(place, i, b, known, middle, 1, t1, partial)
         else:
             parts = advance(middle, slots_of(place, 1, b), blocks_of(place, t1, b))
         for k in range(2):
@@ -326,8 +331,8 @@
     middle_blocks(place, (0, known - HALO), env, middle, t0, traces, radius)
     last = (0, known - 2 * HALO)
     stores = final_blocks(place, last, middle, t1, traces, radius, stage, out, sems)
-    begin(place, (known - HALO, known), env, 0, t0, partial0)
-    begin(place, (last[1], last[1] + HALO), middle, 1, t1, partial1)
+    begin(place, (known - HALO, known), known, env, 0, t0, partial0)
+    begin(place, (last[1], last[1] + HALO), known - HALO, middle, 1, t1, partial1)
     stores.wait(*range(*last))
 
 
@@ -341,9 +346,9 @@
     traces[...] = old_traces[...]
     ends = hi == width
     upto = width if ends else hi - HALO
-    middle_blocks(place, (lo - HALO, upto), env, middle, t0, traces, radius, old_partial0)
+    middle_blocks(place, (lo - HALO, upto), env, middle, t0, traces, radius, old_partial0, lo)
     last = (lo - 2 * HALO, width if ends else upto - HALO)
-    stores = final_blocks(place, last, middle, t1, traces, radius, stage, out, sems, old_partial1)
+    stores = final_blocks(place, last, middle, t1, traces, radius, stage, out, sems, old_partial1, lo - HALO)
     if ends:
         (totals,) = results
         sums = jnp.sum(traces[...], axis=1, keepdims=True)
@@ -352,8 +357,8 @@
                 at = 4 * j + 2 * t
                 totals[j, t : t + 1] = jnp.concatenate([sums[at : at + 1], sums[at + 1 : at + 2]], axis=1)
     else:
-        begin(place, (upto, hi), env, 0, t0, results[0])
-        begin(place, (last[1], upto), middle, 1, t1, results[1])
+        begin(place, (upto, upto + results[0].shape[0]), hi, env, 0, t0, results[0])
+        begin(place, (last[1], upto), upto, middle, 1, t1, results[1])
     stores.wait(*range(*last))
 
 
@@ -450,7 +455,11 @@
     )
     row = RUNS[1][1] - RUNS[1][0]
     for run, buffer in zip(RUNS[2:], got[2:]):
-        results = (partial_shape, partial_shape) if run[1] < width else (((2, 2, 2), F32, pltpu.VMEM),)
+        if run[1] == width:
+            results = (((2, 2, 2), F32, pltpu.VMEM),)
+        else:
+            begun = 2 * HALO if run[1] + HALO == width else HALO
+            results = (((begun, 2 * size, size), F32, pltpu.VMEM), partial_shape)
         final, env, middle, traces, *partials = call(
             functools.partial(next_kernel, width, run, row),
             "run_%d" % run[0],

time: 43.8 us -> 43.4 us (level)
  transfers between devices with their start and end apart: 8 -> 8, of which waited for: 5 -> 5; matrix products, arithmetic and copies ran while one was open for 0% -> 0% of each run, Pallas kernels for 25% -> 26%
where the time goes in v6:
time: 43.4 us; the launch traced here: 43.1 us
  Pallas kernels  18.9 us (44%)
  starting transfers between devices  13.7 us (32%)
  waiting for transfers between devices  9.25 us (21%)
  between operations  0.73 us (2%)
  other arithmetic  0.58 us (1%)
    pallas_call x6, Pallas kernels, call(): pl.pallas_call(kernel, out_shape=tuple((memory(s, d) for s, d, memory in...  18.9 us
    ppermute x3, starting transfers between devices, shards(): got += [lax.ppermute(s, 'site', ring[:-1]) for s in sents]  8.71 us
    ppermute x3, waiting for transfers between devices, shards(): got += [lax.ppermute(s, 'site', ring[:-1]) for s in sents]  7.37 us
    ppermute x4, starting transfers between devices, across(): return lax.ppermute(array, 'sec', swap)  3.76 us
    ppermute x4, waiting for transfers between devices, across(): return lax.ppermute(array, 'sec', swap)  1.87 us
    ppermute x1, starting transfers between devices, shards(): got = [lax.ppermute(sent, 'site', ring)]  1.24 us
  transfers between devices with their start and end apart: 8, of which 5 were waited for; matrix products, arithmetic and copies ran while one was open for 0% of the time, Pallas kernels for 26%

profile of v6, /device:TPU:17, one launch (start us, length us, event | category | flops | bytes accessed | tf_op | source)
XLA Modules:
  0.0 43.1 jit_solution(15486083781653137456)
XLA Ops:
  0.6 3.5 %anchor.1 = (bf16[784,256]{1,0:T(8,128)(2,1)S(1)}, bf16[4,512,256]{2,1,0:T(8,128)(2,1)S(1)}, bf16[16,512,256]{2,1,0:T(8,128)(2,1)S(1)}, bf16[2,10,256,256]{3,2,1...) custom-call(s32[16,2,20]{2,1,0:T(2,128)} %sources.1, ...), custom_call_target="tpu_custom_call" | custom-call | tf_op jit(solution)/shard_map/anchor/pallas_call | solution.py:376
  4.1 0.7 %collective-permute-start = (bf16[4,512,256]{2,1,0:T(8,128)(2,1)S(1)}, bf16[4,512,256]{2,1,0:T(8,128)(2,1)S(1)}, u32[]{:S(2)}, u32[]{:S(2)}) collective-permute-start(bf16[4,512,256]{2,1,0:T(8,128)(2,1)S(1)} %get-tuple-element.39), channel_id=1, source_target_pairs={{0,1},{1,0},{2,3},{3,2},{4,5},{5,4},{6,7},{7,6},{8,9},{9,8},{10,11... | collective-permute-start | bytes 3145736 | tf_op jit(solution)/shard_map/ppermute | solution.py:407
  4.9 1.2 %collective-permute-start.2 = (bf16[784,256]{1,0:T(8,128)(2,1)S(1)}, bf16[784,256]{1,0:T(8,128)(2,1)S(1)}, u32[]{:S(2)}, u32[]{:S(2)}) collective-permute-start(bf16[784,256]{1,0:T(8,128)(2,1)S(1)} %get-tuple-element.48), channel_id=1, source_target_pairs={{0,2},{2,4},{4,6},{6,8},{8,10},{10,12},{12,14},{14,0},{1,3},{3,5},... | collective-permute-start | bytes 1204232 | tf_op jit(solution)/shard_map/ppermute | solution.py:428
  6.1 1.0 %collective-permute-done.halo = bf16[4,512,256]{2,1,0:T(8,128)(2,1)S(1)} collective-permute-done((bf16[4,512,256]{2,1,0:T(8,128)(2,1)S(1)}, bf16[4,512,256]{2,1,0:T(8,128)(2,1)S(1)}, u32[]{:S(2)}, u32[]{:S(2)}) %collective-permute-start) | collective-permute-done | bytes 1048608 | tf_op jit(solution)/shard_map/ppermute | solution.py:407
  7.2 4.0 %anchor_rest.1 = (bf16[16,512,256]{2,1,0:T(8,128)(2,1)S(1)}, bf16[2,10,256,256]{3,2,1,0:T(8,128)(2,1)S(1)}, bf16[2,10,256,256]{3,2,1,0:T(8,128)(2,1)S(1)}, bf16[...) custom-call(s32[4]{0:T(128)S(4)} %get-tuple-element.36.steps, ...), custom_call_target="tpu_custom_call", output_to_operand_aliasing={{0}: (3, {}), {1}: (5, {}), {2}: (6, {})} | custom-call | tf_op jit(solution)/shard_map/anchor_rest/pallas_call | solution.py:376
  11.2 3.1 %collective-permute-start.1 = (bf16[528,256]{1,0:T(8,128)(2,1)S(1)}, bf16[528,256]{1,0:T(8,128)(2,1)S(1)}, u32[]{:S(2)}, u32[]{:S(2)}) collective-permute-start(bf16[528,256]{1,0:T(8,128)(2,1)S(1)} %get-tuple-element.47), channel_id=1, source_target_pairs={{0,2},{2,4},{4,6},{6,8},{8,10},{10,12},{12,14},{1,3},{3,5},{5,7},{... | collective-permute-start | bytes 811016 | tf_op jit(solution)/shard_map/ppermute | solution.py:438
  14.3 3.1 %collective-permute-start.5 = (bf16[768,256]{1,0:T(8,128)(2,1)S(1)}, bf16[768,256]{1,0:T(8,128)(2,1)S(1)}, u32[]{:S(2)}, u32[]{:S(2)}) collective-permute-start(bf16[768,256]{1,0:T(8,128)(2,1)S(1)} %get-tuple-element.55), channel_id=1, source_target_pairs={{0,2},{2,4},{4,6},{6,8},{8,10},{10,12},{12,14},{1,3},{3,5},{5,7},{... | collective-permute-start | bytes 1179656 | tf_op jit(solution)/shard_map/ppermute | solution.py:438
  17.5 0.0 collective-permute-done.2.first
  17.5 0.3 first_run.1
  17.8 1.0 %collective-permute-start.4 = (bf16[528,256]{1,0:T(8,128)(2,1)S(1)}, bf16[528,256]{1,0:T(8,128)(2,1)S(1)}, u32[]{:S(2)}, u32[]{:S(2)}) collective-permute-start(bf16[528,256]{1,0:T(8,128)(2,1)S(1)} %get-tuple-element.53), channel_id=1, source_target_pairs={{0,1},{1,0},{2,3},{3,2},{4,5},{5,4},{6,7},{7,6},{8,9},{9,8},{10,11... | collective-permute-start | bytes 811016 | tf_op jit(solution)/shard_map/ppermute | solution.py:407
  18.8 3.7 %collective-permute-done.1.ours = bf16[528,256]{1,0:T(8,128)(2,1)S(1)} collective-permute-done((bf16[528,256]{1,0:T(8,128)(2,1)S(1)}, bf16[528,256]{1,0:T(8,128)(2,1)S(1)}, u32[]{:S(2)}, u32[]{:S(2)}) %collective-permute-start.1) | collective-permute-done | bytes 270368 | tf_op jit(solution)/shard_map/ppermute | solution.py:438
  22.5 1.2 %collective-permute-start.3 = (bf16[528,256]{1,0:T(8,128)(2,1)S(1)}, bf16[528,256]{1,0:T(8,128)(2,1)S(1)}, u32[]{:S(2)}, u32[]{:S(2)}) collective-permute-start(bf16[528,256]{1,0:T(8,128)(2,1)S(1)} %collective-permute-done.1.ours), channel_id=1, source_target_pairs={{0,1},{1,0},{2,3},{3,2},{4,5},{5,4},{6,7},{7,6},{8,9},{9,8},{10,11... | collective-permute-start | bytes 811016 | tf_op jit(solution)/shard_map/ppermute | solution.py:407
  23.7 2.4 %collective-permute-start.6 = (bf16[512,256]{1,0:T(8,128)(2,1)S(1)}, bf16[512,256]{1,0:T(8,128)(2,1)S(1)}, u32[]{:S(2)}, u32[]{:S(2)}) collective-permute-start(bf16[512,256]{1,0:T(8,128)(2,1)S(1)} %get-tuple-element.62), channel_id=1, source_target_pairs={{0,2},{2,4},{4,6},{6,8},{8,10},{10,12},{12,14},{1,3},{3,5},{5,7},{... | collective-permute-start | bytes 786440 | tf_op jit(solution)/shard_map/ppermute | solution.py:438
  26.1 0.0 collective-permute-done.4.far
  26.1 0.0 collective-permute-done.3.near
  26.1 3.5 %edge.1 = (bf16[1,2,10,256,256]{4,3,2,1,0:T(8,128)(2,1)}, bf16[16,512,256]{2,1,0:T(8,128)(2,1)S(1)}, bf16[16,512,256]{2,1,0:T(8,128)(2,1)S(1)}, f32[8,256]{1,0:T...) custom-call(s32[4]{0:T(128)S(4)} %get-tuple-element.36.steps, ...), custom_call_target="tpu_custom_call", output_to_operand_aliasing={{1}: (6, {}), {2}: (7, {})} | custom-call | tf_op jit(solution)/shard_map/edge/pallas_call | solution.py:376
  29.7 1.3 %collective-permute-done.5.buffer = bf16[768,256]{1,0:T(8,128)(2,1)S(1)} collective-permute-done((bf16[768,256]{1,0:T(8,128)(2,1)S(1)}, bf16[768,256]{1,0:T(8,128)(2,1)S(1)}, u32[]{:S(2)}, u32[]{:S(2)}) %collective-permute-start.5) | collective-permute-done | bytes 393248 | tf_op jit(solution)/shard_map/ppermute | solution.py:438
  30.9 3.2 %run_5.1 = (bf16[1,2,10,256,256]{4,3,2,1,0:T(8,128)(2,1)}, bf16[16,512,256]{2,1,0:T(8,128)(2,1)S(1)}, bf16[16,512,256]{2,1,0:T(8,128)(2,1)S(1)}, f32[8,256]{1,0:...) custom-call(s32[4]{0:T(128)S(4)} %get-tuple-element.36.steps, ...), custom_call_target="tpu_custom_call", output_to_operand_aliasing={{1}: (9, {}), {2}: (10, {}), {0}: (11, {})} | custom-call | tf_op jit(solution)/shard_map/run_5/pallas_call | solution.py:376
  34.1 2.4 %collective-permute-done.6.buffer = bf16[512,256]{1,0:T(8,128)(2,1)S(1)} collective-permute-done((bf16[512,256]{1,0:T(8,128)(2,1)S(1)}, bf16[512,256]{1,0:T(8,128)(2,1)S(1)}, u32[]{:S(2)}, u32[]{:S(2)}) %collective-permute-start.6) | collective-permute-done | bytes 262176 | tf_op jit(solution)/shard_map/ppermute | solution.py:438
  36.5 4.4 %run_8.1 = (bf16[1,2,10,256,256]{4,3,2,1,0:T(8,128)(2,1)}, bf16[16,512,256]{2,1,0:T(8,128)(2,1)S(1)}, bf16[16,512,256]{2,1,0:T(8,128)(2,1)S(1)}, f32[8,256]{1,0:T(8,128)}, f32[2,2,2]{2,1,0:T(2,128)S(1)}) custom-call(s32[4]{0:T(128)S(4)} %get-tuple-element.36.steps, ...), custom_call_target="tpu_custom_call", output_to_operand_aliasing={{1}: (9, {}), {2}: (10, {}), {0}: (11, {})} | custom-call | tf_op jit(solution)/shard_map/run_8/pallas_call | solution.py:376
  40.9 0.8 %collective-permute-start.7 = (f32[2,2,2]{2,1,0:T(2,128)S(1)}, f32[2,2,2]{2,1,0:T(2,128)S(1)}, u32[]{:S(2)}, u32[]{:S(2)}) collective-permute-start(f32[2,2,2]{2,1,0:T(2,128)S(1)} %get-tuple-element.69), channel_id=1, source_target_pairs={{0,1},{1,0},{2,3},{3,2},{4,5},{5,4},{6,7},{7,6},{8,9},{9,8},{10,11... | collective-permute-start | bytes 104 | tf_op jit(solution)/shard_map/ppermute | solution.py:407
  41.7 0.8 %collective-permute-done.7 = f32[2,2,2]{2,1,0:T(2,128)S(1)} collective-permute-done((f32[2,2,2]{2,1,0:T(2,128)S(1)}, f32[2,2,2]{2,1,0:T(2,128)S(1)}, u32[]{:S(2)}, u32[]{:S(2)}) %collective-permute-start.7) | collective-permute-done | bytes 64 | tf_op jit(solution)/shard_map/ppermute | solution.py:407
  42.6 0.6 %add.3 = f32[2,2,2]{2,1,0:T(2,128)} add(f32[2,2,2]{2,1,0:T(2,128)S(1)} %get-tuple-element.69, f32[2,2,2]{2,1,0:T(2,128)S(1)} %collective-permute-done.7) | non-fusion elementwise | flops 8 | bytes 96 | tf_op jit(solution)/shard_map/add | solution.py:474
Async XLA Ops:
  4.1 3.0 %collective-permute-start = (bf16[4,512,256]{2,1,0:T(8,128)(2,1)S(1)}, bf16[4,512,256]{2,1,0:T(8,128)(2,1)S(1)}, u32[]{:S(2)}, u32[]{:S(2)}) collective-permute-start(bf16[4,512,256]{2,1,0:T(8,128)(2,1)S(1)} %get-tuple-element.39), channel_id=1, source_target_pairs={{0,1},{1,0},{2,3},{3,2},{4,5},{5,4},{6,7},{7,6},{8,9},{9,8},{10,11... | collective-permute-start | bytes 3145736 | tf_op jit(solution)/shard_map/ppermute | solution.py:407
  4.9 12.6 %collective-permute-start.2 = (bf16[784,256]{1,0:T(8,128)(2,1)S(1)}, bf16[784,256]{1,0:T(8,128)(2,1)S(1)}, u32[]{:S(2)}, u32[]{:S(2)}) collective-permute-start(bf16[784,256]{1,0:T(8,128)(2,1)S(1)} %get-tuple-element.48), channel_id=1, source_target_pairs={{0,2},{2,4},{4,6},{6,8},{8,10},{10,12},{12,14},{14,0},{1,3},{3,5},... | collective-permute-start | bytes 1204232 | tf_op jit(solution)/shard_map/ppermute | solution.py:428
  11.2 11.3 %collective-permute-start.1 = (bf16[528,256]{1,0:T(8,128)(2,1)S(1)}, bf16[528,256]{1,0:T(8,128)(2,1)S(1)}, u32[]{:S(2)}, u32[]{:S(2)}) collective-permute-start(bf16[528,256]{1,0:T(8,128)(2,1)S(1)} %get-tuple-element.47), channel_id=1, source_target_pairs={{0,2},{2,4},{4,6},{6,8},{8,10},{10,12},{12,14},{1,3},{3,5},{5,7},{... | collective-permute-start | bytes 811016 | tf_op jit(solution)/shard_map/ppermute | solution.py:438
  14.3 16.6 %collective-permute-start.5 = (bf16[768,256]{1,0:T(8,128)(2,1)S(1)}, bf16[768,256]{1,0:T(8,128)(2,1)S(1)}, u32[]{:S(2)}, u32[]{:S(2)}) collective-permute-start(bf16[768,256]{1,0:T(8,128)(2,1)S(1)} %get-tuple-element.55), channel_id=1, source_target_pairs={{0,2},{2,4},{4,6},{6,8},{8,10},{10,12},{12,14},{1,3},{3,5},{5,7},{... | collective-permute-start | bytes 1179656 | tf_op jit(solution)/shard_map/ppermute | solution.py:438
  17.8 8.3 %collective-permute-start.4 = (bf16[528,256]{1,0:T(8,128)(2,1)S(1)}, bf16[528,256]{1,0:T(8,128)(2,1)S(1)}, u32[]{:S(2)}, u32[]{:S(2)}) collective-permute-start(bf16[528,256]{1,0:T(8,128)(2,1)S(1)} %get-tuple-element.53), channel_id=1, source_target_pairs={{0,1},{1,0},{2,3},{3,2},{4,5},{5,4},{6,7},{7,6},{8,9},{9,8},{10,11... | collective-permute-start | bytes 811016 | tf_op jit(solution)/shard_map/ppermute | solution.py:407
  22.5 3.6 %collective-permute-start.3 = (bf16[528,256]{1,0:T(8,128)(2,1)S(1)}, bf16[528,256]{1,0:T(8,128)(2,1)S(1)}, u32[]{:S(2)}, u32[]{:S(2)}) collective-permute-start(bf16[528,256]{1,0:T(8,128)(2,1)S(1)} %collective-permute-done.1.ours), channel_id=1, source_target_pairs={{0,1},{1,0},{2,3},{3,2},{4,5},{5,4},{6,7},{7,6},{8,9},{9,8},{10,11... | collective-permute-start | bytes 811016 | tf_op jit(solution)/shard_map/ppermute | solution.py:407
  23.7 12.9 %collective-permute-start.6 = (bf16[512,256]{1,0:T(8,128)(2,1)S(1)}, bf16[512,256]{1,0:T(8,128)(2,1)S(1)}, u32[]{:S(2)}, u32[]{:S(2)}) collective-permute-start(bf16[512,256]{1,0:T(8,128)(2,1)S(1)} %get-tuple-element.62), channel_id=1, source_target_pairs={{0,2},{2,4},{4,6},{6,8},{8,10},{10,12},{12,14},{1,3},{3,5},{5,7},{... | collective-permute-start | bytes 786440 | tf_op jit(solution)/shard_map/ppermute | solution.py:438
  40.9 1.7 %collective-permute-start.7 = (f32[2,2,2]{2,1,0:T(2,128)S(1)}, f32[2,2,2]{2,1,0:T(2,128)S(1)}, u32[]{:S(2)}, u32[]{:S(2)}) collective-permute-start(f32[2,2,2]{2,1,0:T(2,128)S(1)} %get-tuple-element.69), channel_id=1, source_target_pairs={{0,1},{1,0},{2,3},{3,2},{4,5},{5,4},{6,7},{7,6},{8,9},{9,8},{10,11... | collective-permute-start | bytes 104 | tf_op jit(solution)/shard_map/ppermute | solution.py:407

commit v7 on v6

--- a/solution.py
+++ b/solution.py
@@ -311,7 +311,8 @@
             parts = advance(middle, slots_of(place, 1, b), blocks_of(place, t1, b))
         for k in range(2):
             stage[b, k] = parts[k].astype(BF16)
-        stores.start(b, stage.at[b], out.at[0, :, place.local(b)], sems.at[b])
+        if out is not None:
+            stores.start(b, stage.at[b], out.at[0, :, place.local(b)], sems.at[b])
         add_traces(place, traces, 6, 1, b, parts, radius)
     return stores
 
@@ -337,10 +338,14 @@
 
 
 def next_kernel(width, run, row, steps, t0, t1, radius, old_traces, ours, buffer, old_partial0, old_partial1, old_env, old_middle,
-                old_out, out, env, middle, traces, *rest):
-    results, (stage, sems) = rest[:-2], rest[-2:]
+                *rest):
+    lo, hi = run
+    if hi == width:
+        env, middle, traces, totals, stage = rest
+        out = sems = None
+    else:
+        out, env, middle, traces, *results, stage, sems = rest[1:]
     place = Place(width, steps)
-    lo, hi = run
     for b in range(lo, hi):
         take(place, buffer, b - lo, below(ours), row + b - lo, env, REACH + b)
     traces[...] = old_traces[...]
@@ -350,16 +355,25 @@
     last = (lo - 2 * HALO, width if ends else upto - HALO)
     stores = final_blocks(place, last, middle, t1, traces, radius, stage, out, sems, old_partial1, lo - HALO)
     if ends:
-        (totals,) = results
+        totals[...] = jnp.zeros_like(totals)
         sums = jnp.sum(traces[...], axis=1, keepdims=True)
         for j in range(2):
             for t in range(2):
                 at = 4 * j + 2 * t
-                totals[j, t : t + 1] = jnp.concatenate([sums[at : at + 1], sums[at + 1 : at + 2]], axis=1)
+                totals[j, t : t + 1, :2] = jnp.concatenate([sums[at : at + 1], sums[at + 1 : at + 2]], axis=1)
     else:
         begin(place, (upto, upto + results[0].shape[0]), hi, env, 0, t0, results[0])
         begin(place, (last[1], upto), upto, middle, 1, t1, results[1])
-    stores.wait(*range(*last))
+    if out is not None:
+        stores.wait(*range(*last))
+
+
+def store_kernel(width, todo, steps, stage, old_out, out, sems):
+    place = Place(width, steps)
+    stores = Loads()
+    for b in range(*todo):
+        stores.start(b, stage.at[b], out.at[0, :, place.local(b)], sems.at[b])
+    stores.wait(*range(*todo))
 
 
 SMEM = pl.BlockSpec(memory_space=pltpu.SMEM)
@@ -454,24 +468,35 @@
         {6: 1, 7: 2},
     )
     row = RUNS[1][1] - RUNS[1][0]
-    for run, buffer in zip(RUNS[2:], got[2:]):
-        if run[1] == width:
-            results = (((2, 2, 2), F32, pltpu.VMEM),)
-        else:
-            begun = 2 * HALO if run[1] + HALO == width else HALO
-            results = (((begun, 2 * size, size), F32, pltpu.VMEM), partial_shape)
-        final, env, middle, traces, *partials = call(
-            functools.partial(next_kernel, width, run, row),
-            "run_%d" % run[0],
-            (steps,),
-            tuple((a, True) for a in (t0, t1, radius, traces, ours, buffer, *partials, env, middle)) + ((final, False),),
-            (out_shape, env_shape, env_shape, trace_shape) + results,
-            stage,
-            {9: 1, 10: 2, 11: 0},
-        )
-        row += run[1] - run[0]
-    (totals,) = partials
-    return final, totals + across(totals)
+    run, last = RUNS[2:]
+    final, env, middle, traces, *partials = call(
+        functools.partial(next_kernel, width, run, row),
+        "third_run",
+        (steps,),
+        tuple((a, True) for a in (t0, t1, radius, traces, ours, got[2], *partials, env, middle)) + ((final, False),),
+        (out_shape, env_shape, env_shape, trace_shape, ((2 * HALO, 2 * size, size), F32, pltpu.VMEM), partial_shape),
+        stage,
+        {9: 1, 10: 2, 11: 0},
+    )
+    env, middle, traces, totals, blocks = call(
+        functools.partial(next_kernel, width, last, row + run[1] - run[0]),
+        "last_run",
+        (steps,),
+        tuple((a, True) for a in (t0, t1, radius, traces, ours, got[3], *partials, env, middle)),
+        (env_shape, env_shape, trace_shape, ((2, 16, 128), F32, pltpu.VMEM), ((width, 2, size, size), BF16, pltpu.VMEM)),
+        aliases={9: 0, 10: 1},
+    )
+    others = across(totals)
+    (final,) = call(
+        functools.partial(store_kernel, width, (last[0] - 2 * HALO, width)),
+        "store",
+        (steps,),
+        ((blocks, True), (final, False)),
+        (out_shape,),
+        stage[1:],
+        {2: 0},
+    )
+    return final, totals[:, :2, :2] + others[:, :2, :2]
 
 
 def solution(mesh):

time: 43.4 us -> 43 us (level)
  waiting for transfers between devices: 9.25 us -> 8.47 us
    ppermute x4, waiting for transfers between devices: 1.87 us -> 1.06 us  [across(): return lax.ppermute(array, 'sec', swap)]
    pallas_call x6 -> x7, Pallas kernels: 18.9 us -> 19.3 us  [call(): pl.pallas_call(kernel, out_shape=tuple((memory(s, d) for s, d, memory in...]
  transfers between devices with their start and end apart: 8 -> 8, of which waited for: 5 -> 4; matrix products, arithmetic and copies ran while one was open for 0% -> 0% of each run, Pallas kernels for 26% -> 29%
where the time goes in v7:
time: 43 us; the launch traced here: 42.7 us
  Pallas kernels  19.3 us (45%)
  starting transfers between devices  13.6 us (32%)
  waiting for transfers between devices  8.47 us (20%)
  between operations  0.74 us (2%)
  other arithmetic  0.58 us (1%)
    pallas_call x7, Pallas kernels, call(): pl.pallas_call(kernel, out_shape=tuple((memory(s, d) for s, d, memory in...  19.3 us
    ppermute x3, starting transfers between devices, shards(): got += [lax.ppermute(s, 'site', ring[:-1]) for s in sents]  8.71 us
    ppermute x3, waiting for transfers between devices, shards(): got += [lax.ppermute(s, 'site', ring[:-1]) for s in sents]  7.41 us
    ppermute x4, starting transfers between devices, across(): return lax.ppermute(array, 'sec', swap)  3.7 us
    ppermute x1, starting transfers between devices, shards(): got = [lax.ppermute(sent, 'site', ring)]  1.24 us
    ppermute x4, waiting for transfers between devices, across(): return lax.ppermute(array, 'sec', swap)  1.06 us
  transfers between devices with their start and end apart: 8, of which 4 were waited for; matrix products, arithmetic and copies ran while one was open for 0% of the time, Pallas kernels for 29%

profile of v7, /device:TPU:17, one launch (start us, length us, event | category | flops | bytes accessed | tf_op | source)
XLA Modules:
  0.0 42.7 jit_solution(17095910466690439674)
XLA Ops:
  0.6 3.5 %anchor.1 = (bf16[784,256]{1,0:T(8,128)(2,1)S(1)}, bf16[4,512,256]{2,1,0:T(8,128)(2,1)S(1)}, bf16[16,512,256]{2,1,0:T(8,128)(2,1)S(1)}, bf16[2,10,256,256]{3,2,1...) custom-call(s32[16,2,20]{2,1,0:T(2,128)} %sources.1, ...), custom_call_target="tpu_custom_call" | custom-call | tf_op jit(solution)/shard_map/anchor/pallas_call | solution.py:390
  4.1 0.7 %collective-permute-start = (bf16[4,512,256]{2,1,0:T(8,128)(2,1)S(1)}, bf16[4,512,256]{2,1,0:T(8,128)(2,1)S(1)}, u32[]{:S(2)}, u32[]{:S(2)}) collective-permute-start(bf16[4,512,256]{2,1,0:T(8,128)(2,1)S(1)} %get-tuple-element.39), channel_id=1, source_target_pairs={{0,1},{1,0},{2,3},{3,2},{4,5},{5,4},{6,7},{7,6},{8,9},{9,8},{10,11... | collective-permute-start | bytes 3145736 | tf_op jit(solution)/shard_map/ppermute | solution.py:421
  4.9 1.2 %collective-permute-start.2 = (bf16[784,256]{1,0:T(8,128)(2,1)S(1)}, bf16[784,256]{1,0:T(8,128)(2,1)S(1)}, u32[]{:S(2)}, u32[]{:S(2)}) collective-permute-start(bf16[784,256]{1,0:T(8,128)(2,1)S(1)} %get-tuple-element.48), channel_id=1, source_target_pairs={{0,2},{2,4},{4,6},{6,8},{8,10},{10,12},{12,14},{14,0},{1,3},{3,5},... | collective-permute-start | bytes 1204232 | tf_op jit(solution)/shard_map/ppermute | solution.py:442
  6.1 1.0 %collective-permute-done.halo = bf16[4,512,256]{2,1,0:T(8,128)(2,1)S(1)} collective-permute-done((bf16[4,512,256]{2,1,0:T(8,128)(2,1)S(1)}, bf16[4,512,256]{2,1,0:T(8,128)(2,1)S(1)}, u32[]{:S(2)}, u32[]{:S(2)}) %collective-permute-start) | collective-permute-done | bytes 1048608 | tf_op jit(solution)/shard_map/ppermute | solution.py:421
  7.2 4.0 %anchor_rest.1 = (bf16[16,512,256]{2,1,0:T(8,128)(2,1)S(1)}, bf16[2,10,256,256]{3,2,1,0:T(8,128)(2,1)S(1)}, bf16[2,10,256,256]{3,2,1,0:T(8,128)(2,1)S(1)}, bf16[...) custom-call(s32[4]{0:T(128)S(4)} %get-tuple-element.36.steps, ...), custom_call_target="tpu_custom_call", output_to_operand_aliasing={{0}: (3, {}), {1}: (5, {}), {2}: (6, {})} | custom-call | tf_op jit(solution)/shard_map/anchor_rest/pallas_call | solution.py:390
  11.2 3.1 %collective-permute-start.1 = (bf16[528,256]{1,0:T(8,128)(2,1)S(1)}, bf16[528,256]{1,0:T(8,128)(2,1)S(1)}, u32[]{:S(2)}, u32[]{:S(2)}) collective-permute-start(bf16[528,256]{1,0:T(8,128)(2,1)S(1)} %get-tuple-element.47), channel_id=1, source_target_pairs={{0,2},{2,4},{4,6},{6,8},{8,10},{10,12},{12,14},{1,3},{3,5},{5,7},{... | collective-permute-start | bytes 811016 | tf_op jit(solution)/shard_map/ppermute | solution.py:452
  14.3 3.1 %collective-permute-start.5 = (bf16[768,256]{1,0:T(8,128)(2,1)S(1)}, bf16[768,256]{1,0:T(8,128)(2,1)S(1)}, u32[]{:S(2)}, u32[]{:S(2)}) collective-permute-start(bf16[768,256]{1,0:T(8,128)(2,1)S(1)} %get-tuple-element.55), channel_id=1, source_target_pairs={{0,2},{2,4},{4,6},{6,8},{8,10},{10,12},{12,14},{1,3},{3,5},{5,7},{... | collective-permute-start | bytes 1179656 | tf_op jit(solution)/shard_map/ppermute | solution.py:452
  17.5 0.0 collective-permute-done.2.first
  17.5 0.3 first_run.1
  17.8 1.0 %collective-permute-start.4 = (bf16[528,256]{1,0:T(8,128)(2,1)S(1)}, bf16[528,256]{1,0:T(8,128)(2,1)S(1)}, u32[]{:S(2)}, u32[]{:S(2)}) collective-permute-start(bf16[528,256]{1,0:T(8,128)(2,1)S(1)} %get-tuple-element.53), channel_id=1, source_target_pairs={{0,1},{1,0},{2,3},{3,2},{4,5},{5,4},{6,7},{7,6},{8,9},{9,8},{10,11... | collective-permute-start | bytes 811016 | tf_op jit(solution)/shard_map/ppermute | solution.py:421
  18.8 3.7 %collective-permute-done.1.ours = bf16[528,256]{1,0:T(8,128)(2,1)S(1)} collective-permute-done((bf16[528,256]{1,0:T(8,128)(2,1)S(1)}, bf16[528,256]{1,0:T(8,128)(2,1)S(1)}, u32[]{:S(2)}, u32[]{:S(2)}) %collective-permute-start.1) | collective-permute-done | bytes 270368 | tf_op jit(solution)/shard_map/ppermute | solution.py:452
  22.5 1.2 %collective-permute-start.3 = (bf16[528,256]{1,0:T(8,128)(2,1)S(1)}, bf16[528,256]{1,0:T(8,128)(2,1)S(1)}, u32[]{:S(2)}, u32[]{:S(2)}) collective-permute-start(bf16[528,256]{1,0:T(8,128)(2,1)S(1)} %collective-permute-done.1.ours), channel_id=1, source_target_pairs={{0,1},{1,0},{2,3},{3,2},{4,5},{5,4},{6,7},{7,6},{8,9},{9,8},{10,11... | collective-permute-start | bytes 811016 | tf_op jit(solution)/shard_map/ppermute | solution.py:421
  23.7 2.4 %collective-permute-start.6 = (bf16[512,256]{1,0:T(8,128)(2,1)S(1)}, bf16[512,256]{1,0:T(8,128)(2,1)S(1)}, u32[]{:S(2)}, u32[]{:S(2)}) collective-permute-start(bf16[512,256]{1,0:T(8,128)(2,1)S(1)} %get-tuple-element.62), channel_id=1, source_target_pairs={{0,2},{2,4},{4,6},{6,8},{8,10},{10,12},{12,14},{1,3},{3,5},{5,7},{... | collective-permute-start | bytes 786440 | tf_op jit(solution)/shard_map/ppermute | solution.py:452
  26.1 0.0 collective-permute-done.4.far
  26.1 0.0 collective-permute-done.3.near
  26.1 3.5 %edge.1 = (bf16[1,2,10,256,256]{4,3,2,1,0:T(8,128)(2,1)}, bf16[16,512,256]{2,1,0:T(8,128)(2,1)S(1)}, bf16[16,512,256]{2,1,0:T(8,128)(2,1)S(1)}, f32[8,256]{1,0:T...) custom-call(s32[4]{0:T(128)S(4)} %get-tuple-element.36.steps, ...), custom_call_target="tpu_custom_call", output_to_operand_aliasing={{1}: (6, {}), {2}: (7, {})} | custom-call | tf_op jit(solution)/shard_map/edge/pallas_call | solution.py:390
  29.7 1.3 %collective-permute-done.5.buffer = bf16[768,256]{1,0:T(8,128)(2,1)S(1)} collective-permute-done((bf16[768,256]{1,0:T(8,128)(2,1)S(1)}, bf16[768,256]{1,0:T(8,128)(2,1)S(1)}, u32[]{:S(2)}, u32[]{:S(2)}) %collective-permute-start.5) | collective-permute-done | bytes 393248 | tf_op jit(solution)/shard_map/ppermute | solution.py:452
  30.9 3.1 %third_run.1 = (bf16[1,2,10,256,256]{4,3,2,1,0:T(8,128)(2,1)}, bf16[16,512,256]{2,1,0:T(8,128)(2,1)S(1)}, bf16[16,512,256]{2,1,0:T(8,128)(2,1)S(1)}, f32[8,256]{...) custom-call(s32[4]{0:T(128)S(4)} %get-tuple-element.36.steps, ...), custom_call_target="tpu_custom_call", output_to_operand_aliasing={{1}: (9, {}), {2}: (10, {}), {0}: (11, {})} | custom-call | tf_op jit(solution)/shard_map/third_run/pallas_call | solution.py:390
  34.1 2.5 %collective-permute-done.6.buffer = bf16[512,256]{1,0:T(8,128)(2,1)S(1)} collective-permute-done((bf16[512,256]{1,0:T(8,128)(2,1)S(1)}, bf16[512,256]{1,0:T(8,128)(2,1)S(1)}, u32[]{:S(2)}, u32[]{:S(2)}) %collective-permute-start.6) | collective-permute-done | bytes 262176 | tf_op jit(solution)/shard_map/ppermute | solution.py:452
  36.5 3.5 %last_run.1 = (bf16[16,512,256]{2,1,0:T(8,128)(2,1)S(1)}, bf16[16,512,256]{2,1,0:T(8,128)(2,1)S(1)}, f32[8,256]{1,0:T(8,128)}, f32[2,16,128]{2,1,0:T(8,128)S(1)}, bf16[10,2,256,256]{3,2,1,0:T(8,128)(2,1)S(1)}) custom-call(s32[4]{0:T(128)S(4)} %get-tuple-element.36.steps, ...), custom_call_target="tpu_custom_call", output_to_operand_aliasing={{0}: (9, {}), {1}: (10, {})} | custom-call | tf_op jit(solution)/shard_map/last_run/pallas_call | solution.py:390
  40.1 0.8 %collective-permute-start.7 = (f32[2,16,128]{2,1,0:T(8,128)S(1)}, f32[2,16,128]{2,1,0:T(8,128)S(1)}, u32[]{:S(2)}, u32[]{:S(2)}) collective-permute-start(f32[2,16,128]{2,1,0:T(8,128)S(1)} %get-tuple-element.69), channel_id=1, source_target_pairs={{0,1},{1,0},{2,3},{3,2},{4,5},{5,4},{6,7},{7,6},{8,9},{9,8},{10,11... | collective-permute-start | bytes 49160 | tf_op jit(solution)/shard_map/ppermute | solution.py:421
  40.9 1.2 %store.1 = bf16[1,2,10,256,256]{4,3,2,1,0:T(8,128)(2,1)} custom-call(s32[4]{0:T(128)S(4)} %get-tuple-element.36.steps, bf16[10,2,256,256]{3,2,1,0:T(8,128)(2,1)S(1)} %get-tuple-element.67.stage, bf16[1,2,10,256,256]{4,3,2,1,0:T(8,128)(2,1)} %get-tuple-element.68.old_out), custom_call_target="tpu_custom_call", output_to_operand_aliasing={{}: (2, {})} | custom-call | tf_op jit(solution)/shard_map/store/pallas_call | solution.py:390
  42.1 0.0 collective-permute-done.7
  42.1 0.6 %slice_add_fusion = f32[2,2,2]{2,1,0:T(2,128)} fusion(f32[2,16,128]{2,1,0:T(8,128)S(1)} %collective-permute-done.7, f32[2,16,128]{2,1,0:T(8,128)S(1)} %get-tuple-element.69), kind=kLoop, calls=%fused_computation | loop fusion | flops 8 | bytes 96 | tf_op jit(solution)/shard_map/add | solution.py:499
Async XLA Ops:
  4.1 3.0 %collective-permute-start = (bf16[4,512,256]{2,1,0:T(8,128)(2,1)S(1)}, bf16[4,512,256]{2,1,0:T(8,128)(2,1)S(1)}, u32[]{:S(2)}, u32[]{:S(2)}) collective-permute-start(bf16[4,512,256]{2,1,0:T(8,128)(2,1)S(1)} %get-tuple-element.39), channel_id=1, source_target_pairs={{0,1},{1,0},{2,3},{3,2},{4,5},{5,4},{6,7},{7,6},{8,9},{9,8},{10,11... | collective-permute-start | bytes 3145736 | tf_op jit(solution)/shard_map/ppermute | solution.py:421
  4.9 12.6 %collective-permute-start.2 = (bf16[784,256]{1,0:T(8,128)(2,1)S(1)}, bf16[784,256]{1,0:T(8,128)(2,1)S(1)}, u32[]{:S(2)}, u32[]{:S(2)}) collective-permute-start(bf16[784,256]{1,0:T(8,128)(2,1)S(1)} %get-tuple-element.48), channel_id=1, source_target_pairs={{0,2},{2,4},{4,6},{6,8},{8,10},{10,12},{12,14},{14,0},{1,3},{3,5},... | collective-permute-start | bytes 1204232 | tf_op jit(solution)/shard_map/ppermute | solution.py:442
  11.2 11.3 %collective-permute-start.1 = (bf16[528,256]{1,0:T(8,128)(2,1)S(1)}, bf16[528,256]{1,0:T(8,128)(2,1)S(1)}, u32[]{:S(2)}, u32[]{:S(2)}) collective-permute-start(bf16[528,256]{1,0:T(8,128)(2,1)S(1)} %get-tuple-element.47), channel_id=1, source_target_pairs={{0,2},{2,4},{4,6},{6,8},{8,10},{10,12},{12,14},{1,3},{3,5},{5,7},{... | collective-permute-start | bytes 811016 | tf_op jit(solution)/shard_map/ppermute | solution.py:452
  14.3 16.6 %collective-permute-start.5 = (bf16[768,256]{1,0:T(8,128)(2,1)S(1)}, bf16[768,256]{1,0:T(8,128)(2,1)S(1)}, u32[]{:S(2)}, u32[]{:S(2)}) collective-permute-start(bf16[768,256]{1,0:T(8,128)(2,1)S(1)} %get-tuple-element.55), channel_id=1, source_target_pairs={{0,2},{2,4},{4,6},{6,8},{8,10},{10,12},{12,14},{1,3},{3,5},{5,7},{... | collective-permute-start | bytes 1179656 | tf_op jit(solution)/shard_map/ppermute | solution.py:452
  17.8 8.3 %collective-permute-start.4 = (bf16[528,256]{1,0:T(8,128)(2,1)S(1)}, bf16[528,256]{1,0:T(8,128)(2,1)S(1)}, u32[]{:S(2)}, u32[]{:S(2)}) collective-permute-start(bf16[528,256]{1,0:T(8,128)(2,1)S(1)} %get-tuple-element.53), channel_id=1, source_target_pairs={{0,1},{1,0},{2,3},{3,2},{4,5},{5,4},{6,7},{7,6},{8,9},{9,8},{10,11... | collective-permute-start | bytes 811016 | tf_op jit(solution)/shard_map/ppermute | solution.py:421
  22.5 3.6 %collective-permute-start.3 = (bf16[528,256]{1,0:T(8,128)(2,1)S(1)}, bf16[528,256]{1,0:T(8,128)(2,1)S(1)}, u32[]{:S(2)}, u32[]{:S(2)}) collective-permute-start(bf16[528,256]{1,0:T(8,128)(2,1)S(1)} %collective-permute-done.1.ours), channel_id=1, source_target_pairs={{0,1},{1,0},{2,3},{3,2},{4,5},{5,4},{6,7},{7,6},{8,9},{9,8},{10,11... | collective-permute-start | bytes 811016 | tf_op jit(solution)/shard_map/ppermute | solution.py:421
  23.7 12.9 %collective-permute-start.6 = (bf16[512,256]{1,0:T(8,128)(2,1)S(1)}, bf16[512,256]{1,0:T(8,128)(2,1)S(1)}, u32[]{:S(2)}, u32[]{:S(2)}) collective-permute-start(bf16[512,256]{1,0:T(8,128)(2,1)S(1)} %get-tuple-element.62), channel_id=1, source_target_pairs={{0,2},{2,4},{4,6},{6,8},{8,10},{10,12},{12,14},{1,3},{3,5},{5,7},{... | collective-permute-start | bytes 786440 | tf_op jit(solution)/shard_map/ppermute | solution.py:452
  40.1 2.0 %collective-permute-start.7 = (f32[2,16,128]{2,1,0:T(8,128)S(1)}, f32[2,16,128]{2,1,0:T(8,128)S(1)}, u32[]{:S(2)}, u32[]{:S(2)}) collective-permute-start(f32[2,16,128]{2,1,0:T(8,128)S(1)} %get-tuple-element.69), channel_id=1, source_target_pairs={{0,1},{1,0},{2,3},{3,2},{4,5},{5,4},{6,7},{7,6},{8,9},{9,8},{10,11... | collective-permute-start | bytes 49160 | tf_op jit(solution)/shard_map/ppermute | solution.py:421

commit v8 on v7

--- a/solution.py
+++ b/solution.py
@@ -212,7 +212,8 @@
 
     def tensors(self, place, source, target, site, lo, hi, sem):
         at = pl.ds(jnp.where(place.core == 0, place.width - hi, lo), hi - lo)
-        self.start((site, lo), source.at[site, :, at], target.at[:, at], sem)
+        for state in range(2):
+            self.start((site, lo, state), source.at[site, state, at], target.at[state, at], sem.at[state])
 
     def wait(self, *keys):
         for key in keys:
@@ -221,7 +222,7 @@
 
 
 def first_kernel(width, run, sources, operators, insert_at, tensors, schmidt,
-                 sent, edge, env, t0, t1, radius, traces, steps, weights, sources_here, operators_here, inserts_here, sems):
+                 sent, edge, env, t0, t1, radius, traces, rows, steps, weights, sources_here, operators_here, inserts_here, sems):
     place = Place(width, steps)
     lo, hi = run
     loads = Loads()
@@ -229,16 +230,16 @@
     loads.start("operators", operators, operators_here, sems.at[1])
     loads.start("insert_at", insert_at, inserts_here, sems.at[2])
     near = hi + HALO
-    loads.tensors(place, tensors, t0, 0, 0, near, sems.at[3])
-    loads.tensors(place, tensors, t1, 1, lo, hi, sems.at[4])
-    loads.start("radius", schmidt, radius, sems.at[5])
+    loads.tensors(place, tensors, t0, 0, 0, near, sems.at[pl.ds(3, 2)])
+    loads.tensors(place, tensors, t1, 1, lo, hi, sems.at[pl.ds(5, 2)])
+    loads.start("radius", schmidt, radius, sems.at[7])
     traces[...] = jnp.zeros_like(traces)
     env[REACH + width :] = jnp.zeros_like(env[REACH + width :])
     loads.wait("sources", "operators", "insert_at")
     fill_steps(place, sources_here, steps)
     fill_weights(operators_here, inserts_here, weights)
     u, v = weights_at(weights, 0), weights_at(weights, 1)
-    loads.wait((0, 0))
+    loads.wait((0, 0, 0), (0, 0, 1))
     for b in range(near):
         blocks = blocks_of(place, t0, b)
         parts = squares(place, blocks, u, b)
@@ -246,21 +247,21 @@
         if b < HALO:
             store_env(edge, HALO - 1 - b, parts)
             edge[2 * HALO - 1 - b] = jnp.concatenate(blocks, axis=0)
-    loads.wait((1, lo), "radius")
-    send_rows(sent, send(place, env, t1, v, traces, radius, sent, run))
+    loads.wait((1, lo, 0), (1, lo, 1), "radius")
+    send_rows(rows, send(place, env, t1, v, traces, radius, sent, run))
 
 
 def second_kernel(width, first_run, runs, steps, weights, tensors, old_env, halo, old_t0, old_t1, radius,
-                  old_traces, *rest):
+                  old_traces, first_rows, *rest):
     env, t0, t1, sents, (traces, sems) = *rest[:3], rest[3:-2], rest[-2:]
     place = Place(width, steps)
     size = t0.shape[-1]
     lo, hi = first_run
     known = hi + HALO
     loads = Loads()
-    loads.tensors(place, tensors, t0, 0, known, width, sems.at[0])
-    loads.tensors(place, tensors, t1, 1, hi, width, sems.at[1])
-    loads.tensors(place, tensors, t1, 1, 0, lo, sems.at[2])
+    loads.tensors(place, tensors, t0, 0, known, width, sems.at[pl.ds(0, 2)])
+    loads.tensors(place, tensors, t1, 1, hi, width, sems.at[pl.ds(2, 2)])
+    loads.tensors(place, tensors, t1, 1, 0, lo, sems.at[pl.ds(4, 2)])
     u, v = weights_at(weights, 0), weights_at(weights, 1)
     traces[...] = old_traces[...]
     for i in range(HALO):
@@ -268,16 +269,16 @@
     for b in range(known):
         parts = [env[REACH + b, k * size : (k + 1) * size] for k in range(2)]
         add_traces(place, traces, 0, 0, b, parts, radius)
-    loads.wait((0, known))
+    loads.wait((0, known, 0), (0, known, 1))
     for b in range(known, width):
         parts = squares(place, blocks_of(place, t0, b), u, b)
         store_env(env, REACH + b, parts)
         add_traces(place, traces, 0, 0, b, parts, radius)
-    loads.wait((1, hi), (1, 0))
+    loads.wait((1, hi, 0), (1, hi, 1), (1, 0, 0), (1, 0, 1))
     rows = []
     for run, sent in zip(runs, sents):
         rows += send(place, env, t1, v, traces, radius, sent, run)
-    send_rows(sents[0], rows)
+    send_rows(sents[0], rows + [first_rows[: hi - lo].astype(F32)])
 
 
 def middle_blocks(place, todo, env, middle, t0, traces, radius, partial=None, known=0):
@@ -290,16 +291,10 @@
         add_traces(place, traces, 2, 0, b, parts, radius)
 
 
-def open_kernel(width, run, steps, first, env, middle, piece):
-    place = Place(width, steps)
-    size = first.shape[1]
+def open_kernel(steps, first, env, middle, piece, width):
     for array in (env, middle):
         array[REACH + width :] = jnp.zeros_like(array[REACH + width :])
-    lo, hi = run
-    for b in range(lo, hi):
-        take(place, first, b - lo, below(first), b - lo, env, REACH + b)
-    piece[: HALO * size] = first[: HALO * size]
-    piece[HALO * size :] = below(first)
+    piece[...] = first[: piece.shape[0]]
 
 
 def final_blocks(place, todo, middle, t1, traces, radius, stage, out, sems, partial=None, known=0):
@@ -317,15 +312,18 @@
     return stores
 
 
-def edge_kernel(width, known, steps, t0, t1, halo, radius, old_traces, old_env, old_middle, ours, near, far,
+def edge_kernel(width, run, steps, t0, t1, halo, radius, old_traces, old_env, old_middle, first, ours, near, far,
                 out, env, middle, traces, partial0, partial1, stage, sems):
     place = Place(width, steps)
+    lo, known = run
     size = t0.shape[-1]
     traces[...] = old_traces[...]
     for i in range(HALO):
         take(place, ours, i, below(ours), i, env, REACH + i)
         take(place, near, i, below(near), i, env, REACH - 1 - i)
-        take(place, far, i, below(far), i, env, REACH - 1 - HALO - i)
+        take(place, far, i, below(near), width - (known - lo) + i, env, REACH - 1 - HALO - i)
+    for b in range(lo, known):
+        take(place, first, b - lo, below(ours), width - known + b, env, REACH + b)
     for i in range(HALO):
         blocks = [halo[HALO + i, state * size : (state + 1) * size] for state in range(2)]
         store_env(middle, REACH - HALO + i, advance(env, slots_of(place, 0, i - HALO), blocks))
@@ -420,23 +418,24 @@
     def across(array):
         return lax.ppermute(array, "sec", swap)
 
-    sent, edge, env, t0, t1, radius, traces, steps, weights = call(
+    sent, edge, env, t0, t1, radius, traces, rows, steps, weights = call(
         functools.partial(first_kernel, width, RUNS[0]),
         "anchor",
         (),
         tuple((a, False) for a in (sources, operators, insert_at, tensors, schmidt)),
         (
-            message(RUNS[0]),
+            message(RUNS[0], 0),
             ((2 * HALO, 2 * size, size), BF16, pltpu.VMEM),
             env_shape,
             tensor_shape,
             tensor_shape,
             radius_shape,
             trace_shape,
+            ((EXTRA, size), BF16, pltpu.VMEM),
             ((4,), jnp.int32, pltpu.SMEM),
             ((2, 4), F32, pltpu.SMEM),
         ),
-        [pltpu.SMEM(a.shape, a.dtype) for a in (sources, operators, insert_at)] + [pltpu.SemaphoreType.DMA((6,))],
+        [pltpu.SMEM(a.shape, a.dtype) for a in (sources, operators, insert_at)] + [pltpu.SemaphoreType.DMA((8,))],
     )
     halo = across(edge)
     got = [lax.ppermute(sent, "site", ring)]
@@ -444,25 +443,25 @@
         functools.partial(second_kernel, width, RUNS[0], RUNS[1:]),
         "anchor_rest",
         (steps, weights),
-        ((tensors, False),) + tuple((a, True) for a in (env, halo, t0, t1, radius, traces)),
+        ((tensors, False),) + tuple((a, True) for a in (env, halo, t0, t1, radius, traces, rows)),
         (env_shape, tensor_shape, tensor_shape) + (message(RUNS[1]), message(RUNS[2], 0), message(RUNS[3], 0)) + (trace_shape,),
-        [pltpu.SemaphoreType.DMA((3,))],
+        [pltpu.SemaphoreType.DMA((6,))],
         {3: 0, 5: 1, 6: 2},
     )
     got += [lax.ppermute(s, "site", ring[:-1]) for s in sents]
     env, middle, piece = call(
-        functools.partial(open_kernel, width, RUNS[0]),
+        functools.partial(open_kernel, width=width),
         "first_run",
         (steps,),
         ((got[0], True),),
-        (env_shape, env_shape, message(RUNS[1])),
+        (env_shape, env_shape, message(RUNS[1], 0)),
     )
     ours, env = lax.optimization_barrier((got[1], env))
     final, env, middle, traces, *partials = call(
-        functools.partial(edge_kernel, width, RUNS[0][1]),
+        functools.partial(edge_kernel, width, RUNS[0]),
         "edge",
         (steps,),
-        tuple((a, True) for a in (t0, t1, halo, radius, traces, env, middle, ours, across(ours), across(piece))),
+        tuple((a, True) for a in (t0, t1, halo, radius, traces, env, middle, got[0], ours, across(ours), across(piece))),
         (out_shape, env_shape, env_shape, trace_shape, partial_shape, partial_shape),
         stage,
         {6: 1, 7: 2},

time: 43 us -> 42.8 us (level)
    ppermute x4, starting transfers between devices: 3.7 us -> 3.23 us  [across(): return lax.ppermute(array, 'sec', swap)]
where the time goes in v8:
time: 42.8 us; the launch traced here: 42.5 us
  Pallas kernels  19.1 us (45%)
  starting transfers between devices  13.2 us (31%)
  waiting for transfers between devices  8.84 us (21%)
  between operations  0.74 us (2%)
  other arithmetic  0.58 us (1%)
    pallas_call x7, Pallas kernels, call(): pl.pallas_call(kernel, out_shape=tuple((memory(s, d) for s, d, memory in...  19.1 us
    ppermute x3, starting transfers between devices, shards(): got += [lax.ppermute(s, 'site', ring[:-1]) for s in sents]  8.71 us
    ppermute x3, waiting for transfers between devices, shards(): got += [lax.ppermute(s, 'site', ring[:-1]) for s in sents]  7.78 us
    ppermute x4, starting transfers between devices, across(): return lax.ppermute(array, 'sec', swap)  3.23 us
    ppermute x1, starting transfers between devices, shards(): got = [lax.ppermute(sent, 'site', ring)]  1.24 us
    ppermute x4, waiting for transfers between devices, across(): return lax.ppermute(array, 'sec', swap)  1.05 us
  transfers between devices with their start and end apart: 8, of which 4 were waited for; matrix products, arithmetic and copies ran while one was open for 0% of the time, Pallas kernels for 29%

profile of v8, /device:TPU:17, one launch (start us, length us, event | category | flops | bytes accessed | tf_op | source)
XLA Modules:
  0.0 42.5 jit_solution(5953884057120521422)
XLA Ops:
  0.6 3.5 %anchor.1 = (bf16[768,256]{1,0:T(8,128)(2,1)S(1)}, bf16[4,512,256]{2,1,0:T(8,128)(2,1)S(1)}, bf16[16,512,256]{2,1,0:T(8,128)(2,1)S(1)}, bf16[2,10,256,256]{3,2,1...) custom-call(s32[16,2,20]{2,1,0:T(2,128)} %sources.1, ...), custom_call_target="tpu_custom_call" | custom-call | tf_op jit(solution)/shard_map/anchor/pallas_call | solution.py:388
  4.1 0.7 %collective-permute-start = (bf16[4,512,256]{2,1,0:T(8,128)(2,1)S(1)}, bf16[4,512,256]{2,1,0:T(8,128)(2,1)S(1)}, u32[]{:S(2)}, u32[]{:S(2)}) collective-permute-start(bf16[4,512,256]{2,1,0:T(8,128)(2,1)S(1)} %get-tuple-element.40), channel_id=1, source_target_pairs={{0,1},{1,0},{2,3},{3,2},{4,5},{5,4},{6,7},{7,6},{8,9},{9,8},{10,11... | collective-permute-start | bytes 3145736 | tf_op jit(solution)/shard_map/ppermute | solution.py:419
  4.8 1.2 %collective-permute-start.2 = (bf16[768,256]{1,0:T(8,128)(2,1)S(1)}, bf16[768,256]{1,0:T(8,128)(2,1)S(1)}, u32[]{:S(2)}, u32[]{:S(2)}) collective-permute-start(bf16[768,256]{1,0:T(8,128)(2,1)S(1)} %get-tuple-element.50), channel_id=1, source_target_pairs={{0,2},{2,4},{4,6},{6,8},{8,10},{10,12},{12,14},{14,0},{1,3},{3,5},... | collective-permute-start | bytes 1179656 | tf_op jit(solution)/shard_map/ppermute | solution.py:441
  6.1 1.0 %collective-permute-done.halo = bf16[4,512,256]{2,1,0:T(8,128)(2,1)S(1)} collective-permute-done((bf16[4,512,256]{2,1,0:T(8,128)(2,1)S(1)}, bf16[4,512,256]{2,1,0:T(8,128)(2,1)S(1)}, u32[]{:S(2)}, u32[]{:S(2)}) %collective-permute-start) | collective-permute-done | bytes 1048608 | tf_op jit(solution)/shard_map/ppermute | solution.py:419
  7.1 4.0 %anchor_rest.1 = (bf16[16,512,256]{2,1,0:T(8,128)(2,1)S(1)}, bf16[2,10,256,256]{3,2,1,0:T(8,128)(2,1)S(1)}, bf16[2,10,256,256]{3,2,1,0:T(8,128)(2,1)S(1)}, bf16[...) custom-call(s32[4]{0:T(128)S(4)} %get-tuple-element.37.steps, ...), custom_call_target="tpu_custom_call", output_to_operand_aliasing={{0}: (3, {}), {1}: (5, {}), {2}: (6, {})} | custom-call | tf_op jit(solution)/shard_map/anchor_rest/pallas_call | solution.py:388
  11.1 3.2 %collective-permute-start.1 = (bf16[528,256]{1,0:T(8,128)(2,1)S(1)}, bf16[528,256]{1,0:T(8,128)(2,1)S(1)}, u32[]{:S(2)}, u32[]{:S(2)}) collective-permute-start(bf16[528,256]{1,0:T(8,128)(2,1)S(1)} %get-tuple-element.49), channel_id=1, source_target_pairs={{0,2},{2,4},{4,6},{6,8},{8,10},{10,12},{12,14},{1,3},{3,5},{5,7},{... | collective-permute-start | bytes 811016 | tf_op jit(solution)/shard_map/ppermute | solution.py:451
  14.3 3.1 %collective-permute-start.5 = (bf16[768,256]{1,0:T(8,128)(2,1)S(1)}, bf16[768,256]{1,0:T(8,128)(2,1)S(1)}, u32[]{:S(2)}, u32[]{:S(2)}) collective-permute-start(bf16[768,256]{1,0:T(8,128)(2,1)S(1)} %get-tuple-element.57), channel_id=1, source_target_pairs={{0,2},{2,4},{4,6},{6,8},{8,10},{10,12},{12,14},{1,3},{3,5},{5,7},{... | collective-permute-start | bytes 1179656 | tf_op jit(solution)/shard_map/ppermute | solution.py:451
  17.4 0.0 collective-permute-done.2.first
  17.4 0.1 first_run.1
  17.5 4.6 %collective-permute-done.1.ours = bf16[528,256]{1,0:T(8,128)(2,1)S(1)} collective-permute-done((bf16[528,256]{1,0:T(8,128)(2,1)S(1)}, bf16[528,256]{1,0:T(8,128)(2,1)S(1)}, u32[]{:S(2)}, u32[]{:S(2)}) %collective-permute-start.1) | collective-permute-done | bytes 270368 | tf_op jit(solution)/shard_map/ppermute | solution.py:451
  22.1 1.5 %collective-permute-start.3 = (bf16[528,256]{1,0:T(8,128)(2,1)S(1)}, bf16[528,256]{1,0:T(8,128)(2,1)S(1)}, u32[]{:S(2)}, u32[]{:S(2)}) collective-permute-start(bf16[528,256]{1,0:T(8,128)(2,1)S(1)} %collective-permute-done.1.ours), channel_id=1, source_target_pairs={{0,1},{1,0},{2,3},{3,2},{4,5},{5,4},{6,7},{7,6},{8,9},{9,8},{10,11... | collective-permute-start | bytes 811016 | tf_op jit(solution)/shard_map/ppermute | solution.py:419
  23.6 0.0 collective-permute-start.4
  23.6 2.4 %collective-permute-start.6 = (bf16[512,256]{1,0:T(8,128)(2,1)S(1)}, bf16[512,256]{1,0:T(8,128)(2,1)S(1)}, u32[]{:S(2)}, u32[]{:S(2)}) collective-permute-start(bf16[512,256]{1,0:T(8,128)(2,1)S(1)} %get-tuple-element.64), channel_id=1, source_target_pairs={{0,2},{2,4},{4,6},{6,8},{8,10},{10,12},{12,14},{1,3},{3,5},{5,7},{... | collective-permute-start | bytes 786440 | tf_op jit(solution)/shard_map/ppermute | solution.py:451
  26.1 0.0 collective-permute-done.4.far
  26.1 0.0 collective-permute-done.3.near
  26.1 3.7 %edge.1 = (bf16[1,2,10,256,256]{4,3,2,1,0:T(8,128)(2,1)}, bf16[16,512,256]{2,1,0:T(8,128)(2,1)S(1)}, bf16[16,512,256]{2,1,0:T(8,128)(2,1)S(1)}, f32[8,256]{1,0:T...) custom-call(s32[4]{0:T(128)S(4)} %get-tuple-element.37.steps, ...), custom_call_target="tpu_custom_call", output_to_operand_aliasing={{1}: (6, {}), {2}: (7, {})} | custom-call | tf_op jit(solution)/shard_map/edge/pallas_call | solution.py:388
  29.8 0.7 %collective-permute-done.5.buffer = bf16[768,256]{1,0:T(8,128)(2,1)S(1)} collective-permute-done((bf16[768,256]{1,0:T(8,128)(2,1)S(1)}, bf16[768,256]{1,0:T(8,128)(2,1)S(1)}, u32[]{:S(2)}, u32[]{:S(2)}) %collective-permute-start.5) | collective-permute-done | bytes 393248 | tf_op jit(solution)/shard_map/ppermute | solution.py:451
  30.5 3.1 %third_run.1 = (bf16[1,2,10,256,256]{4,3,2,1,0:T(8,128)(2,1)}, bf16[16,512,256]{2,1,0:T(8,128)(2,1)S(1)}, bf16[16,512,256]{2,1,0:T(8,128)(2,1)S(1)}, f32[8,256]{...) custom-call(s32[4]{0:T(128)S(4)} %get-tuple-element.37.steps, ...), custom_call_target="tpu_custom_call", output_to_operand_aliasing={{1}: (9, {}), {2}: (10, {}), {0}: (11, {})} | custom-call | tf_op jit(solution)/shard_map/third_run/pallas_call | solution.py:388
  33.7 2.5 %collective-permute-done.6.buffer = bf16[512,256]{1,0:T(8,128)(2,1)S(1)} collective-permute-done((bf16[512,256]{1,0:T(8,128)(2,1)S(1)}, bf16[512,256]{1,0:T(8,128)(2,1)S(1)}, u32[]{:S(2)}, u32[]{:S(2)}) %collective-permute-start.6) | collective-permute-done | bytes 262176 | tf_op jit(solution)/shard_map/ppermute | solution.py:451
  36.1 3.6 %last_run.1 = (bf16[16,512,256]{2,1,0:T(8,128)(2,1)S(1)}, bf16[16,512,256]{2,1,0:T(8,128)(2,1)S(1)}, f32[8,256]{1,0:T(8,128)}, f32[2,16,128]{2,1,0:T(8,128)S(1)}, bf16[10,2,256,256]{3,2,1,0:T(8,128)(2,1)S(1)}) custom-call(s32[4]{0:T(128)S(4)} %get-tuple-element.37.steps, ...), custom_call_target="tpu_custom_call", output_to_operand_aliasing={{0}: (9, {}), {1}: (10, {})} | custom-call | tf_op jit(solution)/shard_map/last_run/pallas_call | solution.py:388
  39.7 1.0 %collective-permute-start.7 = (f32[2,16,128]{2,1,0:T(8,128)S(1)}, f32[2,16,128]{2,1,0:T(8,128)S(1)}, u32[]{:S(2)}, u32[]{:S(2)}) collective-permute-start(f32[2,16,128]{2,1,0:T(8,128)S(1)} %get-tuple-element.71), channel_id=1, source_target_pairs={{0,1},{1,0},{2,3},{3,2},{4,5},{5,4},{6,7},{7,6},{8,9},{9,8},{10,11... | collective-permute-start | bytes 49160 | tf_op jit(solution)/shard_map/ppermute | solution.py:419
  40.7 1.2 %store.1 = bf16[1,2,10,256,256]{4,3,2,1,0:T(8,128)(2,1)} custom-call(s32[4]{0:T(128)S(4)} %get-tuple-element.37.steps, bf16[10,2,256,256]{3,2,1,0:T(8,128)(2,1)S(1)} %get-tuple-element.69.stage, bf16[1,2,10,256,256]{4,3,2,1,0:T(8,128)(2,1)} %get-tuple-element.70.old_out), custom_call_target="tpu_custom_call", output_to_operand_aliasing={{}: (2, {})} | custom-call | tf_op jit(solution)/shard_map/store/pallas_call | solution.py:388
  41.9 0.0 collective-permute-done.7
  41.9 0.6 %slice_add_fusion = f32[2,2,2]{2,1,0:T(2,128)} fusion(f32[2,16,128]{2,1,0:T(8,128)S(1)} %collective-permute-done.7, f32[2,16,128]{2,1,0:T(8,128)S(1)} %get-tuple-element.71), kind=kLoop, calls=%fused_computation | loop fusion | flops 8 | bytes 96 | tf_op jit(solution)/shard_map/add | solution.py:498
Async XLA Ops:
  4.1 3.0 %collective-permute-start = (bf16[4,512,256]{2,1,0:T(8,128)(2,1)S(1)}, bf16[4,512,256]{2,1,0:T(8,128)(2,1)S(1)}, u32[]{:S(2)}, u32[]{:S(2)}) collective-permute-start(bf16[4,512,256]{2,1,0:T(8,128)(2,1)S(1)} %get-tuple-element.40), channel_id=1, source_target_pairs={{0,1},{1,0},{2,3},{3,2},{4,5},{5,4},{6,7},{7,6},{8,9},{9,8},{10,11... | collective-permute-start | bytes 3145736 | tf_op jit(solution)/shard_map/ppermute | solution.py:419
  4.8 12.6 %collective-permute-start.2 = (bf16[768,256]{1,0:T(8,128)(2,1)S(1)}, bf16[768,256]{1,0:T(8,128)(2,1)S(1)}, u32[]{:S(2)}, u32[]{:S(2)}) collective-permute-start(bf16[768,256]{1,0:T(8,128)(2,1)S(1)} %get-tuple-element.50), channel_id=1, source_target_pairs={{0,2},{2,4},{4,6},{6,8},{8,10},{10,12},{12,14},{14,0},{1,3},{3,5},... | collective-permute-start | bytes 1179656 | tf_op jit(solution)/shard_map/ppermute | solution.py:441
  11.1 11.0 %collective-permute-start.1 = (bf16[528,256]{1,0:T(8,128)(2,1)S(1)}, bf16[528,256]{1,0:T(8,128)(2,1)S(1)}, u32[]{:S(2)}, u32[]{:S(2)}) collective-permute-start(bf16[528,256]{1,0:T(8,128)(2,1)S(1)} %get-tuple-element.49), channel_id=1, source_target_pairs={{0,2},{2,4},{4,6},{6,8},{8,10},{10,12},{12,14},{1,3},{3,5},{5,7},{... | collective-permute-start | bytes 811016 | tf_op jit(solution)/shard_map/ppermute | solution.py:451
  14.3 16.2 %collective-permute-start.5 = (bf16[768,256]{1,0:T(8,128)(2,1)S(1)}, bf16[768,256]{1,0:T(8,128)(2,1)S(1)}, u32[]{:S(2)}, u32[]{:S(2)}) collective-permute-start(bf16[768,256]{1,0:T(8,128)(2,1)S(1)} %get-tuple-element.57), channel_id=1, source_target_pairs={{0,2},{2,4},{4,6},{6,8},{8,10},{10,12},{12,14},{1,3},{3,5},{5,7},{... | collective-permute-start | bytes 1179656 | tf_op jit(solution)/shard_map/ppermute | solution.py:451
  22.1 4.0 %collective-permute-start.3 = (bf16[528,256]{1,0:T(8,128)(2,1)S(1)}, bf16[528,256]{1,0:T(8,128)(2,1)S(1)}, u32[]{:S(2)}, u32[]{:S(2)}) collective-permute-start(bf16[528,256]{1,0:T(8,128)(2,1)S(1)} %collective-permute-done.1.ours), channel_id=1, source_target_pairs={{0,1},{1,0},{2,3},{3,2},{4,5},{5,4},{6,7},{7,6},{8,9},{9,8},{10,11... | collective-permute-start | bytes 811016 | tf_op jit(solution)/shard_map/ppermute | solution.py:419
  23.6 2.4 %collective-permute-start.4 = (bf16[512,256]{1,0:T(8,128)(2,1)S(1)}, bf16[512,256]{1,0:T(8,128)(2,1)S(1)}, u32[]{:S(2)}, u32[]{:S(2)}) collective-permute-start(bf16[512,256]{1,0:T(8,128)(2,1)S(1)} %get-tuple-element.55), channel_id=1, source_target_pairs={{0,1},{1,0},{2,3},{3,2},{4,5},{5,4},{6,7},{7,6},{8,9},{9,8},{10,11... | collective-permute-start | bytes 786440 | tf_op jit(solution)/shard_map/ppermute | solution.py:419
  23.6 12.5 %collective-permute-start.6 = (bf16[512,256]{1,0:T(8,128)(2,1)S(1)}, bf16[512,256]{1,0:T(8,128)(2,1)S(1)}, u32[]{:S(2)}, u32[]{:S(2)}) collective-permute-start(bf16[512,256]{1,0:T(8,128)(2,1)S(1)} %get-tuple-element.64), channel_id=1, source_target_pairs={{0,2},{2,4},{4,6},{6,8},{8,10},{10,12},{12,14},{1,3},{3,5},{5,7},{... | collective-permute-start | bytes 786440 | tf_op jit(solution)/shard_map/ppermute | solution.py:451
  39.7 2.2 %collective-permute-start.7 = (f32[2,16,128]{2,1,0:T(8,128)S(1)}, f32[2,16,128]{2,1,0:T(8,128)S(1)}, u32[]{:S(2)}, u32[]{:S(2)}) collective-permute-start(f32[2,16,128]{2,1,0:T(8,128)S(1)} %get-tuple-element.71), channel_id=1, source_target_pairs={{0,1},{1,0},{2,3},{3,2},{4,5},{5,4},{6,7},{7,6},{8,9},{9,8},{10,11... | collective-permute-start | bytes 49160 | tf_op jit(solution)/shard_map/ppermute | solution.py:419

commit v9 on v8

--- a/solution.py
+++ b/solution.py
@@ -305,7 +305,10 @@
         else:
             parts = advance(middle, slots_of(place, 1, b), blocks_of(place, t1, b))
         for k in range(2):
-            stage[b, k] = parts[k].astype(BF16)
+            if out is None:
+                stage[k, place.local(b)] = parts[k].astype(BF16)
+            else:
+                stage[b, k] = parts[k].astype(BF16)
         if out is not None:
             stores.start(b, stage.at[b], out.at[0, :, place.local(b)], sems.at[b])
         add_traces(place, traces, 6, 1, b, parts, radius)
@@ -368,10 +371,12 @@
 
 def store_kernel(width, todo, steps, stage, old_out, out, sems):
     place = Place(width, steps)
+    lo, hi = todo
+    at = pl.ds(jnp.where(place.core == 0, width - hi, lo), hi - lo)
     stores = Loads()
-    for b in range(*todo):
-        stores.start(b, stage.at[b], out.at[0, :, place.local(b)], sems.at[b])
-    stores.wait(*range(*todo))
+    for k in range(2):
+        stores.start(k, stage.at[k, at], out.at[0, k, at], sems.at[k])
+    stores.wait(0, 1)
 
 
 SMEM = pl.BlockSpec(memory_space=pltpu.SMEM)
@@ -482,7 +487,7 @@
         "last_run",
         (steps,),
         tuple((a, True) for a in (t0, t1, radius, traces, ours, got[3], *partials, env, middle)),
-        (env_shape, env_shape, trace_shape, ((2, 16, 128), F32, pltpu.VMEM), ((width, 2, size, size), BF16, pltpu.VMEM)),
+        (env_shape, env_shape, trace_shape, ((2, 16, 128), F32, pltpu.VMEM), ((2, width, size, size), BF16, pltpu.VMEM)),
         aliases={9: 0, 10: 1},
     )
     others = across(totals)

time: 42.8 us -> 42.8 us (level)
  no operation moved by 1% of the time
where the time goes in v9:
time: 42.8 us; the launch traced here: 42.5 us
  Pallas kernels  19.2 us (45%)
  starting transfers between devices  13.2 us (31%)
  waiting for transfers between devices  8.84 us (21%)
  between operations  0.74 us (2%)
  other arithmetic  0.58 us (1%)
    pallas_call x7, Pallas kernels, call(): pl.pallas_call(kernel, out_shape=tuple((memory(s, d) for s, d, memory in...  19.2 us
    ppermute x3, starting transfers between devices, shards(): got += [lax.ppermute(s, 'site', ring[:-1]) for s in sents]  8.71 us
    ppermute x3, waiting for transfers between devices, shards(): got += [lax.ppermute(s, 'site', ring[:-1]) for s in sents]  7.78 us
    ppermute x4, starting transfers between devices, across(): return lax.ppermute(array, 'sec', swap)  3.23 us
    ppermute x1, starting transfers between devices, shards(): got = [lax.ppermute(sent, 'site', ring)]  1.24 us
    ppermute x4, waiting for transfers between devices, across(): return lax.ppermute(array, 'sec', swap)  1.05 us
  transfers between devices with their start and end apart: 8, of which 4 were waited for; matrix products, arithmetic and copies ran while one was open for 0% of the time, Pallas kernels for 29%

profile of v9, /device:TPU:17, one launch (start us, length us, event | category | flops | bytes accessed | tf_op | source)
XLA Modules:
  0.0 42.5 jit_solution(8593736482175561789)
XLA Ops:
  0.6 3.5 %anchor.1 = (bf16[768,256]{1,0:T(8,128)(2,1)S(1)}, bf16[4,512,256]{2,1,0:T(8,128)(2,1)S(1)}, bf16[16,512,256]{2,1,0:T(8,128)(2,1)S(1)}, bf16[2,10,256,256]{3,2,1...) custom-call(s32[16,2,20]{2,1,0:T(2,128)} %sources.1, ...), custom_call_target="tpu_custom_call" | custom-call | tf_op jit(solution)/shard_map/anchor/pallas_call | solution.py:393
  4.1 0.7 %collective-permute-start = (bf16[4,512,256]{2,1,0:T(8,128)(2,1)S(1)}, bf16[4,512,256]{2,1,0:T(8,128)(2,1)S(1)}, u32[]{:S(2)}, u32[]{:S(2)}) collective-permute-start(bf16[4,512,256]{2,1,0:T(8,128)(2,1)S(1)} %get-tuple-element.40), channel_id=1, source_target_pairs={{0,1},{1,0},{2,3},{3,2},{4,5},{5,4},{6,7},{7,6},{8,9},{9,8},{10,11... | collective-permute-start | bytes 3145736 | tf_op jit(solution)/shard_map/ppermute | solution.py:424
  4.8 1.2 %collective-permute-start.2 = (bf16[768,256]{1,0:T(8,128)(2,1)S(1)}, bf16[768,256]{1,0:T(8,128)(2,1)S(1)}, u32[]{:S(2)}, u32[]{:S(2)}) collective-permute-start(bf16[768,256]{1,0:T(8,128)(2,1)S(1)} %get-tuple-element.50), channel_id=1, source_target_pairs={{0,2},{2,4},{4,6},{6,8},{8,10},{10,12},{12,14},{14,0},{1,3},{3,5},... | collective-permute-start | bytes 1179656 | tf_op jit(solution)/shard_map/ppermute | solution.py:446
  6.1 1.0 %collective-permute-done.halo = bf16[4,512,256]{2,1,0:T(8,128)(2,1)S(1)} collective-permute-done((bf16[4,512,256]{2,1,0:T(8,128)(2,1)S(1)}, bf16[4,512,256]{2,1,0:T(8,128)(2,1)S(1)}, u32[]{:S(2)}, u32[]{:S(2)}) %collective-permute-start) | collective-permute-done | bytes 1048608 | tf_op jit(solution)/shard_map/ppermute | solution.py:424
  7.1 4.0 %anchor_rest.1 = (bf16[16,512,256]{2,1,0:T(8,128)(2,1)S(1)}, bf16[2,10,256,256]{3,2,1,0:T(8,128)(2,1)S(1)}, bf16[2,10,256,256]{3,2,1,0:T(8,128)(2,1)S(1)}, bf16[...) custom-call(s32[4]{0:T(128)S(4)} %get-tuple-element.37.steps, ...), custom_call_target="tpu_custom_call", output_to_operand_aliasing={{0}: (3, {}), {1}: (5, {}), {2}: (6, {})} | custom-call | tf_op jit(solution)/shard_map/anchor_rest/pallas_call | solution.py:393
  11.1 3.2 %collective-permute-start.1 = (bf16[528,256]{1,0:T(8,128)(2,1)S(1)}, bf16[528,256]{1,0:T(8,128)(2,1)S(1)}, u32[]{:S(2)}, u32[]{:S(2)}) collective-permute-start(bf16[528,256]{1,0:T(8,128)(2,1)S(1)} %get-tuple-element.49), channel_id=1, source_target_pairs={{0,2},{2,4},{4,6},{6,8},{8,10},{10,12},{12,14},{1,3},{3,5},{5,7},{... | collective-permute-start | bytes 811016 | tf_op jit(solution)/shard_map/ppermute | solution.py:456
  14.3 3.1 %collective-permute-start.5 = (bf16[768,256]{1,0:T(8,128)(2,1)S(1)}, bf16[768,256]{1,0:T(8,128)(2,1)S(1)}, u32[]{:S(2)}, u32[]{:S(2)}) collective-permute-start(bf16[768,256]{1,0:T(8,128)(2,1)S(1)} %get-tuple-element.57), channel_id=1, source_target_pairs={{0,2},{2,4},{4,6},{6,8},{8,10},{10,12},{12,14},{1,3},{3,5},{5,7},{... | collective-permute-start | bytes 1179656 | tf_op jit(solution)/shard_map/ppermute | solution.py:456
  17.4 0.0 collective-permute-done.2.first
  17.4 0.1 first_run.1
  17.5 4.6 %collective-permute-done.1.ours = bf16[528,256]{1,0:T(8,128)(2,1)S(1)} collective-permute-done((bf16[528,256]{1,0:T(8,128)(2,1)S(1)}, bf16[528,256]{1,0:T(8,128)(2,1)S(1)}, u32[]{:S(2)}, u32[]{:S(2)}) %collective-permute-start.1) | collective-permute-done | bytes 270368 | tf_op jit(solution)/shard_map/ppermute | solution.py:456
  22.1 1.5 %collective-permute-start.3 = (bf16[528,256]{1,0:T(8,128)(2,1)S(1)}, bf16[528,256]{1,0:T(8,128)(2,1)S(1)}, u32[]{:S(2)}, u32[]{:S(2)}) collective-permute-start(bf16[528,256]{1,0:T(8,128)(2,1)S(1)} %collective-permute-done.1.ours), channel_id=1, source_target_pairs={{0,1},{1,0},{2,3},{3,2},{4,5},{5,4},{6,7},{7,6},{8,9},{9,8},{10,11... | collective-permute-start | bytes 811016 | tf_op jit(solution)/shard_map/ppermute | solution.py:424
  23.6 0.0 collective-permute-start.4
  23.6 2.4 %collective-permute-start.6 = (bf16[512,256]{1,0:T(8,128)(2,1)S(1)}, bf16[512,256]{1,0:T(8,128)(2,1)S(1)}, u32[]{:S(2)}, u32[]{:S(2)}) collective-permute-start(bf16[512,256]{1,0:T(8,128)(2,1)S(1)} %get-tuple-element.64), channel_id=1, source_target_pairs={{0,2},{2,4},{4,6},{6,8},{8,10},{10,12},{12,14},{1,3},{3,5},{5,7},{... | collective-permute-start | bytes 786440 | tf_op jit(solution)/shard_map/ppermute | solution.py:456
  26.1 0.0 collective-permute-done.4.far
  26.1 0.0 collective-permute-done.3.near
  26.1 3.7 %edge.1 = (bf16[1,2,10,256,256]{4,3,2,1,0:T(8,128)(2,1)}, bf16[16,512,256]{2,1,0:T(8,128)(2,1)S(1)}, bf16[16,512,256]{2,1,0:T(8,128)(2,1)S(1)}, f32[8,256]{1,0:T...) custom-call(s32[4]{0:T(128)S(4)} %get-tuple-element.37.steps, ...), custom_call_target="tpu_custom_call", output_to_operand_aliasing={{1}: (6, {}), {2}: (7, {})} | custom-call | tf_op jit(solution)/shard_map/edge/pallas_call | solution.py:393
  29.8 0.7 %collective-permute-done.5.buffer = bf16[768,256]{1,0:T(8,128)(2,1)S(1)} collective-permute-done((bf16[768,256]{1,0:T(8,128)(2,1)S(1)}, bf16[768,256]{1,0:T(8,128)(2,1)S(1)}, u32[]{:S(2)}, u32[]{:S(2)}) %collective-permute-start.5) | collective-permute-done | bytes 393248 | tf_op jit(solution)/shard_map/ppermute | solution.py:456
  30.5 3.1 %third_run.1 = (bf16[1,2,10,256,256]{4,3,2,1,0:T(8,128)(2,1)}, bf16[16,512,256]{2,1,0:T(8,128)(2,1)S(1)}, bf16[16,512,256]{2,1,0:T(8,128)(2,1)S(1)}, f32[8,256]{...) custom-call(s32[4]{0:T(128)S(4)} %get-tuple-element.37.steps, ...), custom_call_target="tpu_custom_call", output_to_operand_aliasing={{1}: (9, {}), {2}: (10, {}), {0}: (11, {})} | custom-call | tf_op jit(solution)/shard_map/third_run/pallas_call | solution.py:393
  33.7 2.5 %collective-permute-done.6.buffer = bf16[512,256]{1,0:T(8,128)(2,1)S(1)} collective-permute-done((bf16[512,256]{1,0:T(8,128)(2,1)S(1)}, bf16[512,256]{1,0:T(8,128)(2,1)S(1)}, u32[]{:S(2)}, u32[]{:S(2)}) %collective-permute-start.6) | collective-permute-done | bytes 262176 | tf_op jit(solution)/shard_map/ppermute | solution.py:456
  36.1 3.6 %last_run.1 = (bf16[16,512,256]{2,1,0:T(8,128)(2,1)S(1)}, bf16[16,512,256]{2,1,0:T(8,128)(2,1)S(1)}, f32[8,256]{1,0:T(8,128)}, f32[2,16,128]{2,1,0:T(8,128)S(1)}, bf16[2,10,256,256]{3,2,1,0:T(8,128)(2,1)S(1)}) custom-call(s32[4]{0:T(128)S(4)} %get-tuple-element.37.steps, ...), custom_call_target="tpu_custom_call", output_to_operand_aliasing={{0}: (9, {}), {1}: (10, {})} | custom-call | tf_op jit(solution)/shard_map/last_run/pallas_call | solution.py:393
  39.7 1.0 %collective-permute-start.7 = (f32[2,16,128]{2,1,0:T(8,128)S(1)}, f32[2,16,128]{2,1,0:T(8,128)S(1)}, u32[]{:S(2)}, u32[]{:S(2)}) collective-permute-start(f32[2,16,128]{2,1,0:T(8,128)S(1)} %get-tuple-element.71), channel_id=1, source_target_pairs={{0,1},{1,0},{2,3},{3,2},{4,5},{5,4},{6,7},{7,6},{8,9},{9,8},{10,11... | collective-permute-start | bytes 49160 | tf_op jit(solution)/shard_map/ppermute | solution.py:424
  40.7 1.2 %store.1 = bf16[1,2,10,256,256]{4,3,2,1,0:T(8,128)(2,1)} custom-call(s32[4]{0:T(128)S(4)} %get-tuple-element.37.steps, bf16[2,10,256,256]{3,2,1,0:T(8,128)(2,1)S(1)} %get-tuple-element.69.stage, bf16[1,2,10,256,256]{4,3,2,1,0:T(8,128)(2,1)} %get-tuple-element.70.old_out), custom_call_target="tpu_custom_call", output_to_operand_aliasing={{}: (2, {})} | custom-call | tf_op jit(solution)/shard_map/store/pallas_call | solution.py:393
  41.9 0.0 collective-permute-done.7
  41.9 0.6 %slice_add_fusion = f32[2,2,2]{2,1,0:T(2,128)} fusion(f32[2,16,128]{2,1,0:T(8,128)S(1)} %collective-permute-done.7, f32[2,16,128]{2,1,0:T(8,128)S(1)} %get-tuple-element.71), kind=kLoop, calls=%fused_computation | loop fusion | flops 8 | bytes 96 | tf_op jit(solution)/shard_map/add | solution.py:503
Async XLA Ops:
  4.1 3.0 %collective-permute-start = (bf16[4,512,256]{2,1,0:T(8,128)(2,1)S(1)}, bf16[4,512,256]{2,1,0:T(8,128)(2,1)S(1)}, u32[]{:S(2)}, u32[]{:S(2)}) collective-permute-start(bf16[4,512,256]{2,1,0:T(8,128)(2,1)S(1)} %get-tuple-element.40), channel_id=1, source_target_pairs={{0,1},{1,0},{2,3},{3,2},{4,5},{5,4},{6,7},{7,6},{8,9},{9,8},{10,11... | collective-permute-start | bytes 3145736 | tf_op jit(solution)/shard_map/ppermute | solution.py:424
  4.8 12.6 %collective-permute-start.2 = (bf16[768,256]{1,0:T(8,128)(2,1)S(1)}, bf16[768,256]{1,0:T(8,128)(2,1)S(1)}, u32[]{:S(2)}, u32[]{:S(2)}) collective-permute-start(bf16[768,256]{1,0:T(8,128)(2,1)S(1)} %get-tuple-element.50), channel_id=1, source_target_pairs={{0,2},{2,4},{4,6},{6,8},{8,10},{10,12},{12,14},{14,0},{1,3},{3,5},... | collective-permute-start | bytes 1179656 | tf_op jit(solution)/shard_map/ppermute | solution.py:446
  11.1 11.0 %collective-permute-start.1 = (bf16[528,256]{1,0:T(8,128)(2,1)S(1)}, bf16[528,256]{1,0:T(8,128)(2,1)S(1)}, u32[]{:S(2)}, u32[]{:S(2)}) collective-permute-start(bf16[528,256]{1,0:T(8,128)(2,1)S(1)} %get-tuple-element.49), channel_id=1, source_target_pairs={{0,2},{2,4},{4,6},{6,8},{8,10},{10,12},{12,14},{1,3},{3,5},{5,7},{... | collective-permute-start | bytes 811016 | tf_op jit(solution)/shard_map/ppermute | solution.py:456
  14.3 16.2 %collective-permute-start.5 = (bf16[768,256]{1,0:T(8,128)(2,1)S(1)}, bf16[768,256]{1,0:T(8,128)(2,1)S(1)}, u32[]{:S(2)}, u32[]{:S(2)}) collective-permute-start(bf16[768,256]{1,0:T(8,128)(2,1)S(1)} %get-tuple-element.57), channel_id=1, source_target_pairs={{0,2},{2,4},{4,6},{6,8},{8,10},{10,12},{12,14},{1,3},{3,5},{5,7},{... | collective-permute-start | bytes 1179656 | tf_op jit(solution)/shard_map/ppermute | solution.py:456
  22.1 4.0 %collective-permute-start.3 = (bf16[528,256]{1,0:T(8,128)(2,1)S(1)}, bf16[528,256]{1,0:T(8,128)(2,1)S(1)}, u32[]{:S(2)}, u32[]{:S(2)}) collective-permute-start(bf16[528,256]{1,0:T(8,128)(2,1)S(1)} %collective-permute-done.1.ours), channel_id=1, source_target_pairs={{0,1},{1,0},{2,3},{3,2},{4,5},{5,4},{6,7},{7,6},{8,9},{9,8},{10,11... | collective-permute-start | bytes 811016 | tf_op jit(solution)/shard_map/ppermute | solution.py:424
  23.6 2.4 %collective-permute-start.4 = (bf16[512,256]{1,0:T(8,128)(2,1)S(1)}, bf16[512,256]{1,0:T(8,128)(2,1)S(1)}, u32[]{:S(2)}, u32[]{:S(2)}) collective-permute-start(bf16[512,256]{1,0:T(8,128)(2,1)S(1)} %get-tuple-element.55), channel_id=1, source_target_pairs={{0,1},{1,0},{2,3},{3,2},{4,5},{5,4},{6,7},{7,6},{8,9},{9,8},{10,11... | collective-permute-start | bytes 786440 | tf_op jit(solution)/shard_map/ppermute | solution.py:424
  23.6 12.5 %collective-permute-start.6 = (bf16[512,256]{1,0:T(8,128)(2,1)S(1)}, bf16[512,256]{1,0:T(8,128)(2,1)S(1)}, u32[]{:S(2)}, u32[]{:S(2)}) collective-permute-start(bf16[512,256]{1,0:T(8,128)(2,1)S(1)} %get-tuple-element.64), channel_id=1, source_target_pairs={{0,2},{2,4},{4,6},{6,8},{8,10},{10,12},{12,14},{1,3},{3,5},{5,7},{... | collective-permute-start | bytes 786440 | tf_op jit(solution)/shard_map/ppermute | solution.py:456
  39.7 2.2 %collective-permute-start.7 = (f32[2,16,128]{2,1,0:T(8,128)S(1)}, f32[2,16,128]{2,1,0:T(8,128)S(1)}, u32[]{:S(2)}, u32[]{:S(2)}) collective-permute-start(f32[2,16,128]{2,1,0:T(8,128)S(1)} %get-tuple-element.71), channel_id=1, source_target_pairs={{0,1},{1,0},{2,3},{3,2},{4,5},{5,4},{6,7},{7,6},{8,9},{9,8},{10,11... | collective-permute-start | bytes 49160 | tf_op jit(solution)/shard_map/ppermute | solution.py:424
